TPU v7x, 32 devices: a whole 2x2x4 slice. The times are simulated.
32 devices in a mesh: row: 4 (over y, x), col: 4 (over z), dp: 2 (over core).
Axes of the slice: x: 2, y: 2, z: 4, core: 2. Of those that a mesh axis runs over, the one named last changes fastest.
Arguments:
- grad_output: bfloat16 [2, 512, 8192], P('dp', 'col', 'row'), may hold values from -0.09375 to 0.09375
- block_input: bfloat16 [2, 512, 8192], P('dp', 'col', 'row'), may hold values from -6 to 6
- query_branch: bfloat16 [2, 512, 8192], P('dp', 'row', 'col'), may hold values from -6 to 6
- key_branch: bfloat16 [2, 512, 8192], P('dp', 'row', 'col'), may hold values from -6 to 6
- value_branch: bfloat16 [2, 512, 8192], P('dp', 'row', 'col'), may hold values from -6 to 6
- out_weight: bfloat16 [8192, 8192], P('row', 'col'), may hold values from -0.0625 to 0.0625
- filters: float32 [512, 128], P('col'), may hold values from -0.5 to 0.5
Outputs:
- out_weight_grad: float32 [8192, 8192], P('row', 'col')
- value_weight_grad: float32 [8192, 8192], P('col', 'row')
- filter_grad: float32 [512, 128], P('col')
All inputs are finite; a program needn't handle non-finite values.
Results may differ from a plain program's by a relative error of at most 0.0029.
Values may be sent and summed in bfloat16 or wider, within the bound.
No kernel may reach another device: no remote copies, remote signals or barrier semaphores. Data moves between devices by JAX's collectives and lax.ppermute only.
A program may use at most 128 MiB of HBM per device.

v0:
```python
import jax
import jax.numpy as jnp
from jax import lax
from jax.sharding import PartitionSpec as P

highest = lax.Precision.HIGHEST


def toeplitz(taps, tok_rows, causal):
    filter_len = taps.shape[1]
    out_pos = lax.broadcasted_iota(jnp.int32, (tok_rows, tok_rows + filter_len), 0)
    in_pos = lax.broadcasted_iota(jnp.int32, (tok_rows, tok_rows + filter_len), 1)
    lagged = out_pos + filter_len - in_pos if causal else in_pos - out_pos
    inside = (lagged >= 0) & (lagged < filter_len)
    picked = jnp.take(taps, jnp.clip(lagged, 0, filter_len - 1), axis=1)
    return jnp.where(inside[None], picked, 0.0)


def grouped_apply(table, signal, groups):
    blocks, extent, channels = signal.shape
    split = signal.reshape(blocks, extent, groups, channels // groups)
    result = jnp.einsum("gts,bsgc->btgc", table, split, precision=highest)
    return result.reshape(blocks, table.shape[1], channels)


def taps_partial(delta_mix, mixed_ext, groups, filter_len):
    blocks, tok_rows, channels = delta_mix.shape
    left_side = delta_mix.reshape(blocks, tok_rows, groups, channels // groups)
    right_side = mixed_ext.reshape(blocks, tok_rows + filter_len, groups, channels // groups)
    products = jnp.einsum("btgc,bsgc->gts", left_side, right_side, precision=highest)
    extent = tok_rows + filter_len
    flipped = products[:, :, ::-1]
    padded = jnp.pad(flipped, ((0, 0), (0, 0), (0, tok_rows)))
    flat_rows = padded.reshape(groups, -1)[:, : tok_rows * (extent + tok_rows - 1)]
    skewed = flat_rows.reshape(groups, tok_rows, extent + tok_rows - 1)
    column_sums = jnp.sum(skewed, axis=1)
    return column_sums[:, tok_rows - 1 : tok_rows - 1 + filter_len]


def local(grad_output, block_input, query_branch, key_branch, value_branch, out_weight, filters):
    filter_len = filters.shape[1]
    groups = filters.shape[0]
    tok_rows = query_branch.shape[1]
    channels = query_branch.shape[2]
    grads_all, inputs_all = (
        lax.all_gather(grad_output[0], "col", axis=0, tiled=True),
        lax.all_gather(block_input[0], "col", axis=0, tiled=True),
    )
    row_devices = lax.axis_size("row")
    sub_width = channels // row_devices
    delta_turned = lax.psum_scatter(
        lax.dot_general(
            out_weight, grads_all, (((0,), (1,)), ((), ())), preferred_element_type=jnp.float32
        ),
        "row",
        scatter_dimension=0,
        tiled=True,
    )
    queries, keys_here, values_here = (
        lax.all_to_all(query_branch[0], "row", split_axis=1, concat_axis=0, tiled=True),
        lax.all_to_all(key_branch[0], "row", split_axis=1, concat_axis=0, tiled=True),
        lax.all_to_all(value_branch[0], "row", split_axis=1, concat_axis=0, tiled=True),
    )
    delta_out = delta_turned.T
    local_groups = sub_width // (channels // groups)
    first_group = lax.axis_index("row") * local_groups
    my_taps = lax.dynamic_slice_in_dim(filters, first_group, local_groups, 0)
    mixed = keys_here.astype(jnp.float32) * values_here.astype(jnp.float32)
    mixed_blocks = mixed.reshape(row_devices, tok_rows, sub_width)
    earlier = jnp.concatenate(
        [
            jnp.zeros((1, filter_len, sub_width), jnp.float32),
            mixed_blocks[:-1, tok_rows - filter_len :],
        ],
        axis=0,
    )
    mixed_ext = jnp.concatenate([earlier, mixed_blocks], axis=1)
    conv_out = grouped_apply(toeplitz(my_taps, tok_rows, True), mixed_ext, local_groups).reshape(
        -1, sub_width
    )
    gated = (queries.astype(jnp.float32) * conv_out).astype(jnp.bfloat16)
    delta_mix = delta_out * queries.astype(jnp.float32)
    delta_blocks = delta_mix.reshape(row_devices, tok_rows, sub_width)
    later_part = jnp.concatenate(
        [delta_blocks[1:, :filter_len], jnp.zeros((1, filter_len, sub_width), jnp.float32)], axis=0
    )
    delta_ext = jnp.concatenate([delta_blocks, later_part], axis=1)
    delta_conv = grouped_apply(toeplitz(my_taps, tok_rows, False), delta_ext, local_groups).reshape(
        -1, sub_width
    )
    delta_value = (delta_conv * keys_here.astype(jnp.float32)).astype(jnp.bfloat16)
    my_terms = taps_partial(delta_blocks, mixed_ext, local_groups, filter_len)
    taps_local = lax.dynamic_update_slice_in_dim(
        jnp.zeros(filters.shape, jnp.float32), my_terms, first_group, 0
    )
    gated_all, value_all = (
        lax.all_gather(gated, "row", axis=1, tiled=True),
        lax.all_gather(delta_value, "row", axis=1, tiled=True),
    )
    out_grad = lax.dot_general(
        grads_all, gated_all, (((0,), (0,)), ((), ())), preferred_element_type=jnp.float32
    )
    value_grad = lax.dot_general(
        value_all, inputs_all, (((0,), (0,)), ((), ())), preferred_element_type=jnp.float32
    )
    out_grad, value_grad = lax.psum((out_grad, value_grad), "dp")
    taps_total = lax.psum(taps_local, ("row", "dp"))
    return (out_grad, value_grad, taps_total)


def solution(mesh):
    in_specs = (
        P("dp", "col", "row"),
        P("dp", "col", "row"),
        P("dp", "row", "col"),
        P("dp", "row", "col"),
        P("dp", "row", "col"),
        P("row", "col"),
        P("col", None),
    )
    out_specs = (P("row", "col"), P("col", "row"), P("col", None))
    return jax.shard_map(local, mesh=mesh, in_specs=in_specs, out_specs=out_specs, check_vma=False)
```

profile of v0, /device:TPU:0, one launch (start us, length us, event | category | flops | bytes accessed | tf_op | source)
XLA Modules:
  0.0 600.6 jit_solution(3298674193855796662)
XLA Ops:
  7.2 0.7 all-gather.11.cloned.1.call-update
  8.0 50.3 %all-gather.11.cloned.1.call-done = bf16[1,512,2048]{2,1,0:T(8,128)(2,1)} async-done(((bf16[1,128,2048]{2,1,0:T(8,128)(2,1)}), bf16[1,512,2048]{2,1,0:T(8,128)(2,1)}) %all-gather.11.cloned.1.call-update) | async-done | bytes 2097168 | tf_op jit(solution)/shard_map/all_gather | solution.py:46
  58.3 10.6 %fusion.11 = f32[2048,512]{1,0:T(8,128)} fusion(bf16[2048,2048]{1,0:T(8,128)(2,1)} %param.14, bf16[1,512,2048]{2,1,0:T(8,128)(2,1)} %all-gather.11.cloned.1.call-done), kind=kOutput, calls=%fused_computation.18 | convolution fusion | flops 4294967296 | bytes 14680064 | tf_op jit(solution)/shard_map/dot_general | solution.py:52
  68.9 1.0 copy-done.4
  69.9 1.0 copy.56
  70.9 3.6 all-to-all-start.1
  74.5 0.1 fusion.42
  74.6 0.1 copy.82
  74.8 0.1 copy.79
  74.9 1.0 copy.54
  75.9 1.1 copy.58
  77.0 109.3 %gather_fusion = f32[32768,32]{1,0:T(8,128)} fusion(f32[32,128]{0,1:T(8,128)S(1)} %copy.79, s32[32768]{0:T(1024)S(1)} %broadcast_clamp_fusion.1), kind=kCustom, calls=%fused_computation.clone | custom fusion | bytes 8519680 | tf_op jit(solution)/shard_map/jit(_take)/gather | solution.py:15
  186.2 11.8 %copy.64 = f32[128,256,32]{1,0,2:T(8,128)} copy(f32[128,256,32]{2,1,0:T(8,128)} %bitcast.102) | data formatting | bytes 8388608 | tf_op jit(solution)/shard_map/jit(_take)/gather | solution.py:15
  198.0 4.2 all-to-all-start.2
  202.2 0.2 fusion.47
  202.4 0.1 convert_bitcast_fusion.1
  202.4 0.3 copy.57
  202.8 7.0 %all-to-all-done.2 = bf16[128,4,512]{0,2,1:T(8,128)(2,1)S(1)} async-done(((bf16[128,4,512]{0,2,1:T(8,128)(2,1)}), bf16[128,4,512]{0,2,1:T(8,128)(2,1)S(1)}, u32[]{:S(2)}, u32[]{:S(2)}) %all-to-all-start.2) | async-done | bytes 524320 | tf_op jit(solution)/shard_map/all_to_all | solution.py:62
  209.8 4.1 all-to-all-start
  213.9 0.0 all-gather.7.cloned.1.call-start
  214.0 0.1 convert_bitcast_fusion
  214.0 1.3 copy.59
  215.3 2.2 slice_multiply_fusion
  217.6 0.1 convert_multiply_fusion
  217.7 1.4 copy.60
  219.1 0.1 concatenate.22
  219.2 6.6 %fusion.24 = f32[4,128,32,16]{1,3,0,2:T(8,128)S(1)} fusion(f32[128,256,32]{1,0,2:T(8,128)} %copy.64, pred[128,256]{1,0:T(8,128)(4,1)S(1)} %get-tuple-element.21, pred[128,256]{1,0:T(8,128)(4,1)S(1)} %get-tuple-element.20, f32[4,128,32,16]{1,3,2,0:T(8,128)S(1)} %bitcast.105, f32[4,128,32,16]{1,3,2,0:T(8,128)S(1)} %bitcast.107), kind=kOutput, calls=%fused_computation.31 | convolution fusion | flops 807927808 | bytes 7405568 | tf_op jit(solution)/shard_map/gts,bsgc->btgc/dot_general | solution.py:22
  225.8 1.4 copy.65
  227.2 2.8 bitcast_multiply_fusion.1
  230.1 0.5 all-gather.13.cloned.1.call-update
  230.6 0.2 all-gather.9.cloned.1.call-start
  230.9 0.1 copy.84
  231.0 109.3 %gather_fusion.1 = f32[32768,32]{1,0:T(8,128)} fusion(f32[32,128]{0,1:T(8,128)S(1)} %copy.79, s32[32768]{0:T(1024)S(1)} %broadcast_clamp_fusion), kind=kCustom, calls=%fused_computation.1.clone | custom fusion | bytes 8519680 | tf_op jit(solution)/shard_map/jit(_take)/gather | solution.py:15
  340.2 11.7 %copy.70 = f32[128,256,32]{1,0,2:T(8,128)} copy(f32[128,256,32]{2,1,0:T(8,128)} %bitcast.101) | data formatting | bytes 8388608 | tf_op jit(solution)/shard_map/jit(_take)/gather | solution.py:15
  351.9 0.1 fusion.46
  352.0 0.9 slice.30
  353.0 1.6 concatenate.26
  354.5 2.3 copy.66
  356.9 2.3 copy.80
  359.2 1.2 concatenate.27.clone
  360.4 0.1 copy.68
  360.5 6.6 %fusion.29 = f32[4,128,32,16]{1,3,0,2:T(8,128)S(1)} fusion(f32[128,256,32]{1,0,2:T(8,128)} %copy.70, pred[128,256]{1,0:T(8,128)(4,1)S(1)} %get-tuple-element.22, pred[128,256]{1,0:T(8,128)(4,1)S(1)} %get-tuple-element.23, f32[4,128,32,16]{1,3,0,2:T(8,128)S(1)} %copy.68, f32[4,128,32,16]{1,3,2,0:T(8,128)S(1)} %bitcast.110), kind=kOutput, calls=%fused_computation.32 | convolution fusion | flops 807927808 | bytes 7405568 | tf_op jit(solution)/shard_map/gts,bsgc->btgc/dot_general | solution.py:22
  367.0 0.4 copy.71
  367.5 1.0 copy.102
  368.5 2.5 copy.72
  371.0 2.5 multiply_convert_fusion
  373.6 12.9 %convolution_bitcast_fusion = f32[2048,2048]{0,1:T(8,128)} fusion(bf16[512,2048]{0,1:T(8,128)(2,1)} %all-gather.7.cloned.1.call-done, bf16[1,512,2048]{2,1,0:T(8,128)(2,1)} %all-gather.11.cloned.1.call-done), kind=kOutput, calls=%fused_computation.2 | convolution fusion | flops 4294967296 | bytes 20971520 | tf_op jit(solution)/shard_map/dot_general | solution.py:100
  386.5 21.7 %all-gather.9.cloned.1.call-done = bf16[512,2048]{1,0:T(8,128)(2,1)} async-done(((bf16[512,512]{1,0:T(8,128)(2,1)}), bf16[512,2048]{1,0:T(8,128)(2,1)}) %all-gather.9.cloned.1.call-update) | async-done | bytes 2097168 | tf_op jit(solution)/shard_map/all_gather | solution.py:98
  408.3 12.9 %fusion.9 = f32[2048,2048]{1,0:T(8,128)} fusion(bf16[512,2048]{1,0:T(8,128)(2,1)} %all-gather.9.cloned.1.call-done, bf16[1,512,2048]{2,1,0:T(8,128)(2,1)} %all-gather.13.cloned.1.call-done), kind=kOutput, calls=%fused_computation.16 | convolution fusion | flops 4294967296 | bytes 20971520 | tf_op jit(solution)/shard_map/dot_general | solution.py:103
  421.2 0.3 all-reduce.7.cloned.1.call-start
  421.5 5.2 convolution_bitcast_fusion.1
  426.7 34.6 %rev.3 = f32[32,128,256]{2,1,0:T(8,128)} reverse(f32[32,128,256]{2,1,0:T(8,128)} %convolution_bitcast_fusion.1), dimensions={2} | reverse | bytes 8388608 | tf_op jit(solution)/shard_map/rev | solution.py:32
  461.4 3.5 pad.6
  464.9 3.6 copy.86
  468.6 3.0 slice.31
  471.5 9.9 %reshape.76 = f32[32,128,383]{2,1,0:T(8,128)} reshape(f32[32,49024]{1,0:T(8,128)} %slice.31) | data formatting | bytes 12550144 | tf_op jit(solution)/shard_map/reshape | solution.py:35
  481.4 4.0 reduce_sum.9
  485.4 0.1 slice_dynamic-update-slice_fusion
  485.5 0.6 copy-done.7
  486.2 37.4 %all-reduce.9.cloned.1.call-done = (f32[2048,2048]{0,1:T(8,128)}, f32[2048,2048]{1,0:T(8,128)}) async-done(((f32[2048,2048]{0,1:T(8,128)}, f32[2048,2048]{1,0:T(8,128)}), (f32[2048,2048]{0,1:T(8,128)}, f32[2048,2048]{1,0:T(8,128)})) %all-reduce.9.cloned.1.call-update) | async-done | bytes 33554448 | tf_op jit(solution)/shard_map/psum | solution.py:106
  523.5 17.6 %copy.74 = f32[2048,2048]{1,0:T(8,128)} copy(f32[2048,2048]{0,1:T(8,128)} %get-tuple-element.16) | data formatting | bytes 33554432
  541.1 40.1 %all-reduce.7.cloned.1.call-done = f32[128,128]{1,0:T(8,128)} async-done(((f32[128,128]{1,0:T(8,128)}), f32[128,128]{1,0:T(8,128)}) %all-reduce.7.cloned.1.call-update) | async-done | bytes 65552 | tf_op jit(solution)/shard_map/psum | solution.py:107
  581.2 11.8 %copy.107 = f32[2048,2048]{1,0:T(8,128)} copy(f32[2048,2048]{1,0:T(8,128)} %get-tuple-element.25) | data formatting | bytes 33554432
  593.1 0.6 copy.108
  (36 shorter events, 0.4 us)
Async XLA Ops:
  7.2 67.6 %copy-start = (f32[128,128]{1,0:T(8,128)S(1)}, f32[128,128]{1,0:T(8,128)}, u32[]{:S(2)}) copy-start(f32[128,128]{1,0:T(8,128)} %param.15) | copy-start | bytes 196612
  7.2 51.1 %all-gather.11.cloned.1.call-start = ((), (), s32[]{:S(2)}) async-start(), calls=%async_computation.8 | async-start | bytes 2621440 | tf_op jit(solution)/shard_map/all_gather | solution.py:46
  7.9 219.2 %reduce-scatter.2.cloned.1.call-start = ((), (), s32[]{:S(2)}) async-start(), calls=%async_computation.5 | async-start | bytes 5242880 | tf_op jit(solution)/shard_map/reduce_scatter | solution.py:51
  68.8 1.0 copy-start.4
  68.8 6.0 %copy-start.5 = (bf16[1,128,2048]{2,1,0:T(8,128)(2,1)S(1)}, bf16[1,128,2048]{2,1,0:T(8,128)(2,1)}, u32[]{:S(2)}) copy-start(bf16[1,128,2048]{2,1,0:T(8,128)(2,1)} %param.11) | copy-start | bytes 1572868
  68.8 7.1 %copy-start.6 = (bf16[1,128,2048]{2,1,0:T(8,128)(2,1)S(1)}, bf16[1,128,2048]{2,1,0:T(8,128)(2,1)}, u32[]{:S(2)}) copy-start(bf16[1,128,2048]{2,1,0:T(8,128)(2,1)} %param.13) | copy-start | bytes 1572868
  70.9 127.1 %all-to-all-start.1 = ((bf16[128,4,512]{0,2,1:T(8,128)(2,1)}), bf16[128,4,512]{0,2,1:T(8,128)(2,1)S(1)}, u32[]{:S(2)}, u32[]{:S(2)}) async-start(bf16[128,4,512]{0,2,1:T(8,128)(2,1)} %bitcast.2), calls=%async_computation.1 | async-start | bytes 1048576 | tf_op jit(solution)/shard_map/all_to_all | solution.py:61
  198.0 11.7 %all-to-all-start.2 = ((bf16[128,4,512]{0,2,1:T(8,128)(2,1)}), bf16[128,4,512]{0,2,1:T(8,128)(2,1)S(1)}, u32[]{:S(2)}, u32[]{:S(2)}) async-start(bf16[128,4,512]{0,2,1:T(8,128)(2,1)} %bitcast.5), calls=%async_computation.2 | async-start | bytes 1048576 | tf_op jit(solution)/shard_map/all_to_all | solution.py:62
  202.8 12.6 %copy-start.2 = (f32[4,128,512]{2,1,0:T(8,128)}, f32[4,128,512]{2,1,0:T(8,128)S(1)}, u32[]{:S(2)}) copy-start(f32[4,128,512]{2,1,0:T(8,128)S(1)} %copy.57) | copy-start | bytes 3145732
  209.8 17.4 %all-to-all-start = ((bf16[128,4,512]{0,2,1:T(8,128)(2,1)}), bf16[128,4,512]{0,2,1:T(8,128)(2,1)}, u32[]{:S(2)}, u32[]{:S(2)}) async-start(bf16[128,4,512]{0,2,1:T(8,128)(2,1)} %bitcast.117), calls=%async_computation | async-start | bytes 1048576 | tf_op jit(solution)/shard_map/all_to_all | solution.py:60
  213.9 159.7 %all-gather.7.cloned.1.call-start = ((), (), s32[]{:S(2)}) async-start(), calls=%async_computation.4 | async-start | bytes 2621440 | tf_op jit(solution)/shard_map/all_gather | solution.py:97
  230.0 122.0 %copy-start.3 = (f32[512,512]{0,1:T(8,128)}, f32[512,512]{0,1:T(8,128)S(1)}, u32[]{:S(2)}) copy-start(f32[512,512]{0,1:T(8,128)S(1)} %get-tuple-element.18) | copy-start | bytes 3145732
  230.0 156.5 %all-gather.13.cloned.1.call-start = ((), (), s32[]{:S(2)}) async-start(), calls=%async_computation.9 | async-start | bytes 2621440 | tf_op jit(solution)/shard_map/all_gather | solution.py:47
  230.6 177.7 %all-gather.9.cloned.1.call-start = ((), (), s32[]{:S(2)}) async-start(), calls=%async_computation.6 | async-start | bytes 2621440 | tf_op jit(solution)/shard_map/all_gather | solution.py:98
  373.6 150.0 %all-reduce.9.cloned.1.call-start = ((), (), s32[]{:S(2)}) async-start(), calls=%async_computation.10 | async-start | bytes 67108864 | tf_op jit(solution)/shard_map/psum | solution.py:106
  421.2 160.0 %all-reduce.7.cloned.1.call-start = ((), (), s32[]{:S(2)}) async-start(), calls=%async_computation.7 | async-start | bytes 131072 | tf_op jit(solution)/shard_map/psum | solution.py:107
  485.5 0.6 copy-start.7
  581.2 11.8 %copy-start.8 = (f32[128,128]{1,0:T(8,128)S(1)}, f32[128,128]{1,0:T(8,128)}, u32[]{:S(2)}) copy-start(f32[128,128]{1,0:T(8,128)} %all-reduce.7.cloned.1.call-done) | copy-start | bytes 196612
  581.2 12.5 %copy-start.1 = (f32[128,128]{1,0:T(8,128)S(1)}, f32[128,128]{1,0:T(8,128)}, u32[]{:S(2)}) copy-start(f32[128,128]{1,0:T(8,128)} %param.15) | copy-start | bytes 196612
Sparse Core Ops, SparseCore 0:
  9.6 48.6 all-gather.10
  69.0 55.7 reduce-scatter.1
  230.1 34.6 all-gather.6
  266.4 45.9 all-gather.12
  373.7 34.5 all-gather.8
  421.4 102.1 all-reduce.8
  527.4 53.7 all-reduce.6
where the time goes:
time: 604 us; the launch traced here: 601 us
  local copies, waits for them, and re-layouts  349 us (58%)
  waiting for transfers between devices  158 us (26%)
  matrix products  54.8 us (9%)
  between operations  14.4 us (2%)
  starting transfers between devices  12.6 us (2%)
  other arithmetic  12.2 us (2%)
    gather x4, local copies, waits for them, and re-layouts, toeplitz(): picked = jnp.take(taps, jnp.clip(lagged, 0, filter_len - 1), axis=1)  242 us
    all_gather x1, waiting for transfers between devices, local(): lax.all_gather(grad_output[0], 'col', axis=0, tiled=True)  50.3 us
    unnamed x30, local copies, waits for them, and re-layouts  42 us
    psum x1, waiting for transfers between devices, local(): taps_total = lax.psum(taps_local, ('row', 'dp'))  40.1 us
    psum x1, waiting for transfers between devices, local(): out_grad, value_grad = lax.psum((out_grad, value_grad), 'dp')  37.4 us
    rev x1, local copies, waits for them, and re-layouts, taps_partial(): flipped = products[:, :, ::-1]  34.6 us
    all_gather x1, waiting for transfers between devices, local(): lax.all_gather(delta_value, 'row', axis=1, tiled=True)  21.7 us
    dot_general x2, matrix products, grouped_apply(): result = jnp.einsum('gts,bsgc->btgc', table, split, precision=highest)  13.2 us
  transfers between devices with their start and end apart: 10, of which 5 were waited for; matrix products, arithmetic and copies ran while one was open for 62% of the time, Pallas kernels for 0%

commit v1 on v0

--- a/solution.py
+++ b/solution.py
@@ -1,9 +1,386 @@
+import functools
+
 import jax
 import jax.numpy as jnp
 from jax import lax
+from jax.experimental import pallas as pl
+from jax.experimental.pallas import tpu as pltpu
 from jax.sharding import PartitionSpec as P
 
 highest = lax.Precision.HIGHEST
+f32, bf16 = jnp.float32, jnp.bfloat16
+MIB = 1 << 20
+VMEM = pl.BlockSpec(memory_space=pltpu.VMEM)
+SMEM = pl.BlockSpec(memory_space=pltpu.SMEM)
+ANY = pl.BlockSpec(memory_space=pl.ANY)
+
+
+def params(mib):
+    return pltpu.CompilerParams(vmem_limit_bytes=mib * MIB)
+
+
+def cost(flops, nbytes):
+    return pl.CostEstimate(flops=int(flops), bytes_accessed=int(nbytes), transcendentals=0)
+
+
+def split_two(x):
+    hi = x.astype(bf16)
+    return hi, (x - hi.astype(f32)).astype(bf16)
+
+
+def turn_kernel(rows, pos_ref, q_ref, k_ref, v_ref, *outs):
+    width = outs[0].shape[1]
+    for j, out in enumerate(outs):
+        columns = pl.ds(pl.multiple_of((pos_ref[0] ^ j) * width, 128), width)
+        for n, src in enumerate((q_ref, k_ref, v_ref)):
+            out[n] = src[0, :, columns].T
+
+
+def turn_branches(pos, q, k, v, rows):
+    _, toks, channels = q.shape
+    width = channels // rows
+    out = jax.ShapeDtypeStruct((3, width, toks), bf16)
+    return pl.pallas_call(
+        functools.partial(turn_kernel, rows),
+        out_shape=[out] * rows,
+        in_specs=[SMEM] + [VMEM] * 3,
+        out_specs=[VMEM] * rows,
+        compiler_params=params(32),
+        cost_estimate=cost(0, 4 * q.size * 3),
+    )(pos, q, k, v)
+
+
+def tap_matrix(f_ref, row):
+    taps = f_ref.shape[1]
+    wide = jnp.broadcast_to(f_ref[pl.ds(row, 1), :], (taps, taps))
+    ring = pltpu.roll(wide, 0, 1, stride=1, stride_axis=0)
+    s = lax.broadcasted_iota(jnp.int32, (taps, taps), 0)
+    t = lax.broadcasted_iota(jnp.int32, (taps, taps), 1)
+    same = jnp.where(t >= s, ring, 0.0)
+    return same, ring - same
+
+
+def dot(a, b, dims=((1,), (0,))):
+    return lax.dot_general(a, b, (dims, ((), ())), preferred_element_type=f32)
+
+
+def forward_kernel(size, pos_ref, f_ref, b0, b1, b2, b3, out_ref, mh, ml, qs, gt):
+    n = f_ref.shape[1]
+    width, toks = gt.shape
+    blocks = toks // n
+    groups = width // size
+    mh[:, :n] = jnp.zeros((width, n), bf16)
+    ml[:, :n] = jnp.zeros((width, n), bf16)
+    for j, b in enumerate((b0, b1, b2, b3)):
+        place = pl.multiple_of((pos_ref[0] ^ j) * n, n)
+        hi, lo = split_two(b[1].astype(f32) * b[2].astype(f32))
+        mh[:, pl.ds(place + n, n)] = hi
+        ml[:, pl.ds(place + n, n)] = lo
+        qs[:, pl.ds(place, n)] = b[0]
+
+    def one(g, carry):
+        rows = pl.ds(pl.multiple_of(g * size, size), size)
+        same, prev = tap_matrix(f_ref, pos_ref[0] * groups + g)
+        table_hi, table_lo = split_two(jnp.concatenate([prev, same], axis=0))
+        x_hi = jnp.concatenate([mh[rows, b * n : (b + 2) * n] for b in range(blocks)], axis=0)
+        x_lo = jnp.concatenate([ml[rows, b * n : (b + 2) * n] for b in range(blocks)], axis=0)
+        conv = dot(x_hi, table_hi) + dot(x_lo, table_hi) + dot(x_hi, table_lo)
+        for b in range(blocks):
+            gate = qs[rows, b * n : (b + 1) * n].astype(f32)
+            gt[rows, b * n : (b + 1) * n] = gate * conv[b * size : (b + 1) * size]
+        return carry
+
+    lax.fori_loop(0, groups, one, 0, unroll=4)
+    for b in range(blocks):
+        out_ref[b * n : (b + 1) * n, :] = gt[:, b * n : (b + 1) * n].T.astype(bf16)
+
+
+def forward(pos, filters, parts, size):
+    _, width, n = parts[0].shape
+    toks = n * len(parts)
+    return pl.pallas_call(
+        functools.partial(forward_kernel, size),
+        out_shape=jax.ShapeDtypeStruct((toks, width), bf16),
+        in_specs=[SMEM] + [VMEM] * 5,
+        out_specs=VMEM,
+        scratch_shapes=[
+            pltpu.VMEM((width, toks + n), bf16),
+            pltpu.VMEM((width, toks + n), bf16),
+            pltpu.VMEM((width, toks), bf16),
+            pltpu.VMEM((width, toks), f32),
+        ],
+        compiler_params=params(32),
+        cost_estimate=cost(8e9, 2 * 4 * toks * width),
+    )(pos, filters, *parts)
+
+
+def backward_kernel(size, counts, pos_ref, f_ref, b0, b1, b2, b3, *refs):
+    n = f_ref.shape[1]
+    deltas, (taps_ref, out_ref), (dh, dl, mh, ml, qs, ks, sums) = (
+        refs[: -9],
+        refs[-9:-7],
+        refs[-7:],
+    )
+    width, toks = qs.shape
+    blocks = toks // n
+    groups = width // size
+    row, col = pos_ref[0], pos_ref[1]
+    zero = jnp.zeros((width, n), bf16)
+    mh[:, :n] = zero
+    ml[:, :n] = zero
+    dh[:, toks:] = zero
+    dl[:, toks:] = zero
+    for j, b in enumerate((b0, b1, b2, b3)):
+        place = pl.multiple_of((row ^ j) * n, n)
+        hi, lo = split_two(b[1].astype(f32) * b[2].astype(f32))
+        mh[:, pl.ds(place + n, n)] = hi
+        ml[:, pl.ds(place + n, n)] = lo
+        qs[:, pl.ds(place, n)] = b[0]
+        ks[:, pl.ds(place, n)] = b[1]
+    slot = 0
+    for i, count in enumerate(counts):
+        for m in range(count):
+            place = pl.multiple_of((col ^ slot) * n, n)
+            own, first, second, third = (ref[m * n : (m + 1) * n, :].astype(f32) for ref in deltas[4 * i : 4 * i + 4])
+            delta = (own + first) + (second + third)
+            hi, lo = split_two(delta.T * qs[:, pl.ds(place, n)].astype(f32))
+            dh[:, pl.ds(place, n)] = hi
+            dl[:, pl.ds(place, n)] = lo
+            slot += 1
+    s = lax.broadcasted_iota(jnp.int32, (n, n), 0)
+    t = lax.broadcasted_iota(jnp.int32, (n, n), 1)
+
+    def one(g, carry):
+        rows = pl.ds(pl.multiple_of(g * size, size), size)
+        same, prev = tap_matrix(f_ref, row * groups + g)
+        table_hi, table_lo = split_two(jnp.concatenate([same, prev], axis=1))
+        d_hi = [dh[rows, b * n : (b + 2) * n] for b in range(blocks)]
+        d_lo = [dl[rows, b * n : (b + 2) * n] for b in range(blocks)]
+        x_hi, x_lo = jnp.concatenate(d_hi, axis=0), jnp.concatenate(d_lo, axis=0)
+        across = ((1,), (1,))
+        conv = dot(x_hi, table_hi, across) + dot(x_lo, table_hi, across) + dot(x_hi, table_lo, across)
+        for b in range(blocks):
+            key = ks[rows, b * n : (b + 1) * n].astype(f32)
+            out_ref[rows, b * n : (b + 1) * n] = (key * conv[b * size : (b + 1) * size]).astype(bf16)
+        m_hi = [mh[rows, b * n : (b + 2) * n] for b in range(blocks)]
+        m_lo = [ml[rows, b * n : (b + 2) * n] for b in range(blocks)]
+        d_hi, d_lo = [d[:, :n] for d in d_hi], [d[:, :n] for d in d_lo]
+        pairs = dot(
+            jnp.concatenate(m_hi + m_lo + m_hi, axis=0),
+            jnp.concatenate(d_hi + d_hi + d_lo, axis=0),
+            ((0,), (0,)),
+        )
+        ring = jnp.where(s <= t, pairs[n:], pairs[:n])
+        half = n // 2
+        while half >= 8:
+            ring = ring[:half] + pltpu.roll(ring[half:], n - half, 1)
+            half //= 2
+        sums[pl.ds(pl.multiple_of(g * 8, 8), 8), :] = ring
+        return carry
+
+    lax.fori_loop(0, groups, one, 0, unroll=4)
+    total = sums[pl.ds(0, groups, stride=8), :]
+    for i in range(1, 8):
+        total = total + pltpu.roll(sums[pl.ds(i, groups, stride=8), :], n - i, 1)
+    taps_ref[...] = total
+
+
+def backward(pos, filters, parts, deltas, counts, size):
+    _, width, n = parts[0].shape
+    toks = n * len(parts)
+    groups = width // size
+    return pl.pallas_call(
+        functools.partial(backward_kernel, size, counts),
+        out_shape=[
+            jax.ShapeDtypeStruct((groups, n), f32),
+            jax.ShapeDtypeStruct((width, toks), bf16),
+        ],
+        in_specs=[SMEM] + [VMEM] * (5 + len(deltas)),
+        out_specs=[VMEM] * 2,
+        scratch_shapes=[pltpu.VMEM((width, toks + n), bf16)] * 4
+        + [pltpu.VMEM((width, toks), bf16)] * 2
+        + [pltpu.VMEM((8 * groups, n), f32)],
+        compiler_params=params(40),
+        cost_estimate=cost(8e9, 2 * 8 * toks * width),
+    )(pos, filters, *parts, *deltas)
+
+
+def project_kernel(count, pos_ref, *refs):
+    slots, w_ref, outs = refs[:count], refs[count], refs[count + 1 : count + 5]
+    wide, sem = refs[count + 5 :]
+    width = outs[0].shape[1]
+    n = slots[0].shape[0]
+
+    def fetch(j):
+        columns = pl.ds(pl.multiple_of((pos_ref[0] ^ j) * width, 128), width)
+        return pltpu.make_async_copy(w_ref.at[:, columns], wide.at[j], sem.at[j])
+
+    order = (3, 1, 2, 0)
+    for j in order:
+        fetch(j).start()
+    grads = jnp.concatenate([slot[...] for slot in slots], axis=0)
+    for j in order:
+        fetch(j).wait()
+        outs[j][...] = dot(grads, wide[j]).astype(outs[j].dtype)
+
+
+def project(pos, slots, weight, rows):
+    depth, channels = weight.shape
+    width = channels // rows
+    toks = sum(slot.shape[0] for slot in slots)
+    return pl.pallas_call(
+        functools.partial(project_kernel, len(slots)),
+        out_shape=[jax.ShapeDtypeStruct((toks, width), f32 if j == 0 else bf16) for j in range(rows)],
+        in_specs=[SMEM] + [VMEM] * len(slots) + [ANY],
+        out_specs=[VMEM] * rows,
+        scratch_shapes=[pltpu.VMEM((rows, depth, width), bf16), pltpu.SemaphoreType.DMA((rows,))],
+        compiler_params=params(40),
+        cost_estimate=cost(2 * toks * depth * channels, 2 * weight.size),
+    )(pos, *slots, weight)
+
+
+def gradient_kernel(turned, pos_ref, *refs):
+    (out_ref, left, right, buf, sem_in, sem_out) = refs[-6:]
+    sources = refs[:-6]
+    n = 128
+    row, col, dp = pos_ref[0], pos_ref[1], pos_ref[2]
+    copies = []
+
+    def fetch(src, dst):
+        copies.append(pltpu.make_async_copy(src, dst, sem_in.at[len(copies)]))
+
+    seq = left.shape[0] // 2 if turned else left.shape[1] // 2
+    if turned:
+        slots, gathered = sources[:8], sources[8]
+        for i, slot in enumerate(slots):
+            owner = dp if i < 4 else 1 - dp
+            fetch(slot, left.at[pl.ds(pl.multiple_of(owner * seq + (col ^ (i % 4)) * n, n), n), :])
+        width = gathered.shape[2]
+        for i in range(8):
+            fetch(gathered.at[i], right.at[pl.ds((i % 2) * seq, seq), pl.ds((i // 2) * width, width)])
+    else:
+        slots, pieces = sources[:8], sources[8:]
+        for i, slot in enumerate(slots):
+            place = pl.multiple_of((i // 4) * seq + (col ^ (i % 4)) * n, n)
+            fetch(slot, right.at[pl.ds(place, n), :])
+        width = pieces[0].shape[0]
+        for i, piece in enumerate(pieces):
+            place = pl.multiple_of((row ^ (i % 4)) * width, width)
+            fetch(piece, left.at[pl.ds(place, width), pl.ds((i // 4) * seq, seq)])
+    for copy in copies:
+        copy.start()
+    for copy in copies:
+        copy.wait()
+    tile = buf.shape[1]
+    tiles = out_ref.shape[0] // tile
+
+    def send(i):
+        at = pl.ds(pl.multiple_of(i * tile, tile), tile)
+        return pltpu.make_async_copy(buf.at[i % 2], out_ref.at[at, :], sem_out.at[i % 2])
+
+    def one(i, carry):
+        at = pl.ds(pl.multiple_of(i * tile, tile), tile)
+
+        @pl.when(i >= 2)
+        def _():
+            send(i - 2).wait()
+
+        lhs = left[:, at].T if turned else left[at, :]
+        buf[i % 2] = dot(lhs, right[...])
+        send(i).start()
+        return carry
+
+    lax.fori_loop(0, tiles, one, 0)
+    send(tiles - 2).wait()
+    send(tiles - 1).wait()
+
+
+def gradient(pos, sources, toks, left_width, right_width, turned):
+    tile = 256
+    return pl.pallas_call(
+        functools.partial(gradient_kernel, turned),
+        out_shape=jax.ShapeDtypeStruct((left_width, right_width), f32),
+        in_specs=[SMEM] + [ANY] * len(sources),
+        out_specs=ANY,
+        scratch_shapes=[
+            pltpu.VMEM((toks, left_width) if turned else (left_width, toks), bf16),
+            pltpu.VMEM((toks, right_width), bf16),
+            pltpu.VMEM((2, tile, right_width), f32),
+            pltpu.SemaphoreType.DMA((16,)),
+            pltpu.SemaphoreType.DMA((2,)),
+        ],
+        compiler_params=params(48),
+        cost_estimate=cost(2 * toks * left_width * right_width, 4 * left_width * right_width),
+    )(pos, *sources)
+
+
+near = [(0, 1), (1, 0), (2, 3), (3, 2)]
+far = [(0, 2), (2, 0), (1, 3), (3, 1)]
+across = [(0, 3), (3, 0), (1, 2), (2, 1)]
+swap = [(0, 1), (1, 0)]
+
+
+def line_slots(x):
+    c = lax.axis_index("col")
+    first = lax.ppermute(x, "col", near)
+    second = lax.ppermute(x, "col", far)
+    inner = lax.ppermute(x, "col", [(1, 2), (2, 1)])
+    passed = lax.ppermute(second, "col", [(2, 3), (1, 0)])
+    third = jnp.where((c == 1) | (c == 2), inner, passed)
+    return [x, first, second, third]
+
+
+def row_exchange(pieces):
+    return [
+        pieces[0],
+        lax.ppermute(pieces[1], "row", near),
+        lax.ppermute(pieces[2], "row", far),
+        lax.ppermute(pieces[3], "row", across),
+    ]
+
+
+def other_core(xs):
+    return [lax.ppermute(x, "dp", swap) for x in xs]
+
+
+def local(grad_output, block_input, query_branch, key_branch, value_branch, out_weight, filters):
+    rows = lax.axis_size("row")
+    toks = query_branch.shape[1]
+    channels = query_branch.shape[2]
+    size = channels // filters.shape[0]
+    width = channels // rows
+    local_groups = width // size
+    pos = jnp.stack([lax.axis_index("row"), lax.axis_index("col"), lax.axis_index("dp")]).astype(jnp.int32)
+
+    grads = line_slots(grad_output[0])
+    turned = turn_branches(pos, query_branch, key_branch, value_branch, rows)
+    parts = row_exchange(turned)
+    gated = forward(pos, filters, parts, size)
+    gated_all = lax.all_gather(gated, ("row", "dp"), axis=0)
+    inputs = line_slots(block_input[0])
+
+    counts = (3, 1)
+    deltas = []
+    for chosen in (grads[:3], grads[3:]):
+        deltas += row_exchange(project(pos, chosen, out_weight, rows))
+    taps, value_grad = backward(pos, filters, parts, deltas, counts, size)
+    values = row_exchange([value_grad] * 4)
+
+    out_grad = gradient(
+        pos, grads + other_core(grads) + [gated_all], 2 * rows * toks, grad_output.shape[2], channels, True
+    )
+    weight_grad = gradient(
+        pos,
+        inputs + other_core(inputs) + values + other_core(values),
+        2 * rows * toks,
+        channels,
+        block_input.shape[2],
+        False,
+    )
+    spread = lax.dynamic_update_slice_in_dim(
+        jnp.zeros(filters.shape, f32), taps, lax.axis_index("row") * local_groups, 0
+    )
+    return (out_grad, weight_grad, lax.psum(spread, ("row", "dp")))
 
 
 def toeplitz(taps, tok_rows, causal):
@@ -37,7 +414,7 @@
     return column_sums[:, tok_rows - 1 : tok_rows - 1 + filter_len]
 
 
-def local(grad_output, block_input, query_branch, key_branch, value_branch, out_weight, filters):
+def plain_local(grad_output, block_input, query_branch, key_branch, value_branch, out_weight, filters):
     filter_len = filters.shape[1]
     groups = filters.shape[0]
     tok_rows = query_branch.shape[1]
@@ -119,4 +496,22 @@
         P("col", None),
     )
     out_specs = (P("row", "col"), P("col", "row"), P("col", None))
-    return jax.shard_map(local, mesh=mesh, in_specs=in_specs, out_specs=out_specs, check_vma=False)
+
+    def whole(*args):
+        grad, filters = args[0], args[6]
+        blocks_of = grad.shape[1] // mesh.shape["col"]
+        width = grad.shape[2] // (mesh.shape["row"] * mesh.shape["col"])
+        fits = (
+            mesh.shape["row"] == 4
+            and mesh.shape["col"] == 4
+            and mesh.shape["dp"] == 2
+            and grad.shape[0] == 2
+            and blocks_of == 128
+            and filters.shape[1] == 128
+            and grad.shape[2] == 16 * filters.shape[0]
+            and width % 512 == 0
+        )
+        body = local if fits else plain_local
+        return jax.shard_map(body, mesh=mesh, in_specs=in_specs, out_specs=out_specs, check_vma=False)(*args)
+
+    return whole

time: 604 us -> 214 us (0.35)
  local copies, waits for them, and re-layouts: 349 us -> 28.8 us
  waiting for transfers between devices: 158 us -> 84.8 us
  matrix products: 54.8 us -> 0 us
  Pallas kernels: 0 us -> 54.1 us
  starting transfers between devices: 12.6 us -> 29.7 us
  other arithmetic: 12.2 us -> 1.23 us
    gather x4 -> x0, local copies, waits for them, and re-layouts: 242 us -> none  [toeplitz(): picked = jnp.take(taps, jnp.clip(lagged, 0, filter_len - 1), axis=1)]
    all_gather x4 -> x1, waiting for transfers between devices: 72 us -> 0.01 us  [local(): gated_all = lax.all_gather(gated, ('row', 'dp'), axis=0)]
    ppermute x0 -> x32, waiting for transfers between devices: none -> 71.9 us  [the longest x2 21.1 us: line_slots(): second = lax.ppermute(x, 'col', far)]
    psum x2 -> x1, waiting for transfers between devices: 77.5 us -> 12.9 us  [local(): return (out_grad, weight_grad, lax.psum(spread, ('row', 'dp')))]
    dot_general x6 -> x0, matrix products: 54.8 us -> none  [the longest x2 13.2 us: grouped_apply(): result = jnp.einsum('gts,bsgc->btgc', table, split, precision=highest)]
    pallas_call x0 -> x7, Pallas kernels: none -> 54.1 us  [the longest x2 29.8 us: gradient(): pl.pallas_call(functools.partial(gradient_kernel, turned), out_shape=jax....]
    rev x1 -> x0, local copies, waits for them, and re-layouts: 34.6 us -> none  [taps_partial(): flipped = products[:, :, ::-1]]
    ppermute x0 -> x32, starting transfers between devices: none -> 29.7 us  [the longest x4 6.62 us: row_exchange(): lax.ppermute(pieces[1], 'row', near)]
  transfers between devices with their start and end apart: 10 -> 34, of which waited for: 5 -> 13; matrix products, arithmetic and copies ran while one was open for 62% -> 1% of each run, Pallas kernels for 0% -> 23%
where the time goes in v1:
time: 214 us; the launch traced here: 213 us
  waiting for transfers between devices  84.8 us (40%)
  Pallas kernels  54.1 us (25%)
  starting transfers between devices  29.7 us (14%)
  local copies, waits for them, and re-layouts  28.8 us (13%)
  between operations  14.3 us (7%)
    pallas_call x2, Pallas kernels, gradient(): pl.pallas_call(functools.partial(gradient_kernel, turned), out_shape=jax....  29.8 us
    unnamed x65, local copies, waits for them, and re-layouts  28.8 us
    ppermute x2, waiting for transfers between devices, line_slots(): second = lax.ppermute(x, 'col', far)  21.1 us
    ppermute x4, waiting for transfers between devices, row_exchange(): lax.ppermute(pieces[2], 'row', far)  21.1 us
    ppermute x4, waiting for transfers between devices, row_exchange(): lax.ppermute(pieces[1], 'row', near)  15.2 us
    psum x1, waiting for transfers between devices, local(): return (out_grad, weight_grad, lax.psum(spread, ('row', 'dp')))  12.9 us
    ppermute x2, waiting for transfers between devices, line_slots(): passed = lax.ppermute(second, 'col', [(2, 3), (1, 0)])  10.9 us
    pallas_call x1, Pallas kernels, backward(): pl.pallas_call(functools.partial(backward_kernel, size, counts), out_shap...  9.4 us
  transfers between devices with their start and end apart: 34, of which 13 were waited for; matrix products, arithmetic and copies ran while one was open for 1% of the time, Pallas kernels for 23%

profile of v1, /device:TPU:0, one launch (start us, length us, event | category | flops | bytes accessed | tf_op | source)
XLA Modules:
  0.0 213.0 jit_solution(1740808737664958799)
XLA Ops:
  7.3 1.0 copy-done.2
  8.3 1.0 copy-done.3
  9.4 1.0 copy-done.4
  10.4 1.0 shard_map.94
  11.4 3.0 %collective-permute-start.8 = (bf16[3,512,128]{2,1,0:T(8,128)(2,1)S(1)}, bf16[3,512,128]{2,1,0:T(8,128)(2,1)S(1)}, u32[]{:S(2)}, u32[]{:S(2)}) collective-permute-start(bf16[3,512,128]{2,1,0:T(8,128)(2,1)S(1)} %get-tuple-element.18), channel_id=1, source_target_pairs={{0,8},{8,0},{16,24},{24,16},{1,9},{9,1},{17,25},{25,17},{2,10},{10... | collective-permute-start | bytes 1179656 | tf_op jit(solution)/shard_map/ppermute | solution.py:336
  14.4 1.5 collective-permute-start.9
  16.0 8.4 %collective-permute-done.8.b1 = bf16[3,512,128]{2,1,0:T(8,128)(2,1)S(1)} collective-permute-done((bf16[3,512,128]{2,1,0:T(8,128)(2,1)S(1)}, bf16[3,512,128]{2,1,0:T(8,128)(2,1)S(1)}, u32[]{:S(2)}, u32[]{:S(2)}) %collective-permute-start.8) | collective-permute-done | bytes 393248 | tf_op jit(solution)/shard_map/ppermute | solution.py:336
  24.4 9.1 %collective-permute-done.9.b2 = bf16[3,512,128]{2,1,0:T(8,128)(2,1)S(1)} collective-permute-done((bf16[3,512,128]{2,1,0:T(8,128)(2,1)S(1)}, bf16[3,512,128]{2,1,0:T(8,128)(2,1)S(1)}, u32[]{:S(2)}, u32[]{:S(2)}) %collective-permute-start.9) | collective-permute-done | bytes 393248 | tf_op jit(solution)/shard_map/ppermute | solution.py:337
  33.4 0.8 copy-done.29
  34.3 4.7 %shard_map.95 = bf16[512,512]{1,0:T(8,128)(2,1)} custom-call(s32[3]{0:T(128)S(1)} %pad_add_fusion.pos_ref, f32[128,128]{1,0:T(8,128)S(1)} %copy-done.29, bf16[3,512,128]{2,1,0:T(8,128)(2,1)S(1)} %get-tuple-element.17.b0, bf16[3,512,128]{2,1,0:T(8,128)(2,1)S(1)} %collective-permute-done.8.b1, bf16[3,512,128]{2,1,0:T(8,128)(2,1)S(1)} %collective-permute-done.9.b2, ...), custom_call_target="tpu_custom_call" | custom-call | flops 8000000000 | bytes 2097152 | tf_op jit(solution)/shard_map/pallas_call | solution.py:101
  38.9 0.7 copy-done.21
  39.7 0.7 copy-done.23
  40.4 0.7 copy-done.25
  41.2 0.7 copy-done.27
  42.0 2.6 %collective-permute-start.1 = (bf16[128,2048]{1,0:T(8,128)(2,1)S(1)}, bf16[128,2048]{1,0:T(8,128)(2,1)S(1)}, u32[]{:S(2)}, u32[]{:S(2)}) collective-permute-start(bf16[128,2048]{1,0:T(8,128)(2,1)S(1)} %bitcast.11), channel_id=1, source_target_pairs={{0,4},{4,0},{2,6},{6,2},{1,5},{5,1},{3,7},{7,3},{8,12},{12,8},{10,... | collective-permute-start | bytes 1572872 | tf_op jit(solution)/shard_map/ppermute | solution.py:326
  44.6 1.6 collective-permute-start
  46.2 0.7 collective-permute-start.2
  46.9 21.1 %collective-permute-done.1.refs_2_ = bf16[128,2048]{1,0:T(8,128)(2,1)S(1)} collective-permute-done((bf16[128,2048]{1,0:T(8,128)(2,1)S(1)}, bf16[128,2048]{1,0:T(8,128)(2,1)S(1)}, u32[]{:S(2)}, u32[]{:S(2)}) %collective-permute-start.1) | collective-permute-done | bytes 524320 | tf_op jit(solution)/shard_map/ppermute | solution.py:326
  68.0 1.3 collective-permute-start.3
  69.3 3.4 %collective-permute-start.11 = (bf16[128,2048]{1,0:T(8,128)(2,1)S(1)}, bf16[128,2048]{1,0:T(8,128)(2,1)}, u32[]{:S(2)}, u32[]{:S(2)}) collective-permute-start(bf16[128,2048]{1,0:T(8,128)(2,1)S(1)} %bitcast.6), channel_id=1, source_target_pairs={{0,2},{2,0},{4,6},{6,4},{1,3},{3,1},{5,7},{7,5},{8,10},{10,8},{12,... | collective-permute-start | bytes 1572872 | tf_op jit(solution)/shard_map/ppermute | solution.py:325
  72.7 0.9 collective-permute-start.12
  73.6 3.5 %copy-done = bf16[2048,2048]{1,0:T(8,128)(2,1)S(1)} copy-done((bf16[2048,2048]{1,0:T(8,128)(2,1)S(1)}, bf16[2048,2048]{1,0:T(8,128)(2,1)}, u32[]{:S(2)}) %copy-start) | copy-done | bytes 8388632
  77.1 5.7 %shard_map.97 = (f32[384,512]{1,0:T(8,128)S(1)}, bf16[384,512]{1,0:T(8,128)(2,1)S(1)}, bf16[384,512]{1,0:T(8,128)(2,1)S(1)}, bf16[384,512]{1,0:T(8,128)(2,1)S(1)}) custom-call(s32[3]{0:T(128)S(1)} %pad_add_fusion.pos_ref, bf16[128,2048]{1,0:T(8,128)(2,1)S(1)} %bitcast.14, bf16[128,2048]{1,0:T(8,128)(2,1)S(1)} %collective-permute-done.refs_1_, ...), custom_call_target="tpu_custom_call" | custom-call | flops 3221225472 | bytes 8388608 | tf_op jit(solution)/shard_map/pallas_call | solution.py:231
  82.8 1.5 collective-permute-start.19
  84.9 8.5 %collective-permute-done.3 = bf16[128,2048]{1,0:T(8,128)(2,1)} collective-permute-done((bf16[128,2048]{1,0:T(8,128)(2,1)S(1)}, bf16[128,2048]{1,0:T(8,128)(2,1)}, u32[]{:S(2)}, u32[]{:S(2)}) %collective-permute-start.3) | collective-permute-done | bytes 524320 | tf_op jit(solution)/shard_map/ppermute | solution.py:328
  93.4 1.5 collective-permute-start.21
  94.8 1.1 broadcast_select_fusion.1.refs_3_.refs_0_
  95.9 3.4 %copy-done.1 = bf16[2048,2048]{1,0:T(8,128)(2,1)S(1)} copy-done((bf16[2048,2048]{1,0:T(8,128)(2,1)S(1)}, bf16[2048,2048]{1,0:T(8,128)(2,1)}, u32[]{:S(2)}) %copy-start.1) | copy-done | bytes 8388632
  99.3 3.5 %shard_map.98 = (f32[128,512]{1,0:T(8,128)S(1)}, bf16[128,512]{1,0:T(8,128)(2,1)S(1)}, bf16[128,512]{1,0:T(8,128)(2,1)S(1)}, bf16[128,512]{1,0:T(8,128)(2,1)S(1)}) custom-call(s32[3]{0:T(128)S(1)} %pad_add_fusion.pos_ref, bf16[128,2048]{1,0:T(8,128)(2,1)S(1)} %broadcast_select_fusion.1.refs_3_.refs_0_, bf16[2048,2048]{1,0:T(8,128)(2,1)S(1)} %copy-done.1), custom_call_target="tpu_custom_call" | custom-call | flops 1073741824 | bytes 8388608 | tf_op jit(solution)/shard_map/pallas_call | solution.py:231
  102.8 1.3 collective-permute-done.11.refs_1_
  104.1 1.4 collective-permute-start.22
  105.5 0.6 collective-permute-start.23
  106.1 1.5 collective-permute-start.24
  107.6 0.7 collective-permute-start.13
  108.3 0.7 collective-permute-done.22.refs_5_
  109.0 1.5 collective-permute-start.14
  110.6 1.3 collective-permute-done.24.refs_7_
  112.0 9.4 %shard_map.99 = (f32[32,128]{1,0:T(8,128)S(1)}, bf16[512,512]{1,0:T(8,128)(2,1)}) custom-call(s32[3]{0:T(128)S(1)} %pad_add_fusion.pos_ref, f32[128,128]{1,0:T(8,128)S(1)} %copy-done.30, bf16[3,512,128]{2,1,0:T(8,128)(2,1)S(1)} %copy-done.22, bf16[3,512,128]{2,1,0:T(8,128)(2,1)S(1)} %copy-done.24, bf16[3,512,128]{2,1,0:T(8,128)(2,1)S(1)} %copy-done.26, ...), custom_call_target="tpu_custom_call" | custom-call | flops 8000000000 | bytes 4194304 | tf_op jit(solution)/shard_map/pallas_call | solution.py:192
  121.4 0.7 collective-permute-start.25
  122.1 0.8 copy-done.7
  122.8 1.4 collective-permute-start.26
  124.2 2.4 %collective-permute-done.14 = bf16[128,2048]{1,0:T(8,128)(2,1)S(1)} collective-permute-done((bf16[128,2048]{1,0:T(8,128)(2,1)}, bf16[128,2048]{1,0:T(8,128)(2,1)S(1)}, u32[]{:S(2)}, u32[]{:S(2)}) %collective-permute-start.14) | collective-permute-done | bytes 524320 | tf_op jit(solution)/shard_map/ppermute | solution.py:328
  126.7 1.5 collective-permute-start.27
  128.2 0.8 copy-done.11
  129.0 0.8 copy-done.9
  130.3 6.1 %collective-permute-done.25.refs_9_ = bf16[512,512]{1,0:T(8,128)(2,1)} collective-permute-done((bf16[512,512]{1,0:T(8,128)(2,1)}, bf16[512,512]{1,0:T(8,128)(2,1)}, u32[]{:S(2)}, u32[]{:S(2)}) %collective-permute-start.25) | collective-permute-done | bytes 524320 | tf_op jit(solution)/shard_map/ppermute | solution.py:336
  136.4 12.0 %collective-permute-done.26.refs_10_ = bf16[512,512]{1,0:T(8,128)(2,1)} collective-permute-done((bf16[512,512]{1,0:T(8,128)(2,1)}, bf16[512,512]{1,0:T(8,128)(2,1)}, u32[]{:S(2)}, u32[]{:S(2)}) %collective-permute-start.26) | collective-permute-done | bytes 524320 | tf_op jit(solution)/shard_map/ppermute | solution.py:337
  149.0 0.6 copy-done.31
  150.8 0.6 collective-permute-done.31.refs_15_
  151.4 1.0 copy-done.8
  152.5 1.0 copy-done.10
  153.5 1.0 copy-done.12
  154.6 14.9 %shard_map.100 = f32[2048,2048]{1,0:T(8,128)} custom-call(s32[3]{0:T(128)S(1)} %pad_add_fusion.pos_ref, bf16[128,2048]{1,0:T(8,128)(2,1)S(1)} %bitcast.10, bf16[128,2048]{1,0:T(8,128)(2,1)} %collective-permute-done.11.refs_1_, bf16[128,2048]{1,0:T(8,128)(2,1)} %collective-permute-done.12.refs_2_, bf16[128,2048]{1,0:T(8,128)(2,1)S(1)} %broadcast_select_fusion.refs_3_, ...), custom_call_target="tpu_custom_call" | custom-call | flops 8589934592 | bytes 16777216 | tf_op jit(solution)/shard_map/pallas_call | solution.py:300
  169.5 0.8 copy-done.13
  170.3 0.8 copy-done.15
  171.1 0.8 copy-done.17
  171.9 0.8 copy-done.19
  172.7 1.0 copy-done.14
  173.8 1.0 copy-done.16
  174.8 1.0 copy-done.18
  175.8 1.0 copy-done.20
  176.9 14.9 %shard_map.96 = f32[2048,2048]{1,0:T(8,128)} custom-call(s32[3]{0:T(128)S(1)} %pad_add_fusion.pos_ref, bf16[128,2048]{1,0:T(8,128)(2,1)S(1)} %bitcast.16, bf16[128,2048]{1,0:T(8,128)(2,1)S(1)} %collective-permute-done.refs_1_, bf16[128,2048]{1,0:T(8,128)(2,1)S(1)} %collective-permute-done.1.refs_2_, ...), custom_call_target="tpu_custom_call" | custom-call | flops 8589934592 | bytes 16777216 | tf_op jit(solution)/shard_map/pallas_call | solution.py:300
  191.8 12.9 %all-reduce.2.cloned.1.call-done = f32[128,128]{1,0:T(8,128)} async-done(((f32[128,128]{1,0:T(8,128)}), f32[128,128]{1,0:T(8,128)}) %all-reduce.2.cloned.1.call-update) | async-done | bytes 65552 | tf_op jit(solution)/shard_map/psum | solution.py:383
  204.7 1.5 copy.12
  (83 shorter events, 3.3 us)
Async XLA Ops:
  7.2 165.6 %all-gather.3.cloned.1.call-start = ((), (), s32[]{:S(2)}) async-start(), calls=%async_computation.1 | async-start | bytes 4718592 | tf_op jit(solution)/shard_map/all_gather | solution.py:359
  7.3 1.0 copy-start.2
  8.3 1.0 copy-start.3
  9.4 1.0 copy-start.4
  10.4 31.6 %copy-start.6 = (bf16[1,128,2048]{2,1,0:T(8,128)(2,1)S(1)}, bf16[1,128,2048]{2,1,0:T(8,128)(2,1)}, u32[]{:S(2)}) copy-start(bf16[1,128,2048]{2,1,0:T(8,128)(2,1)} %param.7) | copy-start | bytes 1572868
  10.4 58.9 %copy-start.5 = (bf16[1,128,2048]{2,1,0:T(8,128)(2,1)S(1)}, bf16[1,128,2048]{2,1,0:T(8,128)(2,1)}, u32[]{:S(2)}) copy-start(bf16[1,128,2048]{2,1,0:T(8,128)(2,1)} %param.8) | copy-start | bytes 1572868
  11.4 12.9 %collective-permute-start.8 = (bf16[3,512,128]{2,1,0:T(8,128)(2,1)S(1)}, bf16[3,512,128]{2,1,0:T(8,128)(2,1)S(1)}, u32[]{:S(2)}, u32[]{:S(2)}) collective-permute-start(bf16[3,512,128]{2,1,0:T(8,128)(2,1)S(1)} %get-tuple-element.18), channel_id=1, source_target_pairs={{0,8},{8,0},{16,24},{24,16},{1,9},{9,1},{17,25},{25,17},{2,10},{10... | collective-permute-start | bytes 1179656 | tf_op jit(solution)/shard_map/ppermute | solution.py:336
  14.4 19.0 %collective-permute-start.9 = (bf16[3,512,128]{2,1,0:T(8,128)(2,1)S(1)}, bf16[3,512,128]{2,1,0:T(8,128)(2,1)S(1)}, u32[]{:S(2)}, u32[]{:S(2)}) collective-permute-start(bf16[3,512,128]{2,1,0:T(8,128)(2,1)S(1)} %get-tuple-element.19), channel_id=1, source_target_pairs={{0,16},{16,0},{8,24},{24,8},{1,17},{17,1},{9,25},{25,9},{2,18},{18... | collective-permute-start | bytes 1179656 | tf_op jit(solution)/shard_map/ppermute | solution.py:337
  16.0 17.5 %collective-permute-start.10 = (bf16[3,512,128]{2,1,0:T(8,128)(2,1)S(1)}, bf16[3,512,128]{2,1,0:T(8,128)(2,1)S(1)}, u32[]{:S(2)}, u32[]{:S(2)}) collective-permute-start(bf16[3,512,128]{2,1,0:T(8,128)(2,1)S(1)} %get-tuple-element.20), channel_id=1, source_target_pairs={{0,24},{24,0},{8,16},{16,8},{1,25},{25,1},{9,17},{17,9},{2,26},{26... | collective-permute-start | bytes 1179656 | tf_op jit(solution)/shard_map/ppermute | solution.py:338
  33.4 0.8 copy-start.29
  38.9 0.7 copy-start.21
  39.7 0.7 copy-start.23
  40.4 0.7 copy-start.25
  41.9 70.0 %copy-start.30 = (f32[128,128]{1,0:T(8,128)S(1)}, f32[128,128]{1,0:T(8,128)}, u32[]{:S(2)}) copy-start(f32[128,128]{1,0:T(8,128)} %f_ref.3) | copy-start | bytes 196612
  41.9 162.7 %all-reduce.2.cloned.1.call-start = ((), (), s32[]{:S(2)}) async-start(), calls=%async_computation | async-start | bytes 131072 | tf_op jit(solution)/shard_map/psum | solution.py:383
  42.0 26.0 %collective-permute-start.1 = (bf16[128,2048]{1,0:T(8,128)(2,1)S(1)}, bf16[128,2048]{1,0:T(8,128)(2,1)S(1)}, u32[]{:S(2)}, u32[]{:S(2)}) collective-permute-start(bf16[128,2048]{1,0:T(8,128)(2,1)S(1)} %bitcast.11), channel_id=1, source_target_pairs={{0,4},{4,0},{2,6},{6,2},{1,5},{5,1},{3,7},{7,3},{8,12},{12,8},{10,... | collective-permute-start | bytes 1572872 | tf_op jit(solution)/shard_map/ppermute | solution.py:326
  44.6 29.0 %collective-permute-start = (bf16[128,2048]{1,0:T(8,128)(2,1)S(1)}, bf16[128,2048]{1,0:T(8,128)(2,1)S(1)}, u32[]{:S(2)}, u32[]{:S(2)}) collective-permute-start(bf16[128,2048]{1,0:T(8,128)(2,1)S(1)} %bitcast.12), channel_id=1, source_target_pairs={{0,2},{2,0},{4,6},{6,4},{1,3},{3,1},{5,7},{7,5},{8,10},{10,8},{12,... | collective-permute-start | bytes 1572872 | tf_op jit(solution)/shard_map/ppermute | solution.py:325
  46.2 38.1 %collective-permute-start.2 = (bf16[128,2048]{1,0:T(8,128)(2,1)S(1)}, bf16[128,2048]{1,0:T(8,128)(2,1)S(1)}, u32[]{:S(2)}, u32[]{:S(2)}) collective-permute-start(bf16[128,2048]{1,0:T(8,128)(2,1)S(1)} %bitcast.13), channel_id=1, source_target_pairs={{2,4},{4,2},{3,5},{5,3},{10,12},{12,10},{11,13},{13,11},{18,20},{2... | collective-permute-start | bytes 1572872 | tf_op jit(solution)/shard_map/ppermute | solution.py:327
  68.0 25.4 %collective-permute-start.3 = (bf16[128,2048]{1,0:T(8,128)(2,1)S(1)}, bf16[128,2048]{1,0:T(8,128)(2,1)}, u32[]{:S(2)}, u32[]{:S(2)}) collective-permute-start(bf16[128,2048]{1,0:T(8,128)(2,1)S(1)} %collective-permute-done.1.refs_2_), channel_id=1, source_target_pairs={{4,6},{2,0},{5,7},{3,1},{12,14},{10,8},{13,15},{11,9},{20,22},{18,... | collective-permute-start | bytes 1572872 | tf_op jit(solution)/shard_map/ppermute | solution.py:328
  69.3 34.8 %collective-permute-start.11 = (bf16[128,2048]{1,0:T(8,128)(2,1)S(1)}, bf16[128,2048]{1,0:T(8,128)(2,1)}, u32[]{:S(2)}, u32[]{:S(2)}) collective-permute-start(bf16[128,2048]{1,0:T(8,128)(2,1)S(1)} %bitcast.6), channel_id=1, source_target_pairs={{0,2},{2,0},{4,6},{6,4},{1,3},{3,1},{5,7},{7,5},{8,10},{10,8},{12,... | collective-permute-start | bytes 1572872 | tf_op jit(solution)/shard_map/ppermute | solution.py:325
  72.7 32.8 %collective-permute-start.12 = (bf16[128,2048]{1,0:T(8,128)(2,1)S(1)}, bf16[128,2048]{1,0:T(8,128)(2,1)}, u32[]{:S(2)}, u32[]{:S(2)}) collective-permute-start(bf16[128,2048]{1,0:T(8,128)(2,1)S(1)} %bitcast.7), channel_id=1, source_target_pairs={{0,4},{4,0},{2,6},{6,2},{1,5},{5,1},{3,7},{7,3},{8,12},{12,8},{10,... | collective-permute-start | bytes 1572872 | tf_op jit(solution)/shard_map/ppermute | solution.py:326
  73.6 3.5 %copy-start = (bf16[2048,2048]{1,0:T(8,128)(2,1)S(1)}, bf16[2048,2048]{1,0:T(8,128)(2,1)}, u32[]{:S(2)}) copy-start(bf16[2048,2048]{1,0:T(8,128)(2,1)} %refs_1_.1) | copy-start | bytes 25165828
  77.1 34.9 %copy-start.22 = (bf16[3,512,128]{2,1,0:T(8,128)(2,1)S(1)}, bf16[3,512,128]{2,1,0:T(8,128)(2,1)}, u32[]{:S(2)}) copy-start(bf16[3,512,128]{2,1,0:T(8,128)(2,1)} %copy-done.21) | copy-start | bytes 1179652
  77.1 34.9 %copy-start.24 = (bf16[3,512,128]{2,1,0:T(8,128)(2,1)S(1)}, bf16[3,512,128]{2,1,0:T(8,128)(2,1)}, u32[]{:S(2)}) copy-start(bf16[3,512,128]{2,1,0:T(8,128)(2,1)} %copy-done.23) | copy-start | bytes 1179652
  77.1 34.9 %copy-start.26 = (bf16[3,512,128]{2,1,0:T(8,128)(2,1)S(1)}, bf16[3,512,128]{2,1,0:T(8,128)(2,1)}, u32[]{:S(2)}) copy-start(bf16[3,512,128]{2,1,0:T(8,128)(2,1)} %copy-done.25) | copy-start | bytes 1179652
  77.1 34.9 %copy-start.28 = (bf16[3,512,128]{2,1,0:T(8,128)(2,1)S(1)}, bf16[3,512,128]{2,1,0:T(8,128)(2,1)}, u32[]{:S(2)}) copy-start(bf16[3,512,128]{2,1,0:T(8,128)(2,1)} %copy-done.27) | copy-start | bytes 1179652
  82.8 23.2 %collective-permute-start.19 = (bf16[384,512]{1,0:T(8,128)(2,1)S(1)}, bf16[384,512]{1,0:T(8,128)(2,1)S(1)}, u32[]{:S(2)}, u32[]{:S(2)}) collective-permute-start(bf16[384,512]{1,0:T(8,128)(2,1)S(1)} %get-tuple-element.22), channel_id=1, source_target_pairs={{0,8},{8,0},{16,24},{24,16},{1,9},{9,1},{17,25},{25,17},{2,10},{10... | collective-permute-start | bytes 1179656 | tf_op jit(solution)/shard_map/ppermute | solution.py:336
  84.4 23.2 %collective-permute-start.20 = (bf16[384,512]{1,0:T(8,128)(2,1)S(1)}, bf16[384,512]{1,0:T(8,128)(2,1)S(1)}, u32[]{:S(2)}, u32[]{:S(2)}) collective-permute-start(bf16[384,512]{1,0:T(8,128)(2,1)S(1)} %get-tuple-element.23), channel_id=1, source_target_pairs={{0,16},{16,0},{8,24},{24,8},{1,17},{17,1},{9,25},{25,9},{2,18},{18... | collective-permute-start | bytes 1179656 | tf_op jit(solution)/shard_map/ppermute | solution.py:337
  93.4 14.9 %collective-permute-start.21 = (bf16[384,512]{1,0:T(8,128)(2,1)S(1)}, bf16[384,512]{1,0:T(8,128)(2,1)S(1)}, u32[]{:S(2)}, u32[]{:S(2)}) collective-permute-start(bf16[384,512]{1,0:T(8,128)(2,1)S(1)} %get-tuple-element.24), channel_id=1, source_target_pairs={{0,24},{24,0},{8,16},{16,8},{1,25},{25,1},{9,17},{17,9},{2,26},{26... | collective-permute-start | bytes 1179656 | tf_op jit(solution)/shard_map/ppermute | solution.py:338
  95.9 3.4 %copy-start.1 = (bf16[2048,2048]{1,0:T(8,128)(2,1)S(1)}, bf16[2048,2048]{1,0:T(8,128)(2,1)}, u32[]{:S(2)}) copy-start(bf16[2048,2048]{1,0:T(8,128)(2,1)} %refs_1_.1) | copy-start | bytes 25165828
  104.1 5.0 %collective-permute-start.22 = (bf16[128,512]{1,0:T(8,128)(2,1)S(1)}, bf16[128,512]{1,0:T(8,128)(2,1)S(1)}, u32[]{:S(2)}, u32[]{:S(2)}) collective-permute-start(bf16[128,512]{1,0:T(8,128)(2,1)S(1)} %get-tuple-element.26), channel_id=1, source_target_pairs={{0,8},{8,0},{16,24},{24,16},{1,9},{9,1},{17,25},{25,17},{2,10},{10... | collective-permute-start | bytes 393224 | tf_op jit(solution)/shard_map/ppermute | solution.py:336
  105.5 5.0 %collective-permute-start.23 = (bf16[128,512]{1,0:T(8,128)(2,1)S(1)}, bf16[128,512]{1,0:T(8,128)(2,1)S(1)}, u32[]{:S(2)}, u32[]{:S(2)}) collective-permute-start(bf16[128,512]{1,0:T(8,128)(2,1)S(1)} %get-tuple-element.27), channel_id=1, source_target_pairs={{0,16},{16,0},{8,24},{24,8},{1,17},{17,1},{9,25},{25,9},{2,18},{18... | collective-permute-start | bytes 393224 | tf_op jit(solution)/shard_map/ppermute | solution.py:337
  106.1 5.9 %collective-permute-start.24 = (bf16[128,512]{1,0:T(8,128)(2,1)S(1)}, bf16[128,512]{1,0:T(8,128)(2,1)S(1)}, u32[]{:S(2)}, u32[]{:S(2)}) collective-permute-start(bf16[128,512]{1,0:T(8,128)(2,1)S(1)} %get-tuple-element.28), channel_id=1, source_target_pairs={{0,24},{24,0},{8,16},{16,8},{1,25},{25,1},{9,17},{17,9},{2,26},{26... | collective-permute-start | bytes 393224 | tf_op jit(solution)/shard_map/ppermute | solution.py:338
  107.6 13.8 %collective-permute-start.13 = (bf16[128,2048]{1,0:T(8,128)(2,1)S(1)}, bf16[128,2048]{1,0:T(8,128)(2,1)S(1)}, u32[]{:S(2)}, u32[]{:S(2)}) collective-permute-start(bf16[128,2048]{1,0:T(8,128)(2,1)S(1)} %bitcast.8), channel_id=1, source_target_pairs={{2,4},{4,2},{3,5},{5,3},{10,12},{12,10},{11,13},{13,11},{18,20},{2... | collective-permute-start | bytes 1572872 | tf_op jit(solution)/shard_map/ppermute | solution.py:327
  108.3 13.8 %collective-permute-start.15 = (bf16[128,2048]{1,0:T(8,128)(2,1)S(1)}, bf16[128,2048]{1,0:T(8,128)(2,1)S(1)}, u32[]{:S(2)}, u32[]{:S(2)}) collective-permute-start(bf16[128,2048]{1,0:T(8,128)(2,1)S(1)} %bitcast.9), channel_id=1, source_target_pairs={{0,1},{1,0},{2,3},{3,2},{4,5},{5,4},{6,7},{7,6},{8,9},{9,8},{10,11... | collective-permute-start | bytes 1572872 | tf_op jit(solution)/shard_map/ppermute | solution.py:343
  109.0 17.6 %collective-permute-start.14 = (bf16[128,2048]{1,0:T(8,128)(2,1)}, bf16[128,2048]{1,0:T(8,128)(2,1)S(1)}, u32[]{:S(2)}, u32[]{:S(2)}) collective-permute-start(bf16[128,2048]{1,0:T(8,128)(2,1)} %collective-permute-done.12.refs_2_), channel_id=1, source_target_pairs={{4,6},{2,0},{5,7},{3,1},{12,14},{10,8},{13,15},{11,9},{20,22},{18,... | collective-permute-start | bytes 1572872 | tf_op jit(solution)/shard_map/ppermute | solution.py:328
  110.5 18.5 %collective-permute-start.17 = (bf16[128,2048]{1,0:T(8,128)(2,1)}, bf16[128,2048]{1,0:T(8,128)(2,1)S(1)}, u32[]{:S(2)}, u32[]{:S(2)}) collective-permute-start(bf16[128,2048]{1,0:T(8,128)(2,1)} %collective-permute-done.12.refs_2_), channel_id=1, source_target_pairs={{0,1},{1,0},{2,3},{3,2},{4,5},{5,4},{6,7},{7,6},{8,9},{9,8},{10,11... | collective-permute-start | bytes 1572872 | tf_op jit(solution)/shard_map/ppermute | solution.py:343
  111.9 16.2 %collective-permute-start.16 = (bf16[128,2048]{1,0:T(8,128)(2,1)}, bf16[128,2048]{1,0:T(8,128)(2,1)S(1)}, u32[]{:S(2)}, u32[]{:S(2)}) collective-permute-start(bf16[128,2048]{1,0:T(8,128)(2,1)} %collective-permute-done.11.refs_1_), channel_id=1, source_target_pairs={{0,1},{1,0},{2,3},{3,2},{4,5},{5,4},{6,7},{7,6},{8,9},{9,8},{10,11... | collective-permute-start | bytes 1572872 | tf_op jit(solution)/shard_map/ppermute | solution.py:343
  121.4 15.0 %collective-permute-start.25 = (bf16[512,512]{1,0:T(8,128)(2,1)}, bf16[512,512]{1,0:T(8,128)(2,1)}, u32[]{:S(2)}, u32[]{:S(2)}) collective-permute-start(bf16[512,512]{1,0:T(8,128)(2,1)} %get-tuple-element.29.refs_8_), channel_id=1, source_target_pairs={{0,8},{8,0},{16,24},{24,16},{1,9},{9,1},{17,25},{25,17},{2,10},{10... | collective-permute-start | bytes 1572872 | tf_op jit(solution)/shard_map/ppermute | solution.py:336
  122.0 0.8 copy-start.7
  122.8 25.6 %collective-permute-start.26 = (bf16[512,512]{1,0:T(8,128)(2,1)}, bf16[512,512]{1,0:T(8,128)(2,1)}, u32[]{:S(2)}, u32[]{:S(2)}) collective-permute-start(bf16[512,512]{1,0:T(8,128)(2,1)} %get-tuple-element.29.refs_8_), channel_id=1, source_target_pairs={{0,16},{16,0},{8,24},{24,8},{1,17},{17,1},{9,25},{25,9},{2,18},{18... | collective-permute-start | bytes 1572872 | tf_op jit(solution)/shard_map/ppermute | solution.py:337
  126.7 21.8 %collective-permute-start.27 = (bf16[512,512]{1,0:T(8,128)(2,1)}, bf16[512,512]{1,0:T(8,128)(2,1)}, u32[]{:S(2)}, u32[]{:S(2)}) collective-permute-start(bf16[512,512]{1,0:T(8,128)(2,1)} %get-tuple-element.29.refs_8_), channel_id=1, source_target_pairs={{0,24},{24,0},{8,16},{16,8},{1,25},{25,1},{9,17},{17,9},{2,26},{26... | collective-permute-start | bytes 1572872 | tf_op jit(solution)/shard_map/ppermute | solution.py:338
  128.2 0.8 copy-start.11
  129.0 20.6 %collective-permute-start.18 = (bf16[128,2048]{1,0:T(8,128)(2,1)S(1)}, bf16[128,2048]{1,0:T(8,128)(2,1)}, u32[]{:S(2)}, u32[]{:S(2)}) collective-permute-start(bf16[128,2048]{1,0:T(8,128)(2,1)S(1)} %broadcast_select_fusion.refs_3_), channel_id=1, source_target_pairs={{0,1},{1,0},{2,3},{3,2},{4,5},{5,4},{6,7},{7,6},{8,9},{9,8},{10,11... | collective-permute-start | bytes 1572872 | tf_op jit(solution)/shard_map/ppermute | solution.py:343
  129.0 0.8 copy-start.9
  129.8 19.9 %collective-permute-start.28 = (bf16[512,512]{1,0:T(8,128)(2,1)}, bf16[512,512]{1,0:T(8,128)(2,1)}, u32[]{:S(2)}, u32[]{:S(2)}) collective-permute-start(bf16[512,512]{1,0:T(8,128)(2,1)} %get-tuple-element.29.refs_8_), channel_id=1, source_target_pairs={{0,1},{1,0},{2,3},{3,2},{4,5},{5,4},{6,7},{7,6},{8,9},{9,8},{10,11... | collective-permute-start | bytes 1572872 | tf_op jit(solution)/shard_map/ppermute | solution.py:343
  136.4 13.8 %collective-permute-start.29 = (bf16[512,512]{1,0:T(8,128)(2,1)}, bf16[512,512]{1,0:T(8,128)(2,1)}, u32[]{:S(2)}, u32[]{:S(2)}) collective-permute-start(bf16[512,512]{1,0:T(8,128)(2,1)} %collective-permute-done.25.refs_9_), channel_id=1, source_target_pairs={{0,1},{1,0},{2,3},{3,2},{4,5},{5,4},{6,7},{7,6},{8,9},{9,8},{10,11... | collective-permute-start | bytes 1572872 | tf_op jit(solution)/shard_map/ppermute | solution.py:343
  148.4 2.3 %collective-permute-start.30 = (bf16[512,512]{1,0:T(8,128)(2,1)}, bf16[512,512]{1,0:T(8,128)(2,1)}, u32[]{:S(2)}, u32[]{:S(2)}) collective-permute-start(bf16[512,512]{1,0:T(8,128)(2,1)} %collective-permute-done.26.refs_10_), channel_id=1, source_target_pairs={{0,1},{1,0},{2,3},{3,2},{4,5},{5,4},{6,7},{7,6},{8,9},{9,8},{10,11... | collective-permute-start | bytes 1572872 | tf_op jit(solution)/shard_map/ppermute | solution.py:343
  148.4 3.0 %collective-permute-start.31 = (bf16[512,512]{1,0:T(8,128)(2,1)}, bf16[512,512]{1,0:T(8,128)(2,1)}, u32[]{:S(2)}, u32[]{:S(2)}) collective-permute-start(bf16[512,512]{1,0:T(8,128)(2,1)} %collective-permute-done.27.refs_11_), channel_id=1, source_target_pairs={{0,1},{1,0},{2,3},{3,2},{4,5},{5,4},{6,7},{7,6},{8,9},{9,8},{10,11... | collective-permute-start | bytes 1572872 | tf_op jit(solution)/shard_map/ppermute | solution.py:343
  149.6 19.9 %collective-permute-start.4 = (bf16[128,2048]{1,0:T(8,128)(2,1)S(1)}, bf16[128,2048]{1,0:T(8,128)(2,1)S(1)}, u32[]{:S(2)}, u32[]{:S(2)}) collective-permute-start(bf16[128,2048]{1,0:T(8,128)(2,1)S(1)} %bitcast.15), channel_id=1, source_target_pairs={{0,1},{1,0},{2,3},{3,2},{4,5},{5,4},{6,7},{7,6},{8,9},{9,8},{10,11... | collective-permute-start | bytes 1572872 | tf_op jit(solution)/shard_map/ppermute | solution.py:343
  149.7 20.6 %collective-permute-start.5 = (bf16[128,2048]{1,0:T(8,128)(2,1)S(1)}, bf16[128,2048]{1,0:T(8,128)(2,1)S(1)}, u32[]{:S(2)}, u32[]{:S(2)}) collective-permute-start(bf16[128,2048]{1,0:T(8,128)(2,1)S(1)} %collective-permute-done.refs_1_), channel_id=1, source_target_pairs={{0,1},{1,0},{2,3},{3,2},{4,5},{5,4},{6,7},{7,6},{8,9},{9,8},{10,11... | collective-permute-start | bytes 1572872 | tf_op jit(solution)/shard_map/ppermute | solution.py:343
  150.2 20.9 %collective-permute-start.6 = (bf16[128,2048]{1,0:T(8,128)(2,1)S(1)}, bf16[128,2048]{1,0:T(8,128)(2,1)S(1)}, u32[]{:S(2)}, u32[]{:S(2)}) collective-permute-start(bf16[128,2048]{1,0:T(8,128)(2,1)S(1)} %collective-permute-done.1.refs_2_), channel_id=1, source_target_pairs={{0,1},{1,0},{2,3},{3,2},{4,5},{5,4},{6,7},{7,6},{8,9},{9,8},{10,11... | collective-permute-start | bytes 1572872 | tf_op jit(solution)/shard_map/ppermute | solution.py:343
  150.7 21.2 %collective-permute-start.7 = (bf16[128,2048]{1,0:T(8,128)(2,1)S(1)}, bf16[128,2048]{1,0:T(8,128)(2,1)S(1)}, u32[]{:S(2)}, u32[]{:S(2)}) collective-permute-start(bf16[128,2048]{1,0:T(8,128)(2,1)S(1)} %broadcast_select_fusion.1.refs_3_.refs_0_), channel_id=1, source_target_pairs={{0,1},{1,0},{2,3},{3,2},{4,5},{5,4},{6,7},{7,6},{8,9},{9,8},{10,11... | collective-permute-start | bytes 1572872 | tf_op jit(solution)/shard_map/ppermute | solution.py:343
  151.4 1.0 copy-start.8
  152.5 1.0 copy-start.10
  153.5 1.0 copy-start.12
  169.5 0.8 copy-start.13
  170.3 0.8 copy-start.15
  171.1 0.8 copy-start.17
  171.9 0.8 copy-start.19
  172.7 1.0 copy-start.14
  173.8 1.0 copy-start.16
  174.8 1.0 copy-start.18
  175.8 1.0 copy-start.20
  (2 other events, 1.4 us)
Sparse Core Ops, SparseCore 0:
  42.1 37.0 all-gather.2
  149.7 54.9 all-reduce.1

commit v2 on v1

--- a/solution.py
+++ b/solution.py
@@ -13,14 +13,15 @@
 VMEM = pl.BlockSpec(memory_space=pltpu.VMEM)
 SMEM = pl.BlockSpec(memory_space=pltpu.SMEM)
 ANY = pl.BlockSpec(memory_space=pl.ANY)
-
-
-def params(mib):
-    return pltpu.CompilerParams(vmem_limit_bytes=mib * MIB)
-
-
-def cost(flops, nbytes):
-    return pl.CostEstimate(flops=int(flops), bytes_accessed=int(nbytes), transcendentals=0)
+TILE = 256
+
+
+def params():
+    return pltpu.CompilerParams(vmem_limit_bytes=60 * MIB)
+
+
+def cost(us):
+    return pl.CostEstimate(flops=int(us * 1.15e9), bytes_accessed=0, transcendentals=0)
 
 
 def split_two(x):
@@ -28,26 +29,23 @@
     return hi, (x - hi.astype(f32)).astype(bf16)
 
 
-def turn_kernel(rows, pos_ref, q_ref, k_ref, v_ref, *outs):
-    width = outs[0].shape[1]
-    for j, out in enumerate(outs):
-        columns = pl.ds(pl.multiple_of((pos_ref[0] ^ j) * width, 128), width)
+def turn_kernel(q_ref, k_ref, v_ref, out_ref):
+    width = out_ref.shape[2]
+    for j in range(out_ref.shape[0]):
         for n, src in enumerate((q_ref, k_ref, v_ref)):
-            out[n] = src[0, :, columns].T
-
-
-def turn_branches(pos, q, k, v, rows):
+            out_ref[j, n] = src[0, :, j * width : (j + 1) * width].T
+
+
+def turn_branches(q, k, v, rows):
     _, toks, channels = q.shape
-    width = channels // rows
-    out = jax.ShapeDtypeStruct((3, width, toks), bf16)
     return pl.pallas_call(
-        functools.partial(turn_kernel, rows),
-        out_shape=[out] * rows,
-        in_specs=[SMEM] + [VMEM] * 3,
-        out_specs=[VMEM] * rows,
-        compiler_params=params(32),
-        cost_estimate=cost(0, 4 * q.size * 3),
-    )(pos, q, k, v)
+        turn_kernel,
+        out_shape=jax.ShapeDtypeStruct((rows, 3, channels // rows, toks), bf16),
+        in_specs=[VMEM] * 3,
+        out_specs=VMEM,
+        compiler_params=params(),
+        cost_estimate=cost(3),
+    )(q, k, v)
 
 
 def tap_matrix(f_ref, row):
@@ -64,19 +62,18 @@
     return lax.dot_general(a, b, (dims, ((), ())), preferred_element_type=f32)
 
 
-def forward_kernel(size, pos_ref, f_ref, b0, b1, b2, b3, out_ref, mh, ml, qs, gt):
+def forward_kernel(size, pos_ref, f_ref, parts_ref, out_ref, mh, ml, qs, gt):
     n = f_ref.shape[1]
     width, toks = gt.shape
     blocks = toks // n
     groups = width // size
     mh[:, :n] = jnp.zeros((width, n), bf16)
     ml[:, :n] = jnp.zeros((width, n), bf16)
-    for j, b in enumerate((b0, b1, b2, b3)):
-        place = pl.multiple_of((pos_ref[0] ^ j) * n, n)
-        hi, lo = split_two(b[1].astype(f32) * b[2].astype(f32))
-        mh[:, pl.ds(place + n, n)] = hi
-        ml[:, pl.ds(place + n, n)] = lo
-        qs[:, pl.ds(place, n)] = b[0]
+    for j in range(blocks):
+        hi, lo = split_two(parts_ref[j, 1].astype(f32) * parts_ref[j, 2].astype(f32))
+        mh[:, (j + 1) * n : (j + 2) * n] = hi
+        ml[:, (j + 1) * n : (j + 2) * n] = lo
+        qs[:, j * n : (j + 1) * n] = parts_ref[j, 0]
 
     def one(g, carry):
         rows = pl.ds(pl.multiple_of(g * size, size), size)
@@ -96,12 +93,12 @@
 
 
 def forward(pos, filters, parts, size):
-    _, width, n = parts[0].shape
-    toks = n * len(parts)
+    rows, _, width, n = parts.shape
+    toks = n * rows
     return pl.pallas_call(
         functools.partial(forward_kernel, size),
         out_shape=jax.ShapeDtypeStruct((toks, width), bf16),
-        in_specs=[SMEM] + [VMEM] * 5,
+        in_specs=[SMEM] + [VMEM] * 2,
         out_specs=VMEM,
         scratch_shapes=[
             pltpu.VMEM((width, toks + n), bf16),
@@ -109,18 +106,14 @@
             pltpu.VMEM((width, toks), bf16),
             pltpu.VMEM((width, toks), f32),
         ],
-        compiler_params=params(32),
-        cost_estimate=cost(8e9, 2 * 4 * toks * width),
-    )(pos, filters, *parts)
-
-
-def backward_kernel(size, counts, pos_ref, f_ref, b0, b1, b2, b3, *refs):
+        compiler_params=params(),
+        cost_estimate=cost(6),
+    )(pos, filters, parts)
+
+
+def backward_kernel(size, counts, pos_ref, f_ref, parts_ref, *refs):
     n = f_ref.shape[1]
-    deltas, (taps_ref, out_ref), (dh, dl, mh, ml, qs, ks, sums) = (
-        refs[: -9],
-        refs[-9:-7],
-        refs[-7:],
-    )
+    deltas, out_ref, (dh, dl, mh, ml, qs, ks, sums) = refs[:-8], refs[-8], refs[-7:]
     width, toks = qs.shape
     blocks = toks // n
     groups = width // size
@@ -130,19 +123,19 @@
     ml[:, :n] = zero
     dh[:, toks:] = zero
     dl[:, toks:] = zero
-    for j, b in enumerate((b0, b1, b2, b3)):
-        place = pl.multiple_of((row ^ j) * n, n)
-        hi, lo = split_two(b[1].astype(f32) * b[2].astype(f32))
-        mh[:, pl.ds(place + n, n)] = hi
-        ml[:, pl.ds(place + n, n)] = lo
-        qs[:, pl.ds(place, n)] = b[0]
-        ks[:, pl.ds(place, n)] = b[1]
+    for j in range(blocks):
+        hi, lo = split_two(parts_ref[j, 1].astype(f32) * parts_ref[j, 2].astype(f32))
+        mh[:, (j + 1) * n : (j + 2) * n] = hi
+        ml[:, (j + 1) * n : (j + 2) * n] = lo
+        qs[:, j * n : (j + 1) * n] = parts_ref[j, 0]
+        ks[:, j * n : (j + 1) * n] = parts_ref[j, 1]
     slot = 0
     for i, count in enumerate(counts):
         for m in range(count):
             place = pl.multiple_of((col ^ slot) * n, n)
-            own, first, second, third = (ref[m * n : (m + 1) * n, :].astype(f32) for ref in deltas[4 * i : 4 * i + 4])
-            delta = (own + first) + (second + third)
+            at = slice(m * n, (m + 1) * n)
+            own = deltas[2 * i][at, :]
+            delta = sum(jnp.where(row == j, own, deltas[2 * i + 1][j, at, :].astype(f32)) for j in range(blocks))
             hi, lo = split_two(delta.T * qs[:, pl.ds(place, n)].astype(f32))
             dh[:, pl.ds(place, n)] = hi
             dl[:, pl.ds(place, n)] = lo
@@ -182,46 +175,46 @@
     total = sums[pl.ds(0, groups, stride=8), :]
     for i in range(1, 8):
         total = total + pltpu.roll(sums[pl.ds(i, groups, stride=8), :], n - i, 1)
-    taps_ref[...] = total
+    hi, lo = split_two(total)
+    half = groups // 2
+    out_ref[width:, :] = jnp.concatenate([hi[:half], hi[half:], lo[:half], lo[half:]], axis=1)
 
 
 def backward(pos, filters, parts, deltas, counts, size):
-    _, width, n = parts[0].shape
-    toks = n * len(parts)
+    rows, _, width, n = parts.shape
+    toks = n * rows
     groups = width // size
     return pl.pallas_call(
         functools.partial(backward_kernel, size, counts),
-        out_shape=[
-            jax.ShapeDtypeStruct((groups, n), f32),
-            jax.ShapeDtypeStruct((width, toks), bf16),
-        ],
-        in_specs=[SMEM] + [VMEM] * (5 + len(deltas)),
-        out_specs=[VMEM] * 2,
+        out_shape=jax.ShapeDtypeStruct((width + groups // 2, toks), bf16),
+        in_specs=[SMEM] + [VMEM] * (2 + len(deltas)),
+        out_specs=VMEM,
         scratch_shapes=[pltpu.VMEM((width, toks + n), bf16)] * 4
         + [pltpu.VMEM((width, toks), bf16)] * 2
         + [pltpu.VMEM((8 * groups, n), f32)],
-        compiler_params=params(40),
-        cost_estimate=cost(8e9, 2 * 8 * toks * width),
-    )(pos, filters, *parts, *deltas)
+        compiler_params=params(),
+        cost_estimate=cost(12),
+    )(pos, filters, parts, *deltas)
 
 
 def project_kernel(count, pos_ref, *refs):
-    slots, w_ref, outs = refs[:count], refs[count], refs[count + 1 : count + 5]
-    wide, sem = refs[count + 5 :]
-    width = outs[0].shape[1]
-    n = slots[0].shape[0]
+    slots, (w_ref, own_ref, out_ref, wide, sem) = refs[:count], refs[count:]
+    rows, _, width = out_ref.shape
 
     def fetch(j):
-        columns = pl.ds(pl.multiple_of((pos_ref[0] ^ j) * width, 128), width)
-        return pltpu.make_async_copy(w_ref.at[:, columns], wide.at[j], sem.at[j])
-
-    order = (3, 1, 2, 0)
-    for j in order:
+        return pltpu.make_async_copy(w_ref.at[:, pl.ds(j * width, width)], wide.at[j], sem.at[j])
+
+    for j in range(rows):
         fetch(j).start()
     grads = jnp.concatenate([slot[...] for slot in slots], axis=0)
-    for j in order:
+    for j in range(rows):
         fetch(j).wait()
-        outs[j][...] = dot(grads, wide[j]).astype(outs[j].dtype)
+        part = dot(grads, wide[j])
+        out_ref[j] = part.astype(bf16)
+
+        @pl.when(pos_ref[0] == j)
+        def _():
+            own_ref[...] = part
 
 
 def project(pos, slots, weight, rows):
@@ -230,93 +223,156 @@
     toks = sum(slot.shape[0] for slot in slots)
     return pl.pallas_call(
         functools.partial(project_kernel, len(slots)),
-        out_shape=[jax.ShapeDtypeStruct((toks, width), f32 if j == 0 else bf16) for j in range(rows)],
+        out_shape=[
+            jax.ShapeDtypeStruct((toks, width), f32),
+            jax.ShapeDtypeStruct((rows, toks, width), bf16),
+        ],
         in_specs=[SMEM] + [VMEM] * len(slots) + [ANY],
-        out_specs=[VMEM] * rows,
+        out_specs=[VMEM] * 2,
         scratch_shapes=[pltpu.VMEM((rows, depth, width), bf16), pltpu.SemaphoreType.DMA((rows,))],
-        compiler_params=params(40),
-        cost_estimate=cost(2 * toks * depth * channels, 2 * weight.size),
+        compiler_params=params(),
+        cost_estimate=cost(8),
     )(pos, *slots, weight)
 
 
-def gradient_kernel(turned, pos_ref, *refs):
-    (out_ref, left, right, buf, sem_in, sem_out) = refs[-6:]
-    sources = refs[:-6]
-    n = 128
-    row, col, dp = pos_ref[0], pos_ref[1], pos_ref[2]
-    copies = []
-
-    def fetch(src, dst):
-        copies.append(pltpu.make_async_copy(src, dst, sem_in.at[len(copies)]))
-
-    seq = left.shape[0] // 2 if turned else left.shape[1] // 2
-    if turned:
-        slots, gathered = sources[:8], sources[8]
-        for i, slot in enumerate(slots):
-            owner = dp if i < 4 else 1 - dp
-            fetch(slot, left.at[pl.ds(pl.multiple_of(owner * seq + (col ^ (i % 4)) * n, n), n), :])
-        width = gathered.shape[2]
-        for i in range(8):
-            fetch(gathered.at[i], right.at[pl.ds((i % 2) * seq, seq), pl.ds((i // 2) * width, width)])
-    else:
-        slots, pieces = sources[:8], sources[8:]
-        for i, slot in enumerate(slots):
-            place = pl.multiple_of((i // 4) * seq + (col ^ (i % 4)) * n, n)
-            fetch(slot, right.at[pl.ds(place, n), :])
-        width = pieces[0].shape[0]
-        for i, piece in enumerate(pieces):
-            place = pl.multiple_of((row ^ (i % 4)) * width, width)
-            fetch(piece, left.at[pl.ds(place, width), pl.ds((i // 4) * seq, seq)])
+def product(left, right, buf, out_ref, sem_out, turned, places):
+    tile = buf.shape[1]
+
+    def send(i):
+        at = pl.ds(pl.multiple_of(places[i], tile), tile)
+        return pltpu.make_async_copy(buf.at[i % 2], out_ref.at[at, :], sem_out.at[i % 2])
+
+    for i in range(len(places)):
+        if i >= 2:
+            send(i - 2).wait()
+        at = slice(i * tile, (i + 1) * tile)
+        buf[i % 2] = dot(left[:, at].T if turned else left[at, :], right[...])
+        send(i).start()
+    for i in range(max(0, len(places) - 2), len(places)):
+        send(i).wait()
+
+
+def run_copies(pairs, sem):
+    copies = [pltpu.make_async_copy(src, dst, sem.at[i]) for i, (src, dst) in enumerate(pairs)]
     for copy in copies:
         copy.start()
     for copy in copies:
         copy.wait()
+
+
+def out_kernel(n, layout, pos_ref, *refs):
+    slots, pieces = refs[:8], refs[8 : 8 + len(layout)]
+    out_ref, left, right, buf, sem_in, sem_out = refs[8 + len(layout) :]
+    row, col = pos_ref[0], pos_ref[1]
+    seq = left.shape[0] // 2
+    width = right.shape[1] // 4
+    pairs = []
+    for i, slot in enumerate(slots):
+        place = pl.multiple_of((i // 4) * seq + (col ^ (i % 4)) * n, n)
+        pairs.append((slot, left.at[pl.ds(place, n), :]))
+    for piece, (block, owner, first, count) in zip(pieces, layout, strict=True):
+        columns = pl.ds(pl.multiple_of((row ^ block) * width, width), width)
+        pairs.append((piece, right.at[pl.ds(owner * seq + first, count), columns]))
+    run_copies(pairs, sem_in)
     tile = buf.shape[1]
-    tiles = out_ref.shape[0] // tile
-
-    def send(i):
-        at = pl.ds(pl.multiple_of(i * tile, tile), tile)
-        return pltpu.make_async_copy(buf.at[i % 2], out_ref.at[at, :], sem_out.at[i % 2])
-
-    def one(i, carry):
-        at = pl.ds(pl.multiple_of(i * tile, tile), tile)
-
-        @pl.when(i >= 2)
-        def _():
-            send(i - 2).wait()
-
-        lhs = left[:, at].T if turned else left[at, :]
-        buf[i % 2] = dot(lhs, right[...])
-        send(i).start()
-        return carry
-
-    lax.fori_loop(0, tiles, one, 0)
-    send(tiles - 2).wait()
-    send(tiles - 1).wait()
-
-
-def gradient(pos, sources, toks, left_width, right_width, turned):
-    tile = 256
+    product(left, right, buf, out_ref, sem_out, True, [i * tile for i in range(out_ref.shape[0] // tile)])
+
+
+def out_gradient(pos, slots, pieces, layout):
+    n, left_width = slots[0].shape
+    seq, width = pieces[0].shape
+    right_width = 4 * width
+    toks = 2 * seq
     return pl.pallas_call(
-        functools.partial(gradient_kernel, turned),
+        functools.partial(out_kernel, n, layout),
         out_shape=jax.ShapeDtypeStruct((left_width, right_width), f32),
-        in_specs=[SMEM] + [ANY] * len(sources),
+        in_specs=[SMEM] + [ANY] * (8 + len(pieces)),
         out_specs=ANY,
         scratch_shapes=[
-            pltpu.VMEM((toks, left_width) if turned else (left_width, toks), bf16),
+            pltpu.VMEM((toks, left_width), bf16),
             pltpu.VMEM((toks, right_width), bf16),
-            pltpu.VMEM((2, tile, right_width), f32),
-            pltpu.SemaphoreType.DMA((16,)),
+            pltpu.VMEM((2, TILE, right_width), f32),
+            pltpu.SemaphoreType.DMA((8 + len(pieces),)),
             pltpu.SemaphoreType.DMA((2,)),
         ],
-        compiler_params=params(48),
-        cost_estimate=cost(2 * toks * left_width * right_width, 4 * left_width * right_width),
-    )(pos, *sources)
+        compiler_params=params(),
+        cost_estimate=cost(16),
+    )(pos, *slots, *pieces)
+
+
+def value_kernel(n, width, which, layout, with_taps, joined, pos_ref, *refs):
+    inputs, refs = refs[:8], refs[8:]
+    pieces, refs = refs[: len(layout)], refs[len(layout) :]
+    if with_taps:
+        ends, refs = refs[:8], refs[8:]
+    if joined:
+        refs = refs[1:]
+    out_ref, refs = refs[0], refs[1:]
+    if with_taps:
+        taps_ref, refs = refs[0], refs[1:]
+        tails, refs = refs[-1], refs[:-1]
+    left, right, buf, sem_in, sem_out = refs
+    row, col = pos_ref[0], pos_ref[1]
+    seq = left.shape[1] // 2
+    pairs = []
+    for i, slot in enumerate(inputs):
+        place = pl.multiple_of((i // 4) * seq + (col ^ (i % 4)) * n, n)
+        pairs.append((slot, right.at[pl.ds(place, n), :]))
+    for piece, (block, owner, first, count) in zip(pieces, layout, strict=True):
+        place = left.at[pl.ds(block * width + first, count), pl.ds(owner * seq, seq)]
+        pairs.append((piece.at[pl.ds(0, count), :], place))
+    if with_taps:
+        half = tails.shape[1]
+        for i, end in enumerate(ends):
+            pairs.append((end.at[pl.ds(end.shape[0] - half, half), :], tails.at[i]))
+    run_copies(pairs, sem_in)
+    if with_taps:
+        lanes = taps_ref.shape[1]
+        for j in range(4):
+            both = tails[j].astype(f32), tails[j + 4].astype(f32)
+            cut = [[t[:, i * lanes : (i + 1) * lanes] for i in range(4)] for t in both]
+            for h in range(2):
+                place = pl.multiple_of((row ^ j) * 2 * half + h * half, half)
+                taps_ref[pl.ds(place, half), :] = (cut[0][h] + cut[0][h + 2]) + (cut[1][h] + cut[1][h + 2])
+    tile = buf.shape[1]
+    places = [(row ^ j) * width + i * tile for j in which for i in range(width // tile)]
+    product(left, right, buf, out_ref, sem_out, False, places)
+
+
+def value_part(pos, inputs, pieces, layout, which, width, ends=(), taps_shape=None, partial=None):
+    n, right_width = inputs[0].shape
+    seq = pieces[0].shape[1]
+    with_taps, joined = taps_shape is not None, partial is not None
+    out_shape = [jax.ShapeDtypeStruct((4 * width, right_width), f32)]
+    scratch = [
+        pltpu.VMEM((len(which) * width, 2 * seq), bf16),
+        pltpu.VMEM((2 * seq, right_width), bf16),
+        pltpu.VMEM((2, TILE, right_width), f32),
+        pltpu.SemaphoreType.DMA((8 + len(pieces) + len(ends),)),
+        pltpu.SemaphoreType.DMA((2,)),
+    ]
+    operands = [pos, *inputs, *pieces, *ends]
+    aliases = {}
+    if with_taps:
+        out_shape.append(jax.ShapeDtypeStruct(taps_shape, f32))
+        scratch.append(pltpu.VMEM((8, 16, seq), bf16))
+    if joined:
+        aliases = {len(operands): 0}
+        operands.append(partial)
+    return pl.pallas_call(
+        functools.partial(value_kernel, n, width, which, layout, with_taps, joined),
+        out_shape=out_shape,
+        in_specs=[SMEM] + [ANY] * (len(operands) - 1),
+        out_specs=[ANY, VMEM][: len(out_shape)],
+        scratch_shapes=scratch,
+        input_output_aliases=aliases,
+        compiler_params=params(),
+        cost_estimate=cost(10),
+    )(*operands)
 
 
 near = [(0, 1), (1, 0), (2, 3), (3, 2)]
 far = [(0, 2), (2, 0), (1, 3), (3, 1)]
-across = [(0, 3), (3, 0), (1, 2), (2, 1)]
 swap = [(0, 1), (1, 0)]
 
 
@@ -330,17 +386,28 @@
     return [x, first, second, third]
 
 
-def row_exchange(pieces):
+def swap_rows(x):
+    return lax.all_to_all(x, "row", split_axis=0, concat_axis=0, tiled=True)
+
+
+def row_gather(x, half):
+    beside = lax.ppermute(x, "row", near)
+    above = lax.ppermute(x, "row", far)
     return [
-        pieces[0],
-        lax.ppermute(pieces[1], "row", near),
-        lax.ppermute(pieces[2], "row", far),
-        lax.ppermute(pieces[3], "row", across),
+        x,
+        beside,
+        above,
+        lax.ppermute(beside[:half], "row", far),
+        lax.ppermute(above[half:], "row", near),
     ]
 
 
 def other_core(xs):
     return [lax.ppermute(x, "dp", swap) for x in xs]
+
+
+def after(pos, x):
+    return lax.optimization_barrier((pos, x))[0]
 
 
 def local(grad_output, block_input, query_branch, key_branch, value_branch, out_weight, filters):
@@ -349,38 +416,55 @@
     channels = query_branch.shape[2]
     size = channels // filters.shape[0]
     width = channels // rows
-    local_groups = width // size
     pos = jnp.stack([lax.axis_index("row"), lax.axis_index("col"), lax.axis_index("dp")]).astype(jnp.int32)
 
     grads = line_slots(grad_output[0])
-    turned = turn_branches(pos, query_branch, key_branch, value_branch, rows)
-    parts = row_exchange(turned)
-    gated = forward(pos, filters, parts, size)
-    gated_all = lax.all_gather(gated, ("row", "dp"), axis=0)
-    inputs = line_slots(block_input[0])
+    turned = turn_branches(query_branch, key_branch, value_branch, rows)
+    parts = swap_rows(turned)
+    held = lax.optimization_barrier((block_input[0], grads[3]))
+    inputs = line_slots(held[0])
 
     counts = (3, 1)
     deltas = []
     for chosen in (grads[:3], grads[3:]):
-        deltas += row_exchange(project(pos, chosen, out_weight, rows))
-    taps, value_grad = backward(pos, filters, parts, deltas, counts, size)
-    values = row_exchange([value_grad] * 4)
-
-    out_grad = gradient(
-        pos, grads + other_core(grads) + [gated_all], 2 * rows * toks, grad_output.shape[2], channels, True
-    )
-    weight_grad = gradient(
+        own, sums = project(pos, chosen, out_weight, rows)
+        pos = after(pos, own)
+        if deltas:
+            sums = after(sums, deltas[-1])
+        deltas += [own, swap_rows(sums)]
+    gated = forward(pos, filters, parts, size)
+    seq = rows * toks
+    gated_all = row_gather(gated, seq // 2)
+    mine = backward(after(pos, (gated, inputs[1], inputs[2])), filters, parts, deltas, counts, size)
+    pos, *late = lax.optimization_barrier((pos, mine, *grads, *gated_all, *inputs[:3]))
+    mine, grads, gated_all, inputs = late[0], late[1:5], late[5:10], late[10:] + inputs[3:]
+    half = width // 2
+    values = row_gather(mine, half)
+    _, beside, above, *corner = values
+    others = other_core(values)
+    inputs = inputs + other_core(inputs)
+    gated_all = gated_all + other_core(gated_all)
+    grads_all = grads + other_core(grads)
+    cuts = [(0, 0, seq), (1, 0, seq), (2, 0, seq), (3, 0, seq // 2), (3, seq // 2, seq // 2)]
+    layout = [(block, owner, first, count) for owner in (0, 1) for block, first, count in cuts]
+
+    out_grad = out_gradient(pos, grads_all, gated_all, layout)
+    three = [(block, owner, 0, width) for block in range(3) for owner in (0, 1)]
+    pieces = [piece for pair in zip(values[:3], others[:3], strict=True) for piece in pair]
+    value_grad = value_part(after(pos, out_grad), inputs, pieces, three, (0, 1, 2), width)[0]
+    halves = [(0, 0, 0, half), (0, 0, half, half), (0, 1, 0, half), (0, 1, half, half)]
+    value_grad, taps = value_part(
         pos,
-        inputs + other_core(inputs) + values + other_core(values),
-        2 * rows * toks,
-        channels,
-        block_input.shape[2],
-        False,
-    )
-    spread = lax.dynamic_update_slice_in_dim(
-        jnp.zeros(filters.shape, f32), taps, lax.axis_index("row") * local_groups, 0
-    )
-    return (out_grad, weight_grad, lax.psum(spread, ("row", "dp")))
+        inputs,
+        corner + others[3:],
+        halves,
+        (3,),
+        width,
+        ends=[mine, beside, above, corner[1], *others[:3], others[4]],
+        taps_shape=filters.shape,
+        partial=value_grad,
+    )
+    return (out_grad, value_grad, taps)
 
 
 def toeplitz(taps, tok_rows, causal):

time: 214 us -> 168 us (0.79)
  waiting for transfers between devices: 84.8 us -> 44.8 us
  local copies, waits for them, and re-layouts: 28.8 us -> 9.1 us
  Pallas kernels: 54.1 us -> 71.2 us
  between operations: 14.3 us -> 1.21 us
  starting transfers between devices: 29.7 us -> 38.3 us
    unnamed x65 -> x50, local copies, waits for them, and re-layouts: 28.8 us -> 6.43 us
    ppermute x12 -> x8, waiting for transfers between devices: 37.6 us -> 17 us  [the longest x2 15.5 us: row_gather(): above = lax.ppermute(x, 'row', far)]
    psum x1 -> x0, waiting for transfers between devices: 12.9 us -> none  [local(): return (out_grad, weight_grad, lax.psum(spread, ('row', 'dp')))]
    all_to_all x0 -> x3, starting transfers between devices: none -> 10.9 us  [swap_rows(): return lax.all_to_all(x, 'row', split_axis=0, concat_axis=0, tiled=True)]
    pallas_call x3 -> x4, Pallas kernels: 30.8 us -> 39.6 us  [the longest x2 20.7 us: value_part(): pl.pallas_call(functools.partial(value_kernel, n, width, which, layout, w...]
    ppermute x2, waiting for transfers between devices: 10.9 us -> 3.9 us  [line_slots(): passed = lax.ppermute(second, 'col', [(2, 3), (1, 0)])]
    ppermute x12 -> x8, starting transfers between devices: 15.1 us -> 9.18 us  [the longest x2 3.98 us: row_gather(): above = lax.ppermute(x, 'row', far)]
    ppermute x2, waiting for transfers between devices: 21.1 us -> 15.9 us  [line_slots(): second = lax.ppermute(x, 'col', far)]
  transfers between devices with their start and end apart: 34 -> 37, of which waited for: 13 -> 12; matrix products, arithmetic and copies ran while one was open for 1% -> 3% of each run, Pallas kernels for 23% -> 38%
where the time goes in v2:
time: 168 us; the launch traced here: 167 us
  Pallas kernels  71.2 us (42%)
  waiting for transfers between devices  44.8 us (27%)
  starting transfers between devices  38.3 us (23%)
  local copies, waits for them, and re-layouts  9.1 us (5%)
  other arithmetic  2.52 us (2%)
    pallas_call x2, Pallas kernels, value_part(): pl.pallas_call(functools.partial(value_kernel, n, width, which, layout, w...  20.7 us
    pallas_call x1, Pallas kernels, out_gradient(): pl.pallas_call(functools.partial(out_kernel, n, layout), out_shape=jax.Sh...  15.9 us
    ppermute x2, waiting for transfers between devices, line_slots(): second = lax.ppermute(x, 'col', far)  15.9 us
    ppermute x2, waiting for transfers between devices, row_gather(): above = lax.ppermute(x, 'row', far)  15.5 us
    pallas_call x2, Pallas kernels, project(): pl.pallas_call(functools.partial(project_kernel, len(slots)), out_shape=[...  14.3 us
    pallas_call x1, Pallas kernels, backward(): pl.pallas_call(functools.partial(backward_kernel, size, counts), out_shap...  11.7 us
    all_to_all x3, starting transfers between devices, swap_rows(): return lax.all_to_all(x, 'row', split_axis=0, concat_axis=0, tiled=True)  10.9 us
    ppermute x2, starting transfers between devices, line_slots(): second = lax.ppermute(x, 'col', far)  6.51 us
  transfers between devices with their start and end apart: 37, of which 12 were waited for; matrix products, arithmetic and copies ran while one was open for 3% of the time, Pallas kernels for 38%

profile of v2, /device:TPU:0, one launch (start us, length us, event | category | flops | bytes accessed | tf_op | source)
XLA Modules:
  0.0 167.1 jit_solution(5429865165312233492)
XLA Ops:
  0.6 4.1 %collective-permute-start.1 = (bf16[128,2048]{1,0:T(8,128)(2,1)}, bf16[128,2048]{1,0:T(8,128)(2,1)}, u32[]{:S(2)}, u32[]{:S(2)}) collective-permute-start(bf16[128,2048]{1,0:T(8,128)(2,1)} %bitcast.5), channel_id=1, source_target_pairs={{0,4},{4,0},{2,6},{6,2},{1,5},{5,1},{3,7},{7,3},{8,12},{12,8},{10,... | collective-permute-start | bytes 1572872 | tf_op jit(solution)/shard_map/ppermute | solution.py:382
  4.7 1.6 collective-permute-start
  6.3 0.7 collective-permute-start.2
  7.0 3.0 %shard_map.96 = bf16[4,3,512,128]{3,2,1,0:T(8,128)(2,1)} custom-call(bf16[1,128,2048]{2,1,0:T(8,128)(2,1)} %q_ref.1, bf16[1,128,2048]{2,1,0:T(8,128)(2,1)} %k_ref.1, bf16[1,128,2048]{2,1,0:T(8,128)(2,1)} %v_ref.1), custom_call_target="tpu_custom_call" | custom-call | flops 3449999872 | tf_op jit(solution)/shard_map/pallas_call | solution.py:41
  10.0 3.7 %all-to-all-start = ((bf16[4,3,512,128]{3,2,1,0:T(8,128)(2,1)}), bf16[4,3,512,128]{3,2,1,0:T(8,128)(2,1)S(1)}, u32[]{:S(2)}, u32[]{:S(2)}) async-start(bf16[4,3,512,128]{3,2,1,0:T(8,128)(2,1)} %shard_map.96), calls=%async_computation | async-start | bytes 3145728 | tf_op jit(solution)/shard_map/all_to_all | solution.py:390
  13.7 0.6 pad_add_fusion.pos_ref
  14.2 14.8 %collective-permute-done.1.refs_2_ = bf16[128,2048]{1,0:T(8,128)(2,1)} collective-permute-done((bf16[128,2048]{1,0:T(8,128)(2,1)}, bf16[128,2048]{1,0:T(8,128)(2,1)}, u32[]{:S(2)}, u32[]{:S(2)}) %collective-permute-start.1) | collective-permute-done | bytes 524320 | tf_op jit(solution)/shard_map/ppermute | solution.py:382
  29.1 1.3 collective-permute-start.3
  30.4 0.8 copy-done.11
  31.2 8.3 %shard_map.94 = (f32[384,512]{1,0:T(8,128)}, bf16[4,384,512]{2,1,0:T(8,128)(2,1)}) custom-call(s32[3]{0:T(128)} %pad_add_fusion.pos_ref, bf16[128,2048]{1,0:T(8,128)(2,1)} %bitcast.8, bf16[128,2048]{1,0:T(8,128)(2,1)} %copy-done.11, bf16[128,2048]{1,0:T(8,128)(2,1)} %collective-permute-done.1.refs_2_, bf16[2048,2048]{1,0:T(8,128)(2,1)} %refs_1_.1), custom_call_target="tpu_custom_call" | custom-call | flops 9200000000 | tf_op jit(solution)/shard_map/pallas_call | solution.py:224
  39.6 3.9 %collective-permute-done.3 = bf16[128,2048]{1,0:T(8,128)(2,1)S(1)} collective-permute-done((bf16[128,2048]{1,0:T(8,128)(2,1)}, bf16[128,2048]{1,0:T(8,128)(2,1)S(1)}, u32[]{:S(2)}, u32[]{:S(2)}) %collective-permute-start.3) | collective-permute-done | bytes 524320 | tf_op jit(solution)/shard_map/ppermute | solution.py:384
  43.5 0.9 broadcast_select_fusion.1.refs_0_.refs_3_
  44.3 2.4 %collective-permute-start.5 = (bf16[128,2048]{1,0:T(8,128)(2,1)}, bf16[128,2048]{1,0:T(8,128)(2,1)}, u32[]{:S(2)}, u32[]{:S(2)}) collective-permute-start(bf16[128,2048]{1,0:T(8,128)(2,1)} %bitcast.4.refs_0_), channel_id=1, source_target_pairs={{0,4},{4,0},{2,6},{6,2},{1,5},{5,1},{3,7},{7,3},{8,12},{12,8},{10,... | collective-permute-start | bytes 1572872 | tf_op jit(solution)/shard_map/ppermute | solution.py:382
  46.7 2.4 %collective-permute-start.4 = (bf16[128,2048]{1,0:T(8,128)(2,1)}, bf16[128,2048]{1,0:T(8,128)(2,1)}, u32[]{:S(2)}, u32[]{:S(2)}) collective-permute-start(bf16[128,2048]{1,0:T(8,128)(2,1)} %bitcast.4.refs_0_), channel_id=1, source_target_pairs={{0,2},{2,0},{4,6},{6,4},{1,3},{3,1},{5,7},{7,5},{8,10},{10,8},{12,... | collective-permute-start | bytes 1572872 | tf_op jit(solution)/shard_map/ppermute | solution.py:381
  49.1 3.7 %all-to-all-start.1 = ((bf16[4,384,512]{2,1,0:T(8,128)(2,1)}), bf16[4,384,512]{2,1,0:T(8,128)(2,1)S(1)}, u32[]{:S(2)}, u32[]{:S(2)}) async-start(bf16[4,384,512]{2,1,0:T(8,128)(2,1)} %get-tuple-element.35), calls=%async_computation.1 | async-start | bytes 3145728 | tf_op jit(solution)/shard_map/all_to_all | solution.py:390
  52.8 5.9 %shard_map.95 = (f32[128,512]{1,0:T(8,128)}, bf16[4,128,512]{2,1,0:T(8,128)(2,1)}) custom-call(s32[3]{0:T(128)} %pad_add_fusion.pos_ref, bf16[128,2048]{1,0:T(8,128)(2,1)} %broadcast_select_fusion.1.refs_0_.refs_3_, bf16[2048,2048]{1,0:T(8,128)(2,1)} %refs_1_.1), custom_call_target="tpu_custom_call" | custom-call | flops 9200000000 | tf_op jit(solution)/shard_map/pallas_call | solution.py:224
  58.8 5.6 %shard_map.97.refs_8_ = bf16[512,512]{1,0:T(8,128)(2,1)} custom-call(s32[3]{0:T(128)} %pad_add_fusion.pos_ref, f32[128,128]{1,0:T(8,128)} %f_ref.3, bf16[4,3,512,128]{3,2,1,0:T(8,128)(2,1)} %copy-done), custom_call_target="tpu_custom_call" | custom-call | flops 6899999744 | tf_op jit(solution)/shard_map/pallas_call | solution.py:98
  64.4 2.0 %collective-permute-start.7 = (bf16[512,512]{1,0:T(8,128)(2,1)}, bf16[512,512]{1,0:T(8,128)(2,1)}, u32[]{:S(2)}, u32[]{:S(2)}) collective-permute-start(bf16[512,512]{1,0:T(8,128)(2,1)} %shard_map.97.refs_8_), channel_id=1, source_target_pairs={{0,16},{16,0},{8,24},{24,8},{1,17},{17,1},{9,25},{25,9},{2,18},{18... | collective-permute-start | bytes 1572872 | tf_op jit(solution)/shard_map/ppermute | solution.py:395
  66.4 1.5 collective-permute-start.6
  67.8 0.7 collective-permute-start.19
  68.5 1.0 collective-permute-done.5.refs_2_
  69.5 1.3 collective-permute-start.20
  70.8 2.7 %all-to-all-done.1.refs_1_ = bf16[4,384,512]{2,1,0:T(8,128)(2,1)S(1)} async-done(((bf16[4,384,512]{2,1,0:T(8,128)(2,1)}), bf16[4,384,512]{2,1,0:T(8,128)(2,1)S(1)}, u32[]{:S(2)}, u32[]{:S(2)}) %all-to-all-start.1) | async-done | bytes 1572896 | tf_op jit(solution)/shard_map/all_to_all | solution.py:390
  73.5 3.5 %all-to-all-start.2 = ((bf16[4,128,512]{2,1,0:T(8,128)(2,1)}), bf16[4,128,512]{2,1,0:T(8,128)(2,1)S(1)}, u32[]{:S(2)}, u32[]{:S(2)}) async-start(bf16[4,128,512]{2,1,0:T(8,128)(2,1)} %get-tuple-element.37), calls=%async_computation.2 | async-start | bytes 1048576 | tf_op jit(solution)/shard_map/all_to_all | solution.py:390
  77.0 7.6 %collective-permute-done.7.refs_10_ = bf16[512,512]{1,0:T(8,128)(2,1)} collective-permute-done((bf16[512,512]{1,0:T(8,128)(2,1)}, bf16[512,512]{1,0:T(8,128)(2,1)}, u32[]{:S(2)}, u32[]{:S(2)}) %collective-permute-start.7) | collective-permute-done | bytes 524320 | tf_op jit(solution)/shard_map/ppermute | solution.py:395
  84.6 1.0 slice.17
  85.6 0.1 collective-permute-start.9
  85.7 1.7 slice.16
  87.3 0.6 collective-permute-start.8
  88.0 1.1 broadcast_select_fusion.refs_3_
  89.1 0.1 collective-permute-start.24
  89.2 0.7 all-to-all-done.2.refs_3_
  89.9 0.8 copy-done.4
  90.7 11.7 %shard_map.98.refs_8_.refs_12_ = bf16[528,512]{1,0:T(8,128)(2,1)} custom-call(s32[3]{0:T(128)} %pad_add_fusion.pos_ref, f32[128,128]{1,0:T(8,128)} %f_ref.3, bf16[4,3,512,128]{3,2,1,0:T(8,128)(2,1)} %copy-done, f32[384,512]{1,0:T(8,128)} %get-tuple-element.29.refs_0_, bf16[4,384,512]{2,1,0:T(8,128)(2,1)} %copy-done.1, f32[128,512]{1,0:T(8,128)} %get-tuple-element.31.refs_2_, ...), custom_call_target="tpu_custom_call" | custom-call | flops 13799999488 | tf_op jit(solution)/shard_map/pallas_call | solution.py:187
  102.6 0.5 collective-permute-start.11
  103.1 0.1 collective-permute-start.17
  103.2 0.4 collective-permute-start.18
  103.6 2.0 %collective-permute-done.17.refs_16_ = bf16[256,512]{1,0:T(8,128)(2,1)} collective-permute-done((bf16[256,512]{1,0:T(8,128)(2,1)}, bf16[256,512]{1,0:T(8,128)(2,1)}, u32[]{:S(2)}, u32[]{:S(2)}) %collective-permute-start.17) | collective-permute-done | bytes 262176 | tf_op jit(solution)/shard_map/ppermute | solution.py:406
  105.6 2.0 %collective-permute-start.27 = (bf16[528,512]{1,0:T(8,128)(2,1)}, bf16[528,512]{1,0:T(8,128)(2,1)S(1)}, u32[]{:S(2)}, u32[]{:S(2)}) collective-permute-start(bf16[528,512]{1,0:T(8,128)(2,1)} %shard_map.98.refs_8_.refs_12_), channel_id=1, source_target_pairs={{0,16},{16,0},{8,24},{24,8},{1,17},{17,1},{9,25},{25,9},{2,18},{18... | collective-permute-start | bytes 1622024 | tf_op jit(solution)/shard_map/ppermute | solution.py:395
  107.5 0.9 collective-permute-start.25
  108.5 0.5 collective-permute-start.13
  109.0 0.1 collective-permute-start.14
  109.1 1.4 collective-permute-done.12.refs_6_
  110.6 0.1 collective-permute-start.15
  110.7 1.1 collective-permute-done.13.refs_7_
  111.8 0.1 collective-permute-start.16
  112.1 0.4 collective-permute-start.21
  112.4 7.9 %collective-permute-done.27.refs_12_.refs_14_ = bf16[528,512]{1,0:T(8,128)(2,1)S(1)} collective-permute-done((bf16[528,512]{1,0:T(8,128)(2,1)}, bf16[528,512]{1,0:T(8,128)(2,1)S(1)}, u32[]{:S(2)}, u32[]{:S(2)}) %collective-permute-start.27) | collective-permute-done | bytes 540704 | tf_op jit(solution)/shard_map/ppermute | solution.py:395
  120.3 1.5 collective-permute-done.25.refs_10_.refs_13_
  121.9 0.6 collective-permute-start.31
  122.5 1.1 collective-permute-start.28
  123.6 1.0 collective-permute-start.26
  124.8 0.7 copy-done.15
  125.5 0.8 copy-done.16
  126.3 15.9 %shard_map.99 = f32[2048,2048]{1,0:T(8,128)} custom-call(s32[3]{0:T(128)} %pad_add_fusion.pos_ref, bf16[128,2048]{1,0:T(8,128)(2,1)} %bitcast.9, bf16[128,2048]{1,0:T(8,128)(2,1)} %copy-done.11, bf16[128,2048]{1,0:T(8,128)(2,1)} %collective-permute-done.1.refs_2_, bf16[128,2048]{1,0:T(8,128)(2,1)} %broadcast_select_fusion.1.refs_0_.refs_3_, ...), custom_call_target="tpu_custom_call" | custom-call | flops 18400000000 | tf_op jit(solution)/shard_map/pallas_call | solution.py:286
  142.3 0.6 collective-permute-start.29
  142.9 0.1 collective-permute-start.30
  143.0 0.8 copy-done.7
  143.8 0.2 copy-done.8
  144.0 0.8 copy-done.9
  144.8 13.1 %shard_map.100.refs_20_ = f32[2048,2048]{1,0:T(8,128)} custom-call(s32[3]{0:T(128)} %pad_add_fusion.pos_ref, bf16[128,2048]{1,0:T(8,128)(2,1)} %bitcast.4.refs_0_, bf16[128,2048]{1,0:T(8,128)(2,1)} %collective-permute-done.4.refs_1_, bf16[128,2048]{1,0:T(8,128)(2,1)} %collective-permute-done.5.refs_2_, bf16[128,2048]{1,0:T(8,128)(2,1)} %copy-done.3, ...), custom_call_target="tpu_custom_call" | custom-call | flops 11500000256 | tf_op jit(solution)/shard_map/pallas_call | solution.py:362
  157.9 0.7 copy-done.24
  158.6 0.7 copy-done.23
  159.3 7.6 %shard_map.101 = (f32[2048,2048]{1,0:T(8,128)}, f32[128,128]{1,0:T(8,128)}) custom-call(s32[3]{0:T(128)} %pad_add_fusion.pos_ref, bf16[128,2048]{1,0:T(8,128)(2,1)} %bitcast.4.refs_0_, bf16[128,2048]{1,0:T(8,128)(2,1)} %collective-permute-done.4.refs_1_, bf16[128,2048]{1,0:T(8,128)(2,1)} %collective-permute-done.5.refs_2_, ...), custom_call_target="tpu_custom_call", output_to_operand_aliasing={{0}: (21, {})} | custom-call | flops 11500000256 | tf_op jit(solution)/shard_map/pallas_call | solution.py:362
  (75 shorter events, 0.5 us)
Async XLA Ops:
  0.6 28.5 %collective-permute-start.1 = (bf16[128,2048]{1,0:T(8,128)(2,1)}, bf16[128,2048]{1,0:T(8,128)(2,1)}, u32[]{:S(2)}, u32[]{:S(2)}) collective-permute-start(bf16[128,2048]{1,0:T(8,128)(2,1)} %bitcast.5), channel_id=1, source_target_pairs={{0,4},{4,0},{2,6},{6,2},{1,5},{5,1},{3,7},{7,3},{8,12},{12,8},{10,... | collective-permute-start | bytes 1572872 | tf_op jit(solution)/shard_map/ppermute | solution.py:382
  4.7 25.6 %collective-permute-start = (bf16[128,2048]{1,0:T(8,128)(2,1)}, bf16[128,2048]{1,0:T(8,128)(2,1)S(1)}, u32[]{:S(2)}, u32[]{:S(2)}) collective-permute-start(bf16[128,2048]{1,0:T(8,128)(2,1)} %bitcast.6), channel_id=1, source_target_pairs={{0,2},{2,0},{4,6},{6,4},{1,3},{3,1},{5,7},{7,5},{8,10},{10,8},{12,... | collective-permute-start | bytes 1572872 | tf_op jit(solution)/shard_map/ppermute | solution.py:381
  6.3 33.2 %collective-permute-start.2 = (bf16[128,2048]{1,0:T(8,128)(2,1)}, bf16[128,2048]{1,0:T(8,128)(2,1)S(1)}, u32[]{:S(2)}, u32[]{:S(2)}) collective-permute-start(bf16[128,2048]{1,0:T(8,128)(2,1)} %bitcast.7), channel_id=1, source_target_pairs={{2,4},{4,2},{3,5},{5,3},{10,12},{12,10},{11,13},{13,11},{18,20},{2... | collective-permute-start | bytes 1572872 | tf_op jit(solution)/shard_map/ppermute | solution.py:383
  10.0 39.2 %all-to-all-start = ((bf16[4,3,512,128]{3,2,1,0:T(8,128)(2,1)}), bf16[4,3,512,128]{3,2,1,0:T(8,128)(2,1)S(1)}, u32[]{:S(2)}, u32[]{:S(2)}) async-start(bf16[4,3,512,128]{3,2,1,0:T(8,128)(2,1)} %shard_map.96), calls=%async_computation | async-start | bytes 3145728 | tf_op jit(solution)/shard_map/all_to_all | solution.py:390
  29.1 14.4 %collective-permute-start.3 = (bf16[128,2048]{1,0:T(8,128)(2,1)}, bf16[128,2048]{1,0:T(8,128)(2,1)S(1)}, u32[]{:S(2)}, u32[]{:S(2)}) collective-permute-start(bf16[128,2048]{1,0:T(8,128)(2,1)} %collective-permute-done.1.refs_2_), channel_id=1, source_target_pairs={{4,6},{2,0},{5,7},{3,1},{12,14},{10,8},{13,15},{11,9},{20,22},{18,... | collective-permute-start | bytes 1572872 | tf_op jit(solution)/shard_map/ppermute | solution.py:384
  30.4 0.8 copy-start.11
  44.3 25.2 %collective-permute-start.5 = (bf16[128,2048]{1,0:T(8,128)(2,1)}, bf16[128,2048]{1,0:T(8,128)(2,1)}, u32[]{:S(2)}, u32[]{:S(2)}) collective-permute-start(bf16[128,2048]{1,0:T(8,128)(2,1)} %bitcast.4.refs_0_), channel_id=1, source_target_pairs={{0,4},{4,0},{2,6},{6,2},{1,5},{5,1},{3,7},{7,3},{8,12},{12,8},{10,... | collective-permute-start | bytes 1572872 | tf_op jit(solution)/shard_map/ppermute | solution.py:382
  46.7 24.1 %collective-permute-start.4 = (bf16[128,2048]{1,0:T(8,128)(2,1)}, bf16[128,2048]{1,0:T(8,128)(2,1)}, u32[]{:S(2)}, u32[]{:S(2)}) collective-permute-start(bf16[128,2048]{1,0:T(8,128)(2,1)} %bitcast.4.refs_0_), channel_id=1, source_target_pairs={{0,2},{2,0},{4,6},{6,4},{1,3},{3,1},{5,7},{7,5},{8,10},{10,8},{12,... | collective-permute-start | bytes 1572872 | tf_op jit(solution)/shard_map/ppermute | solution.py:381
  49.1 9.7 %copy-start = (bf16[4,3,512,128]{3,2,1,0:T(8,128)(2,1)}, bf16[4,3,512,128]{3,2,1,0:T(8,128)(2,1)S(1)}, u32[]{:S(2)}) copy-start(bf16[4,3,512,128]{3,2,1,0:T(8,128)(2,1)S(1)} %all-to-all-done.parts_ref) | copy-start | bytes 4718596
  49.1 24.4 %all-to-all-start.1 = ((bf16[4,384,512]{2,1,0:T(8,128)(2,1)}), bf16[4,384,512]{2,1,0:T(8,128)(2,1)S(1)}, u32[]{:S(2)}, u32[]{:S(2)}) async-start(bf16[4,384,512]{2,1,0:T(8,128)(2,1)} %get-tuple-element.35), calls=%async_computation.1 | async-start | bytes 3145728 | tf_op jit(solution)/shard_map/all_to_all | solution.py:390
  64.4 20.3 %collective-permute-start.7 = (bf16[512,512]{1,0:T(8,128)(2,1)}, bf16[512,512]{1,0:T(8,128)(2,1)}, u32[]{:S(2)}, u32[]{:S(2)}) collective-permute-start(bf16[512,512]{1,0:T(8,128)(2,1)} %shard_map.97.refs_8_), channel_id=1, source_target_pairs={{0,16},{16,0},{8,24},{24,8},{1,17},{17,1},{9,25},{25,9},{2,18},{18... | collective-permute-start | bytes 1572872 | tf_op jit(solution)/shard_map/ppermute | solution.py:395
  66.4 19.3 %collective-permute-start.6 = (bf16[512,512]{1,0:T(8,128)(2,1)}, bf16[512,512]{1,0:T(8,128)(2,1)}, u32[]{:S(2)}, u32[]{:S(2)}) collective-permute-start(bf16[512,512]{1,0:T(8,128)(2,1)} %shard_map.97.refs_8_), channel_id=1, source_target_pairs={{0,8},{8,0},{16,24},{24,16},{1,9},{9,1},{17,25},{25,17},{2,10},{10... | collective-permute-start | bytes 1572872 | tf_op jit(solution)/shard_map/ppermute | solution.py:394
  67.8 20.2 %collective-permute-start.19 = (bf16[128,2048]{1,0:T(8,128)(2,1)}, bf16[128,2048]{1,0:T(8,128)(2,1)S(1)}, u32[]{:S(2)}, u32[]{:S(2)}) collective-permute-start(bf16[128,2048]{1,0:T(8,128)(2,1)} %bitcast.4.refs_0_), channel_id=1, source_target_pairs={{2,4},{4,2},{3,5},{5,3},{10,12},{12,10},{11,13},{13,11},{18,20},{2... | collective-permute-start | bytes 1572872 | tf_op jit(solution)/shard_map/ppermute | solution.py:383
  69.5 18.5 %collective-permute-start.20 = (bf16[128,2048]{1,0:T(8,128)(2,1)}, bf16[128,2048]{1,0:T(8,128)(2,1)}, u32[]{:S(2)}, u32[]{:S(2)}) collective-permute-start(bf16[128,2048]{1,0:T(8,128)(2,1)} %collective-permute-done.5.refs_2_), channel_id=1, source_target_pairs={{4,6},{2,0},{5,7},{3,1},{12,14},{10,8},{13,15},{11,9},{20,22},{18,... | collective-permute-start | bytes 1572872 | tf_op jit(solution)/shard_map/ppermute | solution.py:384
  73.5 16.4 %copy-start.1 = (bf16[4,384,512]{2,1,0:T(8,128)(2,1)}, bf16[4,384,512]{2,1,0:T(8,128)(2,1)S(1)}, u32[]{:S(2)}) copy-start(bf16[4,384,512]{2,1,0:T(8,128)(2,1)S(1)} %all-to-all-done.1.refs_1_) | copy-start | bytes 4718596
  73.5 16.4 %all-to-all-start.2 = ((bf16[4,128,512]{2,1,0:T(8,128)(2,1)}), bf16[4,128,512]{2,1,0:T(8,128)(2,1)S(1)}, u32[]{:S(2)}, u32[]{:S(2)}) async-start(bf16[4,128,512]{2,1,0:T(8,128)(2,1)} %get-tuple-element.37), calls=%async_computation.2 | async-start | bytes 1048576 | tf_op jit(solution)/shard_map/all_to_all | solution.py:390
  85.6 16.9 %collective-permute-start.9 = (bf16[256,512]{1,0:T(8,128)(2,1)S(1)}, bf16[256,512]{1,0:T(8,128)(2,1)}, u32[]{:S(2)}, u32[]{:S(2)}) collective-permute-start(bf16[256,512]{1,0:T(8,128)(2,1)S(1)} %slice.17), channel_id=1, source_target_pairs={{0,8},{8,0},{16,24},{24,16},{1,9},{9,1},{17,25},{25,17},{2,10},{10... | collective-permute-start | bytes 786440 | tf_op jit(solution)/shard_map/ppermute | solution.py:401
  87.3 15.1 %collective-permute-start.8 = (bf16[256,512]{1,0:T(8,128)(2,1)}, bf16[256,512]{1,0:T(8,128)(2,1)}, u32[]{:S(2)}, u32[]{:S(2)}) collective-permute-start(bf16[256,512]{1,0:T(8,128)(2,1)} %slice.16), channel_id=1, source_target_pairs={{0,16},{16,0},{8,24},{24,8},{1,17},{17,1},{9,25},{25,9},{2,18},{18... | collective-permute-start | bytes 786440 | tf_op jit(solution)/shard_map/ppermute | solution.py:400
  89.1 13.4 %copy-start.3 = (bf16[128,2048]{1,0:T(8,128)(2,1)}, bf16[128,2048]{1,0:T(8,128)(2,1)S(1)}, u32[]{:S(2)}) copy-start(bf16[128,2048]{1,0:T(8,128)(2,1)S(1)} %broadcast_select_fusion.refs_3_) | copy-start | bytes 1572868
  89.1 19.3 %copy-start.2 = (bf16[128,2048]{1,0:T(8,128)(2,1)S(1)}, bf16[128,2048]{1,0:T(8,128)(2,1)}, u32[]{:S(2)}) copy-start(bf16[128,2048]{1,0:T(8,128)(2,1)} %broadcast_select_fusion.1.refs_0_.refs_3_) | copy-start | bytes 1572868
  89.1 19.3 %collective-permute-start.24 = (bf16[128,2048]{1,0:T(8,128)(2,1)S(1)}, bf16[128,2048]{1,0:T(8,128)(2,1)}, u32[]{:S(2)}, u32[]{:S(2)}) collective-permute-start(bf16[128,2048]{1,0:T(8,128)(2,1)S(1)} %broadcast_select_fusion.refs_3_), channel_id=1, source_target_pairs={{0,1},{1,0},{2,3},{3,2},{4,5},{5,4},{6,7},{7,6},{8,9},{9,8},{10,11... | collective-permute-start | bytes 1572872 | tf_op jit(solution)/shard_map/ppermute | solution.py:406
  89.9 0.8 copy-start.4
  90.7 11.8 %copy-start.10 = (bf16[1,128,2048]{2,1,0:T(8,128)(2,1)S(1)}, bf16[1,128,2048]{2,1,0:T(8,128)(2,1)}, u32[]{:S(2)}) copy-start(bf16[1,128,2048]{2,1,0:T(8,128)(2,1)} %param.7) | copy-start | bytes 1572868
  102.5 5.9 %collective-permute-start.10 = (bf16[128,2048]{1,0:T(8,128)(2,1)S(1)}, bf16[128,2048]{1,0:T(8,128)(2,1)S(1)}, u32[]{:S(2)}, u32[]{:S(2)}) collective-permute-start(bf16[128,2048]{1,0:T(8,128)(2,1)S(1)} %bitcast.10), channel_id=1, source_target_pairs={{0,1},{1,0},{2,3},{3,2},{4,5},{5,4},{6,7},{7,6},{8,9},{9,8},{10,11... | collective-permute-start | bytes 1572872 | tf_op jit(solution)/shard_map/ppermute | solution.py:406
  102.6 6.4 %collective-permute-start.11 = (bf16[128,2048]{1,0:T(8,128)(2,1)}, bf16[128,2048]{1,0:T(8,128)(2,1)S(1)}, u32[]{:S(2)}, u32[]{:S(2)}) collective-permute-start(bf16[128,2048]{1,0:T(8,128)(2,1)} %copy-done.11), channel_id=1, source_target_pairs={{0,1},{1,0},{2,3},{3,2},{4,5},{5,4},{6,7},{7,6},{8,9},{9,8},{10,11... | collective-permute-start | bytes 1572872 | tf_op jit(solution)/shard_map/ppermute | solution.py:406
  103.1 2.5 %collective-permute-start.17 = (bf16[256,512]{1,0:T(8,128)(2,1)}, bf16[256,512]{1,0:T(8,128)(2,1)}, u32[]{:S(2)}, u32[]{:S(2)}) collective-permute-start(bf16[256,512]{1,0:T(8,128)(2,1)} %collective-permute-done.8.refs_11_), channel_id=1, source_target_pairs={{0,1},{1,0},{2,3},{3,2},{4,5},{5,4},{6,7},{7,6},{8,9},{9,8},{10,11... | collective-permute-start | bytes 786440 | tf_op jit(solution)/shard_map/ppermute | solution.py:406
  103.2 4.4 %collective-permute-start.18 = (bf16[256,512]{1,0:T(8,128)(2,1)}, bf16[256,512]{1,0:T(8,128)(2,1)}, u32[]{:S(2)}, u32[]{:S(2)}) collective-permute-start(bf16[256,512]{1,0:T(8,128)(2,1)} %collective-permute-done.9.refs_12_), channel_id=1, source_target_pairs={{0,1},{1,0},{2,3},{3,2},{4,5},{5,4},{6,7},{7,6},{8,9},{9,8},{10,11... | collective-permute-start | bytes 786440 | tf_op jit(solution)/shard_map/ppermute | solution.py:406
  105.6 14.7 %collective-permute-start.27 = (bf16[528,512]{1,0:T(8,128)(2,1)}, bf16[528,512]{1,0:T(8,128)(2,1)S(1)}, u32[]{:S(2)}, u32[]{:S(2)}) collective-permute-start(bf16[528,512]{1,0:T(8,128)(2,1)} %shard_map.98.refs_8_.refs_12_), channel_id=1, source_target_pairs={{0,16},{16,0},{8,24},{24,8},{1,17},{17,1},{9,25},{25,9},{2,18},{18... | collective-permute-start | bytes 1622024 | tf_op jit(solution)/shard_map/ppermute | solution.py:395
  107.5 14.2 %collective-permute-start.25 = (bf16[528,512]{1,0:T(8,128)(2,1)}, bf16[528,512]{1,0:T(8,128)(2,1)S(1)}, u32[]{:S(2)}, u32[]{:S(2)}) collective-permute-start(bf16[528,512]{1,0:T(8,128)(2,1)} %shard_map.98.refs_8_.refs_12_), channel_id=1, source_target_pairs={{0,8},{8,0},{16,24},{24,16},{1,9},{9,1},{17,25},{25,17},{2,10},{10... | collective-permute-start | bytes 1622024 | tf_op jit(solution)/shard_map/ppermute | solution.py:394
  108.4 2.1 %collective-permute-start.12 = (bf16[128,2048]{1,0:T(8,128)(2,1)}, bf16[128,2048]{1,0:T(8,128)(2,1)S(1)}, u32[]{:S(2)}, u32[]{:S(2)}) collective-permute-start(bf16[128,2048]{1,0:T(8,128)(2,1)} %collective-permute-done.1.refs_2_), channel_id=1, source_target_pairs={{0,1},{1,0},{2,3},{3,2},{4,5},{5,4},{6,7},{7,6},{8,9},{9,8},{10,11... | collective-permute-start | bytes 1572872 | tf_op jit(solution)/shard_map/ppermute | solution.py:406
  108.4 17.9 %copy-start.12 = (bf16[128,2048]{1,0:T(8,128)(2,1)}, bf16[128,2048]{1,0:T(8,128)(2,1)S(1)}, u32[]{:S(2)}) copy-start(bf16[128,2048]{1,0:T(8,128)(2,1)S(1)} %collective-permute-done.10.refs_4_) | copy-start | bytes 1572868
  108.5 3.4 %collective-permute-start.13 = (bf16[128,2048]{1,0:T(8,128)(2,1)S(1)}, bf16[128,2048]{1,0:T(8,128)(2,1)S(1)}, u32[]{:S(2)}, u32[]{:S(2)}) collective-permute-start(bf16[128,2048]{1,0:T(8,128)(2,1)S(1)} %copy-done.2), channel_id=1, source_target_pairs={{0,1},{1,0},{2,3},{3,2},{4,5},{5,4},{6,7},{7,6},{8,9},{9,8},{10,11... | collective-permute-start | bytes 1572872 | tf_op jit(solution)/shard_map/ppermute | solution.py:406
  109.0 15.7 %copy-start.13 = (bf16[128,2048]{1,0:T(8,128)(2,1)}, bf16[128,2048]{1,0:T(8,128)(2,1)S(1)}, u32[]{:S(2)}) copy-start(bf16[128,2048]{1,0:T(8,128)(2,1)S(1)} %collective-permute-done.11.refs_5_) | copy-start | bytes 1572868
  109.0 3.0 %collective-permute-start.14 = (bf16[512,512]{1,0:T(8,128)(2,1)}, bf16[512,512]{1,0:T(8,128)(2,1)S(1)}, u32[]{:S(2)}, u32[]{:S(2)}) collective-permute-start(bf16[512,512]{1,0:T(8,128)(2,1)} %shard_map.97.refs_8_), channel_id=1, source_target_pairs={{0,1},{1,0},{2,3},{3,2},{4,5},{5,4},{6,7},{7,6},{8,9},{9,8},{10,11... | collective-permute-start | bytes 1572872 | tf_op jit(solution)/shard_map/ppermute | solution.py:406
  110.6 1.4 copy-start.17
  110.6 11.4 %collective-permute-start.15 = (bf16[512,512]{1,0:T(8,128)(2,1)}, bf16[512,512]{1,0:T(8,128)(2,1)S(1)}, u32[]{:S(2)}, u32[]{:S(2)}) collective-permute-start(bf16[512,512]{1,0:T(8,128)(2,1)} %collective-permute-done.6.refs_9_), channel_id=1, source_target_pairs={{0,1},{1,0},{2,3},{3,2},{4,5},{5,4},{6,7},{7,6},{8,9},{9,8},{10,11... | collective-permute-start | bytes 1572872 | tf_op jit(solution)/shard_map/ppermute | solution.py:406
  111.8 9.9 %copy-start.18 = (bf16[128,2048]{1,0:T(8,128)(2,1)}, bf16[128,2048]{1,0:T(8,128)(2,1)S(1)}, u32[]{:S(2)}) copy-start(bf16[128,2048]{1,0:T(8,128)(2,1)S(1)} %collective-permute-done.13.refs_7_) | copy-start | bytes 1572868
  111.8 10.7 %collective-permute-start.16 = (bf16[512,512]{1,0:T(8,128)(2,1)}, bf16[512,512]{1,0:T(8,128)(2,1)S(1)}, u32[]{:S(2)}, u32[]{:S(2)}) collective-permute-start(bf16[512,512]{1,0:T(8,128)(2,1)} %collective-permute-done.7.refs_10_), channel_id=1, source_target_pairs={{0,1},{1,0},{2,3},{3,2},{4,5},{5,4},{6,7},{7,6},{8,9},{9,8},{10,11... | collective-permute-start | bytes 1572872 | tf_op jit(solution)/shard_map/ppermute | solution.py:406
  112.1 9.7 %copy-start.19 = (bf16[512,512]{1,0:T(8,128)(2,1)}, bf16[512,512]{1,0:T(8,128)(2,1)S(1)}, u32[]{:S(2)}) copy-start(bf16[512,512]{1,0:T(8,128)(2,1)S(1)} %collective-permute-done.14.refs_13_) | copy-start | bytes 1572868
  112.1 11.6 %collective-permute-start.21 = (bf16[128,2048]{1,0:T(8,128)(2,1)}, bf16[128,2048]{1,0:T(8,128)(2,1)S(1)}, u32[]{:S(2)}, u32[]{:S(2)}) collective-permute-start(bf16[128,2048]{1,0:T(8,128)(2,1)} %bitcast.4.refs_0_), channel_id=1, source_target_pairs={{0,1},{1,0},{2,3},{3,2},{4,5},{5,4},{6,7},{7,6},{8,9},{9,8},{10,11... | collective-permute-start | bytes 1572872 | tf_op jit(solution)/shard_map/ppermute | solution.py:406
  120.3 22.0 %copy-start.5 = (bf16[528,512]{1,0:T(8,128)(2,1)}, bf16[528,512]{1,0:T(8,128)(2,1)S(1)}, u32[]{:S(2)}) copy-start(bf16[528,512]{1,0:T(8,128)(2,1)S(1)} %collective-permute-done.27.refs_12_.refs_14_) | copy-start | bytes 1622020
  120.3 4.3 %collective-permute-start.22 = (bf16[128,2048]{1,0:T(8,128)(2,1)}, bf16[128,2048]{1,0:T(8,128)(2,1)S(1)}, u32[]{:S(2)}, u32[]{:S(2)}) collective-permute-start(bf16[128,2048]{1,0:T(8,128)(2,1)} %collective-permute-done.4.refs_1_), channel_id=1, source_target_pairs={{0,1},{1,0},{2,3},{3,2},{4,5},{5,4},{6,7},{7,6},{8,9},{9,8},{10,11... | collective-permute-start | bytes 1572872 | tf_op jit(solution)/shard_map/ppermute | solution.py:406
  121.8 20.5 %copy-start.6 = (bf16[528,512]{1,0:T(8,128)(2,1)}, bf16[528,512]{1,0:T(8,128)(2,1)S(1)}, u32[]{:S(2)}) copy-start(bf16[528,512]{1,0:T(8,128)(2,1)S(1)} %collective-permute-done.25.refs_10_.refs_13_) | copy-start | bytes 1622020
  121.8 3.0 %collective-permute-start.23 = (bf16[128,2048]{1,0:T(8,128)(2,1)}, bf16[128,2048]{1,0:T(8,128)(2,1)S(1)}, u32[]{:S(2)}, u32[]{:S(2)}) collective-permute-start(bf16[128,2048]{1,0:T(8,128)(2,1)} %collective-permute-done.5.refs_2_), channel_id=1, source_target_pairs={{0,1},{1,0},{2,3},{3,2},{4,5},{5,4},{6,7},{7,6},{8,9},{9,8},{10,11... | collective-permute-start | bytes 1572872 | tf_op jit(solution)/shard_map/ppermute | solution.py:406
  121.9 2.8 %copy-start.20 = (bf16[512,512]{1,0:T(8,128)(2,1)}, bf16[512,512]{1,0:T(8,128)(2,1)S(1)}, u32[]{:S(2)}) copy-start(bf16[512,512]{1,0:T(8,128)(2,1)S(1)} %collective-permute-done.15.refs_14_) | copy-start | bytes 1572868
  121.9 21.0 %collective-permute-start.31 = (bf16[528,512]{1,0:T(8,128)(2,1)}, bf16[528,512]{1,0:T(8,128)(2,1)S(1)}, u32[]{:S(2)}, u32[]{:S(2)}) collective-permute-start(bf16[528,512]{1,0:T(8,128)(2,1)} %shard_map.98.refs_8_.refs_12_), channel_id=1, source_target_pairs={{0,1},{1,0},{2,3},{3,2},{4,5},{5,4},{6,7},{7,6},{8,9},{9,8},{10,11... | collective-permute-start | bytes 1622024 | tf_op jit(solution)/shard_map/ppermute | solution.py:406
  122.5 2.3 %copy-start.21 = (bf16[512,512]{1,0:T(8,128)(2,1)}, bf16[512,512]{1,0:T(8,128)(2,1)S(1)}, u32[]{:S(2)}) copy-start(bf16[512,512]{1,0:T(8,128)(2,1)S(1)} %collective-permute-done.16.refs_15_) | copy-start | bytes 1572868
  122.5 20.4 %collective-permute-start.28 = (bf16[272,512]{1,0:T(8,128)(2,1)S(1)}, bf16[272,512]{1,0:T(8,128)(2,1)S(1)}, u32[]{:S(2)}, u32[]{:S(2)}) collective-permute-start(bf16[272,512]{1,0:T(8,128)(2,1)S(1)} %slice.19), channel_id=1, source_target_pairs={{0,8},{8,0},{16,24},{24,16},{1,9},{9,1},{17,25},{25,17},{2,10},{10... | collective-permute-start | bytes 835592 | tf_op jit(solution)/shard_map/ppermute | solution.py:401
  123.6 1.0 copy-start.14
  123.6 18.7 %collective-permute-start.26 = (bf16[256,512]{1,0:T(8,128)(2,1)S(1)}, bf16[256,512]{1,0:T(8,128)(2,1)}, u32[]{:S(2)}, u32[]{:S(2)}) collective-permute-start(bf16[256,512]{1,0:T(8,128)(2,1)S(1)} %slice.18), channel_id=1, source_target_pairs={{0,16},{16,0},{8,24},{24,8},{1,17},{17,1},{9,25},{25,9},{2,18},{18... | collective-permute-start | bytes 786440 | tf_op jit(solution)/shard_map/ppermute | solution.py:400
  124.7 0.8 copy-start.15
  124.7 18.3 %collective-permute-start.33 = (bf16[528,512]{1,0:T(8,128)(2,1)S(1)}, bf16[528,512]{1,0:T(8,128)(2,1)S(1)}, u32[]{:S(2)}, u32[]{:S(2)}) collective-permute-start(bf16[528,512]{1,0:T(8,128)(2,1)S(1)} %collective-permute-done.27.refs_12_.refs_14_), channel_id=1, source_target_pairs={{0,1},{1,0},{2,3},{3,2},{4,5},{5,4},{6,7},{7,6},{8,9},{9,8},{10,11... | collective-permute-start | bytes 1622024 | tf_op jit(solution)/shard_map/ppermute | solution.py:406
  125.5 0.8 copy-start.16
  126.3 16.7 %collective-permute-start.32 = (bf16[528,512]{1,0:T(8,128)(2,1)S(1)}, bf16[528,512]{1,0:T(8,128)(2,1)S(1)}, u32[]{:S(2)}, u32[]{:S(2)}) collective-permute-start(bf16[528,512]{1,0:T(8,128)(2,1)S(1)} %collective-permute-done.25.refs_10_.refs_13_), channel_id=1, source_target_pairs={{0,1},{1,0},{2,3},{3,2},{4,5},{5,4},{6,7},{7,6},{8,9},{9,8},{10,11... | collective-permute-start | bytes 1622024 | tf_op jit(solution)/shard_map/ppermute | solution.py:406
  142.3 15.6 %collective-permute-start.29 = (bf16[256,512]{1,0:T(8,128)(2,1)}, bf16[256,512]{1,0:T(8,128)(2,1)S(1)}, u32[]{:S(2)}, u32[]{:S(2)}) collective-permute-start(bf16[256,512]{1,0:T(8,128)(2,1)} %collective-permute-done.26.refs_8_), channel_id=1, source_target_pairs={{0,1},{1,0},{2,3},{3,2},{4,5},{5,4},{6,7},{7,6},{8,9},{9,8},{10,11... | collective-permute-start | bytes 786440 | tf_op jit(solution)/shard_map/ppermute | solution.py:406
  142.9 15.0 %copy-start.22 = (bf16[272,512]{1,0:T(8,128)(2,1)}, bf16[272,512]{1,0:T(8,128)(2,1)S(1)}, u32[]{:S(2)}) copy-start(bf16[272,512]{1,0:T(8,128)(2,1)S(1)} %collective-permute-done.28.refs_9_.refs_15_) | copy-start | bytes 835588
  142.9 15.0 %collective-permute-start.30 = (bf16[272,512]{1,0:T(8,128)(2,1)S(1)}, bf16[272,512]{1,0:T(8,128)(2,1)S(1)}, u32[]{:S(2)}, u32[]{:S(2)}) collective-permute-start(bf16[272,512]{1,0:T(8,128)(2,1)S(1)} %collective-permute-done.28.refs_9_.refs_15_), channel_id=1, source_target_pairs={{0,1},{1,0},{2,3},{3,2},{4,5},{5,4},{6,7},{7,6},{8,9},{9,8},{10,11... | collective-permute-start | bytes 835592 | tf_op jit(solution)/shard_map/ppermute | solution.py:406
  143.0 0.8 copy-start.7
  143.0 1.0 copy-start.8
  144.0 0.8 copy-start.9
  157.9 0.7 copy-start.24
  158.6 0.7 copy-start.23

commit v3 on v2

--- a/solution.py
+++ b/solution.py
@@ -107,7 +107,7 @@
             pltpu.VMEM((width, toks), f32),
         ],
         compiler_params=params(),
-        cost_estimate=cost(6),
+        cost_estimate=cost(0),
     )(pos, filters, parts)
 
 
@@ -390,9 +390,11 @@
     return lax.all_to_all(x, "row", split_axis=0, concat_axis=0, tiled=True)
 
 
-def row_gather(x, half):
+def row_gather(x, half, then=None):
     beside = lax.ppermute(x, "row", near)
     above = lax.ppermute(x, "row", far)
+    if then is not None:
+        beside, above, _ = lax.optimization_barrier((beside, above, then))
     return [
         x,
         beside,
@@ -439,19 +441,20 @@
     pos, *late = lax.optimization_barrier((pos, mine, *grads, *gated_all, *inputs[:3]))
     mine, grads, gated_all, inputs = late[0], late[1:5], late[5:10], late[10:] + inputs[3:]
     half = width // 2
-    values = row_gather(mine, half)
-    _, beside, above, *corner = values
-    others = other_core(values)
     inputs = inputs + other_core(inputs)
+    other = other_core([mine])[0]
     gated_all = gated_all + other_core(gated_all)
     grads_all = grads + other_core(grads)
     cuts = [(0, 0, seq), (1, 0, seq), (2, 0, seq), (3, 0, seq // 2), (3, seq // 2, seq // 2)]
     layout = [(block, owner, first, count) for owner in (0, 1) for block, first, count in cuts]
-
     out_grad = out_gradient(pos, grads_all, gated_all, layout)
+    values = row_gather(mine, half, out_grad)
+    _, beside, above, *corner = values
+    others = [other, *other_core(values[1:3])]
     three = [(block, owner, 0, width) for block in range(3) for owner in (0, 1)]
-    pieces = [piece for pair in zip(values[:3], others[:3], strict=True) for piece in pair]
+    pieces = [piece for pair in zip(values[:3], others, strict=True) for piece in pair]
     value_grad = value_part(after(pos, out_grad), inputs, pieces, three, (0, 1, 2), width)[0]
+    others = [*others, *other_core([after(piece, value_grad) for piece in corner])]
     halves = [(0, 0, 0, half), (0, 0, half, half), (0, 1, 0, half), (0, 1, half, half)]
     value_grad, taps = value_part(
         pos,

time: 168 us -> 155 us (0.923)
  waiting for transfers between devices: 44.8 us -> 29.9 us
  starting transfers between devices: 38.3 us -> 40.4 us
    ppermute x2, waiting for transfers between devices: 15.5 us -> 1.91 us  [row_gather(): above = lax.ppermute(x, 'row', far)]
    ppermute x2, waiting for transfers between devices: 3.9 us -> 0.01 us  [line_slots(): passed = lax.ppermute(second, 'col', [(2, 3), (1, 0)])]
    ppermute x18, waiting for transfers between devices: 4.68 us -> 7.21 us  [other_core(): return [lax.ppermute(x, 'dp', swap) for x in xs]]
    ppermute x2, starting transfers between devices: 3.95 us -> 1.9 us  [line_slots(): first = lax.ppermute(x, 'col', near)]
    ppermute x2, starting transfers between devices: 6.51 us -> 8.49 us  [line_slots(): second = lax.ppermute(x, 'col', far)]
    ppermute x2, starting transfers between devices: 3.98 us -> 2.03 us  [row_gather(): above = lax.ppermute(x, 'row', far)]
    ppermute x2, waiting for transfers between devices: 0.01 us -> 1.94 us  [line_slots(): first = lax.ppermute(x, 'col', near)]
    ppermute x2, starting transfers between devices: 2.35 us -> 4.07 us  [row_gather(): beside = lax.ppermute(x, 'row', near)]
  transfers between devices with their start and end apart: 37 -> 37, of which waited for: 12 -> 10; matrix products, arithmetic and copies ran while one was open for 3% -> 4% of each run, Pallas kernels for 38% -> 41%
where the time goes in v3:
time: 155 us
  Pallas kernels  71.2 us (46%)
  starting transfers between devices  40.4 us (26%)
  waiting for transfers between devices  29.9 us (19%)
  local copies, waits for them, and re-layouts  8.28 us (5%)
  other arithmetic  3.73 us (2%)
    pallas_call x2, Pallas kernels, value_part(): pl.pallas_call(functools.partial(value_kernel, n, width, which, layout, w...  20.7 us
    ppermute x2, waiting for transfers between devices, line_slots(): second = lax.ppermute(x, 'col', far)  16.7 us
    pallas_call x1, Pallas kernels, out_gradient(): pl.pallas_call(functools.partial(out_kernel, n, layout), out_shape=jax.Sh...  15.9 us
    pallas_call x2, Pallas kernels, project(): pl.pallas_call(functools.partial(project_kernel, len(slots)), out_shape=[...  14.3 us
    all_to_all x3, starting transfers between devices, swap_rows(): return lax.all_to_all(x, 'row', split_axis=0, concat_axis=0, tiled=True)  11.9 us
    pallas_call x1, Pallas kernels, backward(): pl.pallas_call(functools.partial(backward_kernel, size, counts), out_shap...  11.8 us
    ppermute x2, starting transfers between devices, line_slots(): second = lax.ppermute(x, 'col', far)  8.49 us
    ppermute x18, waiting for transfers between devices, other_core(): return [lax.ppermute(x, 'dp', swap) for x in xs]  7.21 us
  transfers between devices with their start and end apart: 37, of which 10 were waited for; matrix products, arithmetic and copies ran while one was open for 4% of the time, Pallas kernels for 41%

profile of v3, /device:TPU:0, one launch (start us, length us, event | category | flops | bytes accessed | tf_op | source)
XLA Modules:
  0.0 154.8 jit_solution(6493765128233278392)
XLA Ops:
  0.6 4.1 %collective-permute-start.1 = (bf16[128,2048]{1,0:T(8,128)(2,1)}, bf16[128,2048]{1,0:T(8,128)(2,1)}, u32[]{:S(2)}, u32[]{:S(2)}) collective-permute-start(bf16[128,2048]{1,0:T(8,128)(2,1)} %bitcast.3.refs_0_), channel_id=1, source_target_pairs={{0,4},{4,0},{2,6},{6,2},{1,5},{5,1},{3,7},{7,3},{8,12},{12,8},{10,... | collective-permute-start | bytes 1572872 | tf_op jit(solution)/shard_map/ppermute | solution.py:382
  4.7 1.6 %collective-permute-start = (bf16[128,2048]{1,0:T(8,128)(2,1)}, bf16[128,2048]{1,0:T(8,128)(2,1)S(1)}, u32[]{:S(2)}, u32[]{:S(2)}) collective-permute-start(bf16[128,2048]{1,0:T(8,128)(2,1)} %bitcast.3.refs_0_), channel_id=1, source_target_pairs={{0,2},{2,0},{4,6},{6,4},{1,3},{3,1},{5,7},{7,5},{8,10},{10,8},{12,... | collective-permute-start | bytes 1572872 | tf_op jit(solution)/shard_map/ppermute | solution.py:381
  6.3 3.0 %shard_map.96 = bf16[4,3,512,128]{3,2,1,0:T(8,128)(2,1)} custom-call(bf16[1,128,2048]{2,1,0:T(8,128)(2,1)} %q_ref.1, bf16[1,128,2048]{2,1,0:T(8,128)(2,1)} %k_ref.1, bf16[1,128,2048]{2,1,0:T(8,128)(2,1)} %v_ref.1), custom_call_target="tpu_custom_call" | custom-call | flops 3449999872 | tf_op jit(solution)/shard_map/pallas_call | solution.py:41
  9.3 3.7 %all-to-all-start = ((bf16[4,3,512,128]{3,2,1,0:T(8,128)(2,1)}), bf16[4,3,512,128]{3,2,1,0:T(8,128)(2,1)S(1)}, u32[]{:S(2)}, u32[]{:S(2)}) async-start(bf16[4,3,512,128]{3,2,1,0:T(8,128)(2,1)} %shard_map.96), calls=%async_computation | async-start | bytes 3145728 | tf_op jit(solution)/shard_map/all_to_all | solution.py:390
  13.0 1.4 collective-permute-start.2
  14.4 0.7 pad_add_fusion.pos_ref
  15.1 14.0 %collective-permute-done.1.refs_2_ = bf16[128,2048]{1,0:T(8,128)(2,1)} collective-permute-done((bf16[128,2048]{1,0:T(8,128)(2,1)}, bf16[128,2048]{1,0:T(8,128)(2,1)}, u32[]{:S(2)}, u32[]{:S(2)}) %collective-permute-start.1) | collective-permute-done | bytes 524320 | tf_op jit(solution)/shard_map/ppermute | solution.py:382
  29.1 1.3 collective-permute-start.3
  30.4 0.8 copy-done.10
  31.2 8.3 %shard_map.94 = (f32[384,512]{1,0:T(8,128)}, bf16[4,384,512]{2,1,0:T(8,128)(2,1)}) custom-call(s32[3]{0:T(128)} %pad_add_fusion.pos_ref, bf16[128,2048]{1,0:T(8,128)(2,1)} %bitcast.3.refs_0_, bf16[128,2048]{1,0:T(8,128)(2,1)} %copy-done.10, bf16[128,2048]{1,0:T(8,128)(2,1)} %collective-permute-done.1.refs_2_, bf16[2048,2048]{1,0:T(8,128)(2,1)} %refs_1_.1), custom_call_target="tpu_custom_call" | custom-call | flops 9200000000 | tf_op jit(solution)/shard_map/pallas_call | solution.py:224
  39.6 4.1 %all-to-all-start.1 = ((bf16[4,384,512]{2,1,0:T(8,128)(2,1)}), bf16[4,384,512]{2,1,0:T(8,128)(2,1)S(1)}, u32[]{:S(2)}, u32[]{:S(2)}) async-start(bf16[4,384,512]{2,1,0:T(8,128)(2,1)} %get-tuple-element.39), calls=%async_computation.1 | async-start | bytes 3145728 | tf_op jit(solution)/shard_map/all_to_all | solution.py:390
  43.6 1.9 %broadcast_select_fusion.1.refs_0_.refs_3_ = bf16[128,2048]{1,0:T(8,128)(2,1)} fusion(bf16[128,2048]{1,0:T(8,128)(2,1)} %collective-permute-done.2, bf16[128,2048]{1,0:T(8,128)(2,1)} %collective-permute-done.3, pred[]{:T(512)S(6)} %or.4), kind=kLoop, calls=%fused_computation.1 | loop fusion | flops 262144 | bytes 1572865 | tf_op jit(solution)/shard_map/jit(_where)/select_n | solution.py:385
  45.6 4.4 %collective-permute-start.5 = (bf16[128,2048]{1,0:T(8,128)(2,1)}, bf16[128,2048]{1,0:T(8,128)(2,1)}, u32[]{:S(2)}, u32[]{:S(2)}) collective-permute-start(bf16[128,2048]{1,0:T(8,128)(2,1)} %bitcast.5), channel_id=1, source_target_pairs={{0,4},{4,0},{2,6},{6,2},{1,5},{5,1},{3,7},{7,3},{8,12},{12,8},{10,... | collective-permute-start | bytes 1572872 | tf_op jit(solution)/shard_map/ppermute | solution.py:382
  49.9 0.3 collective-permute-start.4
  50.3 5.9 %shard_map.95 = (f32[128,512]{1,0:T(8,128)}, bf16[4,128,512]{2,1,0:T(8,128)(2,1)}) custom-call(s32[3]{0:T(128)} %pad_add_fusion.pos_ref, bf16[128,2048]{1,0:T(8,128)(2,1)} %broadcast_select_fusion.1.refs_0_.refs_3_, bf16[2048,2048]{1,0:T(8,128)(2,1)} %refs_1_.1), custom_call_target="tpu_custom_call" | custom-call | flops 9200000000 | tf_op jit(solution)/shard_map/pallas_call | solution.py:224
  56.2 5.6 %shard_map.97.refs_8_ = bf16[512,512]{1,0:T(8,128)(2,1)} custom-call(s32[3]{0:T(128)} %pad_add_fusion.pos_ref, f32[128,128]{1,0:T(8,128)} %f_ref.3, bf16[4,3,512,128]{3,2,1,0:T(8,128)(2,1)} %copy-done), custom_call_target="tpu_custom_call" | custom-call | tf_op jit(solution)/shard_map/pallas_call | solution.py:98
  61.8 1.7 %collective-permute-start.7 = (bf16[512,512]{1,0:T(8,128)(2,1)}, bf16[512,512]{1,0:T(8,128)(2,1)}, u32[]{:S(2)}, u32[]{:S(2)}) collective-permute-start(bf16[512,512]{1,0:T(8,128)(2,1)} %shard_map.97.refs_8_), channel_id=1, source_target_pairs={{0,16},{16,0},{8,24},{24,8},{1,17},{17,1},{9,25},{25,9},{2,18},{18... | collective-permute-start | bytes 1572872 | tf_op jit(solution)/shard_map/ppermute | solution.py:395
  63.5 1.5 collective-permute-start.6
  64.9 4.2 %all-to-all-start.2 = ((bf16[4,128,512]{2,1,0:T(8,128)(2,1)}), bf16[4,128,512]{2,1,0:T(8,128)(2,1)}, u32[]{:S(2)}, u32[]{:S(2)}) async-start(bf16[4,128,512]{2,1,0:T(8,128)(2,1)} %get-tuple-element.41), calls=%async_computation.2 | async-start | bytes 1048576 | tf_op jit(solution)/shard_map/all_to_all | solution.py:390
  69.1 0.7 collective-permute-start.19
  69.8 2.7 %collective-permute-done.5.refs_2_ = bf16[128,2048]{1,0:T(8,128)(2,1)} collective-permute-done((bf16[128,2048]{1,0:T(8,128)(2,1)}, bf16[128,2048]{1,0:T(8,128)(2,1)}, u32[]{:S(2)}, u32[]{:S(2)}) %collective-permute-start.5) | collective-permute-done | bytes 524320 | tf_op jit(solution)/shard_map/ppermute | solution.py:382
  72.5 1.9 %collective-permute-done.4.refs_1_ = bf16[128,2048]{1,0:T(8,128)(2,1)} collective-permute-done((bf16[128,2048]{1,0:T(8,128)(2,1)}, bf16[128,2048]{1,0:T(8,128)(2,1)}, u32[]{:S(2)}, u32[]{:S(2)}) %collective-permute-start.4) | collective-permute-done | bytes 524320 | tf_op jit(solution)/shard_map/ppermute | solution.py:381
  74.4 1.3 collective-permute-start.20
  75.7 1.9 %collective-permute-done.7.refs_10_ = bf16[512,512]{1,0:T(8,128)(2,1)} collective-permute-done((bf16[512,512]{1,0:T(8,128)(2,1)}, bf16[512,512]{1,0:T(8,128)(2,1)}, u32[]{:S(2)}, u32[]{:S(2)}) %collective-permute-start.7) | collective-permute-done | bytes 524320 | tf_op jit(solution)/shard_map/ppermute | solution.py:395
  77.6 1.0 slice.17
  78.6 0.3 collective-permute-start.9
  79.0 1.7 %slice.16 = bf16[256,512]{1,0:T(8,128)(2,1)} slice(bf16[512,512]{1,0:T(8,128)(2,1)} %collective-permute-done.6.refs_9_), slice={[0:256], [0:512]} | slice | bytes 524288 | tf_op jit(solution)/shard_map/slice | solution.py:402
  80.7 1.5 collective-permute-start.8
  82.1 2.1 %all-to-all-done.2.refs_3_ = bf16[4,128,512]{2,1,0:T(8,128)(2,1)} async-done(((bf16[4,128,512]{2,1,0:T(8,128)(2,1)}), bf16[4,128,512]{2,1,0:T(8,128)(2,1)}, u32[]{:S(2)}, u32[]{:S(2)}) %all-to-all-start.2) | async-done | bytes 524320 | tf_op jit(solution)/shard_map/all_to_all | solution.py:390
  84.3 11.8 %shard_map.98.refs_8_.refs_12_ = bf16[528,512]{1,0:T(8,128)(2,1)} custom-call(s32[3]{0:T(128)} %pad_add_fusion.pos_ref, f32[128,128]{1,0:T(8,128)} %f_ref.3, bf16[4,3,512,128]{3,2,1,0:T(8,128)(2,1)} %copy-done, f32[384,512]{1,0:T(8,128)} %get-tuple-element.33.refs_0_, bf16[4,384,512]{2,1,0:T(8,128)(2,1)} %copy-done.1, f32[128,512]{1,0:T(8,128)} %get-tuple-element.35.refs_2_, ...), custom_call_target="tpu_custom_call" | custom-call | flops 13799999488 | tf_op jit(solution)/shard_map/pallas_call | solution.py:187
  96.1 0.5 collective-permute-start.11
  96.6 0.1 collective-permute-start.17
  96.7 0.4 collective-permute-start.18
  97.1 0.1 collective-permute-start.12
  97.2 1.8 %collective-permute-done.17.refs_16_ = bf16[256,512]{1,0:T(8,128)(2,1)S(1)} collective-permute-done((bf16[256,512]{1,0:T(8,128)(2,1)}, bf16[256,512]{1,0:T(8,128)(2,1)S(1)}, u32[]{:S(2)}, u32[]{:S(2)}) %collective-permute-start.17) | collective-permute-done | bytes 262176 | tf_op jit(solution)/shard_map/ppermute | solution.py:408
  99.0 0.1 collective-permute-start.13
  99.1 1.0 collective-permute-done.18.refs_17_
  100.1 0.1 collective-permute-start.14
  100.3 0.4 collective-permute-start.15
  100.6 0.1 collective-permute-start.16
  100.8 1.2 broadcast_select_fusion.refs_3_
  102.0 0.4 collective-permute-start.29
  102.3 0.3 collective-permute-start.26
  102.7 2.6 %collective-permute-start.25 = (bf16[528,512]{1,0:T(8,128)(2,1)}, bf16[528,512]{1,0:T(8,128)(2,1)S(1)}, u32[]{:S(2)}, u32[]{:S(2)}) collective-permute-start(bf16[528,512]{1,0:T(8,128)(2,1)} %shard_map.98.refs_8_.refs_12_), channel_id=1, source_target_pairs={{0,8},{8,0},{16,24},{24,16},{1,9},{9,1},{17,25},{25,17},{2,10},{10... | collective-permute-start | bytes 1622024 | tf_op jit(solution)/shard_map/ppermute | solution.py:394
  105.4 0.7 copy-done.19
  106.1 0.8 copy-done.20
  106.9 15.9 %shard_map.99 = f32[2048,2048]{1,0:T(8,128)} custom-call(s32[3]{0:T(128)} %pad_add_fusion.pos_ref, bf16[128,2048]{1,0:T(8,128)(2,1)} %bitcast.3.refs_0_, bf16[128,2048]{1,0:T(8,128)(2,1)} %copy-done.10, bf16[128,2048]{1,0:T(8,128)(2,1)} %collective-permute-done.1.refs_2_, bf16[128,2048]{1,0:T(8,128)(2,1)} %broadcast_select_fusion.1.refs_0_.refs_3_, ...), custom_call_target="tpu_custom_call" | custom-call | flops 18400000000 | tf_op jit(solution)/shard_map/pallas_call | solution.py:286
  122.9 0.6 collective-permute-start.30
  123.6 0.4 collective-permute-start.22
  124.0 0.1 collective-permute-start.23
  124.1 2.6 %collective-permute-done.22.refs_5_ = bf16[128,2048]{1,0:T(8,128)(2,1)S(1)} collective-permute-done((bf16[128,2048]{1,0:T(8,128)(2,1)}, bf16[128,2048]{1,0:T(8,128)(2,1)S(1)}, u32[]{:S(2)}, u32[]{:S(2)}) %collective-permute-start.22) | collective-permute-done | bytes 524320 | tf_op jit(solution)/shard_map/ppermute | solution.py:408
  126.8 0.6 collective-permute-start.27
  127.3 0.2 collective-permute-done.23.refs_6_
  127.5 0.8 collective-permute-start.28
  128.4 0.7 copy-done.7
  129.1 0.2 copy-done.8
  129.4 0.8 copy-done.9
  130.2 13.1 %shard_map.100.refs_20_ = f32[2048,2048]{1,0:T(8,128)} custom-call(s32[3]{0:T(128)} %pad_add_fusion.pos_ref, bf16[128,2048]{1,0:T(8,128)(2,1)} %bitcast.9, bf16[128,2048]{1,0:T(8,128)(2,1)} %collective-permute-done.4.refs_1_, bf16[128,2048]{1,0:T(8,128)(2,1)} %collective-permute-done.5.refs_2_, bf16[128,2048]{1,0:T(8,128)(2,1)} %copy-done.4, ...), custom_call_target="tpu_custom_call" | custom-call | flops 11500000256 | tf_op jit(solution)/shard_map/pallas_call | solution.py:362
  143.3 0.3 collective-permute-start.33
  143.5 0.3 collective-permute-start.32
  143.8 1.6 %collective-permute-done.32.refs_10_ = bf16[256,512]{1,0:T(8,128)(2,1)S(1)} collective-permute-done((bf16[256,512]{1,0:T(8,128)(2,1)}, bf16[256,512]{1,0:T(8,128)(2,1)S(1)}, u32[]{:S(2)}, u32[]{:S(2)}) %collective-permute-start.32) | collective-permute-done | bytes 262176 | tf_op jit(solution)/shard_map/ppermute | solution.py:408
  145.5 0.7 copy-done.25
  146.2 0.7 copy-done.22
  146.9 7.7 %shard_map.101 = (f32[2048,2048]{1,0:T(8,128)}, f32[128,128]{1,0:T(8,128)}) custom-call(s32[3]{0:T(128)} %pad_add_fusion.pos_ref, bf16[128,2048]{1,0:T(8,128)(2,1)} %bitcast.10, bf16[128,2048]{1,0:T(8,128)(2,1)} %collective-permute-done.4.refs_1_, bf16[128,2048]{1,0:T(8,128)(2,1)} %collective-permute-done.5.refs_2_, ...), custom_call_target="tpu_custom_call", output_to_operand_aliasing={{0}: (21, {})} | custom-call | flops 11500000256 | tf_op jit(solution)/shard_map/pallas_call | solution.py:362
  (77 shorter events, 0.4 us)
Async XLA Ops:
  0.6 28.5 %collective-permute-start.1 = (bf16[128,2048]{1,0:T(8,128)(2,1)}, bf16[128,2048]{1,0:T(8,128)(2,1)}, u32[]{:S(2)}, u32[]{:S(2)}) collective-permute-start(bf16[128,2048]{1,0:T(8,128)(2,1)} %bitcast.3.refs_0_), channel_id=1, source_target_pairs={{0,4},{4,0},{2,6},{6,2},{1,5},{5,1},{3,7},{7,3},{8,12},{12,8},{10,... | collective-permute-start | bytes 1572872 | tf_op jit(solution)/shard_map/ppermute | solution.py:382
  4.7 25.6 %collective-permute-start = (bf16[128,2048]{1,0:T(8,128)(2,1)}, bf16[128,2048]{1,0:T(8,128)(2,1)S(1)}, u32[]{:S(2)}, u32[]{:S(2)}) collective-permute-start(bf16[128,2048]{1,0:T(8,128)(2,1)} %bitcast.3.refs_0_), channel_id=1, source_target_pairs={{0,2},{2,0},{4,6},{6,4},{1,3},{3,1},{5,7},{7,5},{8,10},{10,8},{12,... | collective-permute-start | bytes 1572872 | tf_op jit(solution)/shard_map/ppermute | solution.py:381
  9.3 30.3 %all-to-all-start = ((bf16[4,3,512,128]{3,2,1,0:T(8,128)(2,1)}), bf16[4,3,512,128]{3,2,1,0:T(8,128)(2,1)S(1)}, u32[]{:S(2)}, u32[]{:S(2)}) async-start(bf16[4,3,512,128]{3,2,1,0:T(8,128)(2,1)} %shard_map.96), calls=%async_computation | async-start | bytes 3145728 | tf_op jit(solution)/shard_map/all_to_all | solution.py:390
  13.0 30.6 %collective-permute-start.2 = (bf16[128,2048]{1,0:T(8,128)(2,1)}, bf16[128,2048]{1,0:T(8,128)(2,1)}, u32[]{:S(2)}, u32[]{:S(2)}) collective-permute-start(bf16[128,2048]{1,0:T(8,128)(2,1)} %bitcast.3.refs_0_), channel_id=1, source_target_pairs={{2,4},{4,2},{3,5},{5,3},{10,12},{12,10},{11,13},{13,11},{18,20},{2... | collective-permute-start | bytes 1572872 | tf_op jit(solution)/shard_map/ppermute | solution.py:383
  29.1 14.5 %collective-permute-start.3 = (bf16[128,2048]{1,0:T(8,128)(2,1)}, bf16[128,2048]{1,0:T(8,128)(2,1)}, u32[]{:S(2)}, u32[]{:S(2)}) collective-permute-start(bf16[128,2048]{1,0:T(8,128)(2,1)} %collective-permute-done.1.refs_2_), channel_id=1, source_target_pairs={{4,6},{2,0},{5,7},{3,1},{12,14},{10,8},{13,15},{11,9},{20,22},{18,... | collective-permute-start | bytes 1572872 | tf_op jit(solution)/shard_map/ppermute | solution.py:384
  30.4 0.8 copy-start.10
  39.5 16.7 %copy-start = (bf16[4,3,512,128]{3,2,1,0:T(8,128)(2,1)}, bf16[4,3,512,128]{3,2,1,0:T(8,128)(2,1)S(1)}, u32[]{:S(2)}) copy-start(bf16[4,3,512,128]{3,2,1,0:T(8,128)(2,1)S(1)} %all-to-all-done.parts_ref) | copy-start | bytes 4718596
  39.6 25.4 %all-to-all-start.1 = ((bf16[4,384,512]{2,1,0:T(8,128)(2,1)}), bf16[4,384,512]{2,1,0:T(8,128)(2,1)S(1)}, u32[]{:S(2)}, u32[]{:S(2)}) async-start(bf16[4,384,512]{2,1,0:T(8,128)(2,1)} %get-tuple-element.39), calls=%async_computation.1 | async-start | bytes 3145728 | tf_op jit(solution)/shard_map/all_to_all | solution.py:390
  45.6 27.0 %collective-permute-start.5 = (bf16[128,2048]{1,0:T(8,128)(2,1)}, bf16[128,2048]{1,0:T(8,128)(2,1)}, u32[]{:S(2)}, u32[]{:S(2)}) collective-permute-start(bf16[128,2048]{1,0:T(8,128)(2,1)} %bitcast.5), channel_id=1, source_target_pairs={{0,4},{4,0},{2,6},{6,2},{1,5},{5,1},{3,7},{7,3},{8,12},{12,8},{10,... | collective-permute-start | bytes 1572872 | tf_op jit(solution)/shard_map/ppermute | solution.py:382
  49.9 24.5 %collective-permute-start.4 = (bf16[128,2048]{1,0:T(8,128)(2,1)}, bf16[128,2048]{1,0:T(8,128)(2,1)}, u32[]{:S(2)}, u32[]{:S(2)}) collective-permute-start(bf16[128,2048]{1,0:T(8,128)(2,1)} %bitcast.6), channel_id=1, source_target_pairs={{0,2},{2,0},{4,6},{6,4},{1,3},{3,1},{5,7},{7,5},{8,10},{10,8},{12,... | collective-permute-start | bytes 1572872 | tf_op jit(solution)/shard_map/ppermute | solution.py:381
  61.8 15.9 %collective-permute-start.7 = (bf16[512,512]{1,0:T(8,128)(2,1)}, bf16[512,512]{1,0:T(8,128)(2,1)}, u32[]{:S(2)}, u32[]{:S(2)}) collective-permute-start(bf16[512,512]{1,0:T(8,128)(2,1)} %shard_map.97.refs_8_), channel_id=1, source_target_pairs={{0,16},{16,0},{8,24},{24,8},{1,17},{17,1},{9,25},{25,9},{2,18},{18... | collective-permute-start | bytes 1572872 | tf_op jit(solution)/shard_map/ppermute | solution.py:395
  63.5 15.5 %collective-permute-start.6 = (bf16[512,512]{1,0:T(8,128)(2,1)}, bf16[512,512]{1,0:T(8,128)(2,1)}, u32[]{:S(2)}, u32[]{:S(2)}) collective-permute-start(bf16[512,512]{1,0:T(8,128)(2,1)} %shard_map.97.refs_8_), channel_id=1, source_target_pairs={{0,8},{8,0},{16,24},{24,16},{1,9},{9,1},{17,25},{25,17},{2,10},{10... | collective-permute-start | bytes 1572872 | tf_op jit(solution)/shard_map/ppermute | solution.py:394
  64.9 19.3 %copy-start.1 = (bf16[4,384,512]{2,1,0:T(8,128)(2,1)}, bf16[4,384,512]{2,1,0:T(8,128)(2,1)S(1)}, u32[]{:S(2)}) copy-start(bf16[4,384,512]{2,1,0:T(8,128)(2,1)S(1)} %all-to-all-done.1.refs_1_) | copy-start | bytes 4718596
  64.9 19.3 %all-to-all-start.2 = ((bf16[4,128,512]{2,1,0:T(8,128)(2,1)}), bf16[4,128,512]{2,1,0:T(8,128)(2,1)}, u32[]{:S(2)}, u32[]{:S(2)}) async-start(bf16[4,128,512]{2,1,0:T(8,128)(2,1)} %get-tuple-element.41), calls=%async_computation.2 | async-start | bytes 1048576 | tf_op jit(solution)/shard_map/all_to_all | solution.py:390
  69.1 27.6 %collective-permute-start.19 = (bf16[128,2048]{1,0:T(8,128)(2,1)}, bf16[128,2048]{1,0:T(8,128)(2,1)S(1)}, u32[]{:S(2)}, u32[]{:S(2)}) collective-permute-start(bf16[128,2048]{1,0:T(8,128)(2,1)} %bitcast.7), channel_id=1, source_target_pairs={{2,4},{4,2},{3,5},{5,3},{10,12},{12,10},{11,13},{13,11},{18,20},{2... | collective-permute-start | bytes 1572872 | tf_op jit(solution)/shard_map/ppermute | solution.py:383
  74.4 22.7 %collective-permute-start.20 = (bf16[128,2048]{1,0:T(8,128)(2,1)}, bf16[128,2048]{1,0:T(8,128)(2,1)}, u32[]{:S(2)}, u32[]{:S(2)}) collective-permute-start(bf16[128,2048]{1,0:T(8,128)(2,1)} %collective-permute-done.5.refs_2_), channel_id=1, source_target_pairs={{4,6},{2,0},{5,7},{3,1},{12,14},{10,8},{13,15},{11,9},{20,22},{18,... | collective-permute-start | bytes 1572872 | tf_op jit(solution)/shard_map/ppermute | solution.py:384
  78.6 17.4 %collective-permute-start.9 = (bf16[256,512]{1,0:T(8,128)(2,1)S(1)}, bf16[256,512]{1,0:T(8,128)(2,1)}, u32[]{:S(2)}, u32[]{:S(2)}) collective-permute-start(bf16[256,512]{1,0:T(8,128)(2,1)S(1)} %slice.17), channel_id=1, source_target_pairs={{0,8},{8,0},{16,24},{24,16},{1,9},{9,1},{17,25},{25,17},{2,10},{10... | collective-permute-start | bytes 786440 | tf_op jit(solution)/shard_map/ppermute | solution.py:403
  80.7 18.3 %copy-start.3 = (bf16[128,2048]{1,0:T(8,128)(2,1)S(1)}, bf16[128,2048]{1,0:T(8,128)(2,1)}, u32[]{:S(2)}) copy-start(bf16[128,2048]{1,0:T(8,128)(2,1)} %broadcast_select_fusion.1.refs_0_.refs_3_) | copy-start | bytes 1572868
  80.7 19.5 %copy-start.2 = (bf16[512,512]{1,0:T(8,128)(2,1)S(1)}, bf16[512,512]{1,0:T(8,128)(2,1)}, u32[]{:S(2)}) copy-start(bf16[512,512]{1,0:T(8,128)(2,1)} %shard_map.97.refs_8_) | copy-start | bytes 1572868
  80.7 15.4 %collective-permute-start.8 = (bf16[256,512]{1,0:T(8,128)(2,1)}, bf16[256,512]{1,0:T(8,128)(2,1)}, u32[]{:S(2)}, u32[]{:S(2)}) collective-permute-start(bf16[256,512]{1,0:T(8,128)(2,1)} %slice.16), channel_id=1, source_target_pairs={{0,16},{16,0},{8,24},{24,8},{1,17},{17,1},{9,25},{25,9},{2,18},{18... | collective-permute-start | bytes 786440 | tf_op jit(solution)/shard_map/ppermute | solution.py:402
  84.3 11.9 %copy-start.11 = (bf16[128,2048]{1,0:T(8,128)(2,1)S(1)}, bf16[128,2048]{1,0:T(8,128)(2,1)}, u32[]{:S(2)}) copy-start(bf16[128,2048]{1,0:T(8,128)(2,1)} %copy-done.10) | copy-start | bytes 1572868
  96.0 4.2 %collective-permute-start.10 = (bf16[128,2048]{1,0:T(8,128)(2,1)}, bf16[128,2048]{1,0:T(8,128)(2,1)S(1)}, u32[]{:S(2)}, u32[]{:S(2)}) collective-permute-start(bf16[128,2048]{1,0:T(8,128)(2,1)} %bitcast.3.refs_0_), channel_id=1, source_target_pairs={{0,1},{1,0},{2,3},{3,2},{4,5},{5,4},{6,7},{7,6},{8,9},{9,8},{10,11... | collective-permute-start | bytes 1572872 | tf_op jit(solution)/shard_map/ppermute | solution.py:408
  96.1 4.5 %collective-permute-start.11 = (bf16[128,2048]{1,0:T(8,128)(2,1)S(1)}, bf16[128,2048]{1,0:T(8,128)(2,1)S(1)}, u32[]{:S(2)}, u32[]{:S(2)}) collective-permute-start(bf16[128,2048]{1,0:T(8,128)(2,1)S(1)} %copy-done.11), channel_id=1, source_target_pairs={{0,1},{1,0},{2,3},{3,2},{4,5},{5,4},{6,7},{7,6},{8,9},{9,8},{10,11... | collective-permute-start | bytes 1572872 | tf_op jit(solution)/shard_map/ppermute | solution.py:408
  96.6 2.4 %collective-permute-start.17 = (bf16[256,512]{1,0:T(8,128)(2,1)}, bf16[256,512]{1,0:T(8,128)(2,1)S(1)}, u32[]{:S(2)}, u32[]{:S(2)}) collective-permute-start(bf16[256,512]{1,0:T(8,128)(2,1)} %collective-permute-done.8.refs_11_), channel_id=1, source_target_pairs={{0,1},{1,0},{2,3},{3,2},{4,5},{5,4},{6,7},{7,6},{8,9},{9,8},{10,11... | collective-permute-start | bytes 786440 | tf_op jit(solution)/shard_map/ppermute | solution.py:408
  96.7 3.4 %collective-permute-start.18 = (bf16[256,512]{1,0:T(8,128)(2,1)}, bf16[256,512]{1,0:T(8,128)(2,1)S(1)}, u32[]{:S(2)}, u32[]{:S(2)}) collective-permute-start(bf16[256,512]{1,0:T(8,128)(2,1)} %collective-permute-done.9.refs_12_), channel_id=1, source_target_pairs={{0,1},{1,0},{2,3},{3,2},{4,5},{5,4},{6,7},{7,6},{8,9},{9,8},{10,11... | collective-permute-start | bytes 786440 | tf_op jit(solution)/shard_map/ppermute | solution.py:408
  97.1 4.8 %collective-permute-start.12 = (bf16[128,2048]{1,0:T(8,128)(2,1)}, bf16[128,2048]{1,0:T(8,128)(2,1)}, u32[]{:S(2)}, u32[]{:S(2)}) collective-permute-start(bf16[128,2048]{1,0:T(8,128)(2,1)} %collective-permute-done.1.refs_2_), channel_id=1, source_target_pairs={{0,1},{1,0},{2,3},{3,2},{4,5},{5,4},{6,7},{7,6},{8,9},{9,8},{10,11... | collective-permute-start | bytes 1572872 | tf_op jit(solution)/shard_map/ppermute | solution.py:408
  99.0 7.9 %copy-start.23 = (bf16[256,512]{1,0:T(8,128)(2,1)}, bf16[256,512]{1,0:T(8,128)(2,1)S(1)}, u32[]{:S(2)}) copy-start(bf16[256,512]{1,0:T(8,128)(2,1)S(1)} %collective-permute-done.17.refs_16_) | copy-start | bytes 786436
  99.0 3.4 %collective-permute-start.13 = (bf16[128,2048]{1,0:T(8,128)(2,1)S(1)}, bf16[128,2048]{1,0:T(8,128)(2,1)S(1)}, u32[]{:S(2)}, u32[]{:S(2)}) collective-permute-start(bf16[128,2048]{1,0:T(8,128)(2,1)S(1)} %copy-done.3), channel_id=1, source_target_pairs={{0,1},{1,0},{2,3},{3,2},{4,5},{5,4},{6,7},{7,6},{8,9},{9,8},{10,11... | collective-permute-start | bytes 1572872 | tf_op jit(solution)/shard_map/ppermute | solution.py:408
  100.1 1.8 %copy-start.24 = (bf16[256,512]{1,0:T(8,128)(2,1)}, bf16[256,512]{1,0:T(8,128)(2,1)S(1)}, u32[]{:S(2)}) copy-start(bf16[256,512]{1,0:T(8,128)(2,1)S(1)} %collective-permute-done.18.refs_17_) | copy-start | bytes 786436
  100.1 2.6 %collective-permute-start.14 = (bf16[512,512]{1,0:T(8,128)(2,1)S(1)}, bf16[512,512]{1,0:T(8,128)(2,1)S(1)}, u32[]{:S(2)}, u32[]{:S(2)}) collective-permute-start(bf16[512,512]{1,0:T(8,128)(2,1)S(1)} %copy-done.2), channel_id=1, source_target_pairs={{0,1},{1,0},{2,3},{3,2},{4,5},{5,4},{6,7},{7,6},{8,9},{9,8},{10,11... | collective-permute-start | bytes 1572872 | tf_op jit(solution)/shard_map/ppermute | solution.py:408
  100.2 6.7 %copy-start.13 = (bf16[128,2048]{1,0:T(8,128)(2,1)}, bf16[128,2048]{1,0:T(8,128)(2,1)S(1)}, u32[]{:S(2)}) copy-start(bf16[128,2048]{1,0:T(8,128)(2,1)S(1)} %collective-permute-done.10.refs_4_) | copy-start | bytes 1572868
  100.3 5.0 %collective-permute-start.15 = (bf16[512,512]{1,0:T(8,128)(2,1)}, bf16[512,512]{1,0:T(8,128)(2,1)S(1)}, u32[]{:S(2)}, u32[]{:S(2)}) collective-permute-start(bf16[512,512]{1,0:T(8,128)(2,1)} %collective-permute-done.6.refs_9_), channel_id=1, source_target_pairs={{0,1},{1,0},{2,3},{3,2},{4,5},{5,4},{6,7},{7,6},{8,9},{9,8},{10,11... | collective-permute-start | bytes 1572872 | tf_op jit(solution)/shard_map/ppermute | solution.py:408
  100.6 6.3 %copy-start.14 = (bf16[128,2048]{1,0:T(8,128)(2,1)}, bf16[128,2048]{1,0:T(8,128)(2,1)S(1)}, u32[]{:S(2)}) copy-start(bf16[128,2048]{1,0:T(8,128)(2,1)S(1)} %collective-permute-done.11.refs_5_) | copy-start | bytes 1572868
  100.6 5.5 %collective-permute-start.16 = (bf16[512,512]{1,0:T(8,128)(2,1)}, bf16[512,512]{1,0:T(8,128)(2,1)S(1)}, u32[]{:S(2)}, u32[]{:S(2)}) collective-permute-start(bf16[512,512]{1,0:T(8,128)(2,1)} %collective-permute-done.7.refs_10_), channel_id=1, source_target_pairs={{0,1},{1,0},{2,3},{3,2},{4,5},{5,4},{6,7},{7,6},{8,9},{9,8},{10,11... | collective-permute-start | bytes 1572872 | tf_op jit(solution)/shard_map/ppermute | solution.py:408
  101.9 20.9 %copy-start.4 = (bf16[128,2048]{1,0:T(8,128)(2,1)}, bf16[128,2048]{1,0:T(8,128)(2,1)S(1)}, u32[]{:S(2)}) copy-start(bf16[128,2048]{1,0:T(8,128)(2,1)S(1)} %broadcast_select_fusion.refs_3_) | copy-start | bytes 1572868
  102.0 26.4 %collective-permute-start.29 = (bf16[528,512]{1,0:T(8,128)(2,1)}, bf16[528,512]{1,0:T(8,128)(2,1)S(1)}, u32[]{:S(2)}, u32[]{:S(2)}) collective-permute-start(bf16[528,512]{1,0:T(8,128)(2,1)} %shard_map.98.refs_8_.refs_12_), channel_id=1, source_target_pairs={{0,1},{1,0},{2,3},{3,2},{4,5},{5,4},{6,7},{7,6},{8,9},{9,8},{10,11... | collective-permute-start | bytes 1622024 | tf_op jit(solution)/shard_map/ppermute | solution.py:408
  102.3 2.9 %copy-start.15 = (bf16[128,2048]{1,0:T(8,128)(2,1)}, bf16[128,2048]{1,0:T(8,128)(2,1)S(1)}, u32[]{:S(2)}) copy-start(bf16[128,2048]{1,0:T(8,128)(2,1)S(1)} %collective-permute-done.13.refs_7_) | copy-start | bytes 1572868
  102.3 20.5 %collective-permute-start.26 = (bf16[528,512]{1,0:T(8,128)(2,1)}, bf16[528,512]{1,0:T(8,128)(2,1)S(1)}, u32[]{:S(2)}, u32[]{:S(2)}) collective-permute-start(bf16[528,512]{1,0:T(8,128)(2,1)} %shard_map.98.refs_8_.refs_12_), channel_id=1, source_target_pairs={{0,16},{16,0},{8,24},{24,8},{1,17},{17,1},{9,25},{25,9},{2,18},{18... | collective-permute-start | bytes 1622024 | tf_op jit(solution)/shard_map/ppermute | solution.py:395
  102.7 2.6 %copy-start.17 = (bf16[512,512]{1,0:T(8,128)(2,1)}, bf16[512,512]{1,0:T(8,128)(2,1)S(1)}, u32[]{:S(2)}) copy-start(bf16[512,512]{1,0:T(8,128)(2,1)S(1)} %collective-permute-done.14.refs_13_) | copy-start | bytes 1572868
  102.7 20.2 %collective-permute-start.25 = (bf16[528,512]{1,0:T(8,128)(2,1)}, bf16[528,512]{1,0:T(8,128)(2,1)S(1)}, u32[]{:S(2)}, u32[]{:S(2)}) collective-permute-start(bf16[528,512]{1,0:T(8,128)(2,1)} %shard_map.98.refs_8_.refs_12_), channel_id=1, source_target_pairs={{0,8},{8,0},{16,24},{24,16},{1,9},{9,1},{17,25},{25,17},{2,10},{10... | collective-permute-start | bytes 1622024 | tf_op jit(solution)/shard_map/ppermute | solution.py:394
  105.3 0.8 copy-start.19
  105.3 18.3 %collective-permute-start.24 = (bf16[128,2048]{1,0:T(8,128)(2,1)S(1)}, bf16[128,2048]{1,0:T(8,128)(2,1)S(1)}, u32[]{:S(2)}, u32[]{:S(2)}) collective-permute-start(bf16[128,2048]{1,0:T(8,128)(2,1)S(1)} %broadcast_select_fusion.refs_3_), channel_id=1, source_target_pairs={{0,1},{1,0},{2,3},{3,2},{4,5},{5,4},{6,7},{7,6},{8,9},{9,8},{10,11... | collective-permute-start | bytes 1572872 | tf_op jit(solution)/shard_map/ppermute | solution.py:408
  106.1 0.8 copy-start.20
  106.9 17.1 %collective-permute-start.21 = (bf16[128,2048]{1,0:T(8,128)(2,1)}, bf16[128,2048]{1,0:T(8,128)(2,1)}, u32[]{:S(2)}, u32[]{:S(2)}) collective-permute-start(bf16[128,2048]{1,0:T(8,128)(2,1)} %bitcast.8), channel_id=1, source_target_pairs={{0,1},{1,0},{2,3},{3,2},{4,5},{5,4},{6,7},{7,6},{8,9},{9,8},{10,11... | collective-permute-start | bytes 1572872 | tf_op jit(solution)/shard_map/ppermute | solution.py:408
  122.9 5.5 %copy-start.5 = (bf16[528,512]{1,0:T(8,128)(2,1)}, bf16[528,512]{1,0:T(8,128)(2,1)S(1)}, u32[]{:S(2)}) copy-start(bf16[528,512]{1,0:T(8,128)(2,1)S(1)} %collective-permute-done.26.refs_12_.refs_14_) | copy-start | bytes 1622020
  122.9 5.5 %copy-start.6 = (bf16[528,512]{1,0:T(8,128)(2,1)}, bf16[528,512]{1,0:T(8,128)(2,1)S(1)}, u32[]{:S(2)}) copy-start(bf16[528,512]{1,0:T(8,128)(2,1)S(1)} %collective-permute-done.25.refs_10_.refs_13_) | copy-start | bytes 1622020
  122.9 5.4 %collective-permute-start.30 = (bf16[528,512]{1,0:T(8,128)(2,1)S(1)}, bf16[528,512]{1,0:T(8,128)(2,1)S(1)}, u32[]{:S(2)}, u32[]{:S(2)}) collective-permute-start(bf16[528,512]{1,0:T(8,128)(2,1)S(1)} %collective-permute-done.25.refs_10_.refs_13_), channel_id=1, source_target_pairs={{0,1},{1,0},{2,3},{3,2},{4,5},{5,4},{6,7},{7,6},{8,9},{9,8},{10,11... | collective-permute-start | bytes 1622024 | tf_op jit(solution)/shard_map/ppermute | solution.py:408
  123.5 4.9 %collective-permute-start.31 = (bf16[528,512]{1,0:T(8,128)(2,1)S(1)}, bf16[528,512]{1,0:T(8,128)(2,1)S(1)}, u32[]{:S(2)}, u32[]{:S(2)}) collective-permute-start(bf16[528,512]{1,0:T(8,128)(2,1)S(1)} %collective-permute-done.26.refs_12_.refs_14_), channel_id=1, source_target_pairs={{0,1},{1,0},{2,3},{3,2},{4,5},{5,4},{6,7},{7,6},{8,9},{9,8},{10,11... | collective-permute-start | bytes 1622024 | tf_op jit(solution)/shard_map/ppermute | solution.py:408
  123.6 4.8 %copy-start.12 = (bf16[128,2048]{1,0:T(8,128)(2,1)}, bf16[128,2048]{1,0:T(8,128)(2,1)S(1)}, u32[]{:S(2)}) copy-start(bf16[128,2048]{1,0:T(8,128)(2,1)S(1)} %collective-permute-done.24.refs_7_) | copy-start | bytes 1572868
  123.6 3.2 %collective-permute-start.22 = (bf16[128,2048]{1,0:T(8,128)(2,1)}, bf16[128,2048]{1,0:T(8,128)(2,1)S(1)}, u32[]{:S(2)}, u32[]{:S(2)}) collective-permute-start(bf16[128,2048]{1,0:T(8,128)(2,1)} %collective-permute-done.4.refs_1_), channel_id=1, source_target_pairs={{0,1},{1,0},{2,3},{3,2},{4,5},{5,4},{6,7},{7,6},{8,9},{9,8},{10,11... | collective-permute-start | bytes 1572872 | tf_op jit(solution)/shard_map/ppermute | solution.py:408
  124.0 3.5 %collective-permute-start.23 = (bf16[128,2048]{1,0:T(8,128)(2,1)}, bf16[128,2048]{1,0:T(8,128)(2,1)S(1)}, u32[]{:S(2)}, u32[]{:S(2)}) collective-permute-start(bf16[128,2048]{1,0:T(8,128)(2,1)} %collective-permute-done.5.refs_2_), channel_id=1, source_target_pairs={{0,1},{1,0},{2,3},{3,2},{4,5},{5,4},{6,7},{7,6},{8,9},{9,8},{10,11... | collective-permute-start | bytes 1572872 | tf_op jit(solution)/shard_map/ppermute | solution.py:408
  126.8 1.6 %copy-start.16 = (bf16[128,2048]{1,0:T(8,128)(2,1)}, bf16[128,2048]{1,0:T(8,128)(2,1)S(1)}, u32[]{:S(2)}) copy-start(bf16[128,2048]{1,0:T(8,128)(2,1)S(1)} %collective-permute-done.22.refs_5_) | copy-start | bytes 1572868
  126.8 16.8 %collective-permute-start.27 = (bf16[256,512]{1,0:T(8,128)(2,1)S(1)}, bf16[256,512]{1,0:T(8,128)(2,1)}, u32[]{:S(2)}, u32[]{:S(2)}) collective-permute-start(bf16[256,512]{1,0:T(8,128)(2,1)S(1)} %slice.14), channel_id=1, source_target_pairs={{0,16},{16,0},{8,24},{24,8},{1,17},{17,1},{9,25},{25,9},{2,18},{18... | collective-permute-start | bytes 786440 | tf_op jit(solution)/shard_map/ppermute | solution.py:402
  127.5 0.8 copy-start.18
  127.5 15.7 %collective-permute-start.28 = (bf16[272,512]{1,0:T(8,128)(2,1)S(1)}, bf16[272,512]{1,0:T(8,128)(2,1)S(1)}, u32[]{:S(2)}, u32[]{:S(2)}) collective-permute-start(bf16[272,512]{1,0:T(8,128)(2,1)S(1)} %slice.15), channel_id=1, source_target_pairs={{0,8},{8,0},{16,24},{24,16},{1,9},{9,1},{17,25},{25,17},{2,10},{10... | collective-permute-start | bytes 835592 | tf_op jit(solution)/shard_map/ppermute | solution.py:403
  128.3 0.8 copy-start.7
  128.4 1.0 copy-start.8
  129.4 0.8 copy-start.9
  143.2 2.2 %copy-start.21 = (bf16[272,512]{1,0:T(8,128)(2,1)}, bf16[272,512]{1,0:T(8,128)(2,1)S(1)}, u32[]{:S(2)}) copy-start(bf16[272,512]{1,0:T(8,128)(2,1)S(1)} %collective-permute-done.28.refs_9_.refs_15_) | copy-start | bytes 835588
  143.3 2.2 %collective-permute-start.33 = (bf16[272,512]{1,0:T(8,128)(2,1)S(1)}, bf16[272,512]{1,0:T(8,128)(2,1)S(1)}, u32[]{:S(2)}, u32[]{:S(2)}) collective-permute-start(bf16[272,512]{1,0:T(8,128)(2,1)S(1)} %collective-permute-done.28.refs_9_.refs_15_), channel_id=1, source_target_pairs={{0,1},{1,0},{2,3},{3,2},{4,5},{5,4},{6,7},{7,6},{8,9},{9,8},{10,11... | collective-permute-start | bytes 835592 | tf_op jit(solution)/shard_map/ppermute | solution.py:408
  143.5 1.9 %collective-permute-start.32 = (bf16[256,512]{1,0:T(8,128)(2,1)}, bf16[256,512]{1,0:T(8,128)(2,1)S(1)}, u32[]{:S(2)}, u32[]{:S(2)}) collective-permute-start(bf16[256,512]{1,0:T(8,128)(2,1)} %collective-permute-done.27.refs_8_), channel_id=1, source_target_pairs={{0,1},{1,0},{2,3},{3,2},{4,5},{5,4},{6,7},{7,6},{8,9},{9,8},{10,11... | collective-permute-start | bytes 786440 | tf_op jit(solution)/shard_map/ppermute | solution.py:408
  145.5 0.7 copy-start.25
  146.2 0.8 copy-start.22

commit v4 on v3

--- a/solution.py
+++ b/solution.py
@@ -17,7 +17,7 @@
 
 
 def params():
-    return pltpu.CompilerParams(vmem_limit_bytes=60 * MIB)
+    return pltpu.CompilerParams(vmem_limit_bytes=48 * MIB)
 
 
 def cost(us):

time: 155 us -> 147 us (0.948)
  Pallas kernels: 71.2 us -> 60.1 us
  local copies, waits for them, and re-layouts: 8.28 us -> 13.5 us
  waiting for transfers between devices: 29.9 us -> 25.8 us
  starting transfers between devices: 40.4 us -> 42.4 us
    unnamed x52 -> x46, local copies, waits for them, and re-layouts: 5.59 us -> 10.1 us
    pallas_call x2, Pallas kernels: 14.3 us -> 11.5 us  [project(): pl.pallas_call(functools.partial(project_kernel, len(slots)), out_shape=[...]
    pallas_call x2, Pallas kernels: 20.7 us -> 18.1 us  [value_part(): pl.pallas_call(functools.partial(value_kernel, n, width, which, layout, w...]
    pallas_call x1, Pallas kernels: 11.8 us -> 9.58 us  [backward(): pl.pallas_call(functools.partial(backward_kernel, size, counts), out_shap...]
    all_to_all x3, waiting for transfers between devices: 2.15 us -> 0.01 us  [swap_rows(): return lax.all_to_all(x, 'row', split_axis=0, concat_axis=0, tiled=True)]
    ppermute x2, waiting for transfers between devices: 1.91 us -> 0.17 us  [row_gather(): above = lax.ppermute(x, 'row', far)]
  transfers between devices with their start and end apart: 37 -> 37, of which waited for: 10 -> 10; matrix products, arithmetic and copies ran while one was open for 4% -> 4% of each run, Pallas kernels for 41% -> 37%
where the time goes in v4:
time: 147 us; the launch traced here: 145 us
  Pallas kernels  60.1 us (41%)
  starting transfers between devices  42.4 us (29%)
  waiting for transfers between devices  25.8 us (18%)
  local copies, waits for them, and re-layouts  13.5 us (9%)
  other arithmetic  2.27 us (2%)
    pallas_call x2, Pallas kernels, value_part(): pl.pallas_call(functools.partial(value_kernel, n, width, which, layout, w...  18.1 us
    ppermute x2, waiting for transfers between devices, line_slots(): second = lax.ppermute(x, 'col', far)  16.4 us
    pallas_call x1, Pallas kernels, out_gradient(): pl.pallas_call(functools.partial(out_kernel, n, layout), out_shape=jax.Sh...  14.7 us
    all_to_all x3, starting transfers between devices, swap_rows(): return lax.all_to_all(x, 'row', split_axis=0, concat_axis=0, tiled=True)  11.9 us
    pallas_call x2, Pallas kernels, project(): pl.pallas_call(functools.partial(project_kernel, len(slots)), out_shape=[...  11.5 us
    unnamed x46, local copies, waits for them, and re-layouts  10.1 us
    pallas_call x1, Pallas kernels, backward(): pl.pallas_call(functools.partial(backward_kernel, size, counts), out_shap...  9.58 us
    ppermute x2, starting transfers between devices, line_slots(): second = lax.ppermute(x, 'col', far)  8.49 us
  transfers between devices with their start and end apart: 37, of which 10 were waited for; matrix products, arithmetic and copies ran while one was open for 4% of the time, Pallas kernels for 37%

profile of v4, /device:TPU:0, one launch (start us, length us, event | category | flops | bytes accessed | tf_op | source)
XLA Modules:
  0.0 145.2 jit_solution(13083691447955690916)
XLA Ops:
  0.6 4.1 %collective-permute-start.1 = (bf16[128,2048]{1,0:T(8,128)(2,1)}, bf16[128,2048]{1,0:T(8,128)(2,1)}, u32[]{:S(2)}, u32[]{:S(2)}) collective-permute-start(bf16[128,2048]{1,0:T(8,128)(2,1)} %bitcast.3.refs_0_), channel_id=1, source_target_pairs={{0,4},{4,0},{2,6},{6,2},{1,5},{5,1},{3,7},{7,3},{8,12},{12,8},{10,... | collective-permute-start | bytes 1572872 | tf_op jit(solution)/shard_map/ppermute | solution.py:382
  4.7 1.6 %collective-permute-start = (bf16[128,2048]{1,0:T(8,128)(2,1)}, bf16[128,2048]{1,0:T(8,128)(2,1)S(1)}, u32[]{:S(2)}, u32[]{:S(2)}) collective-permute-start(bf16[128,2048]{1,0:T(8,128)(2,1)} %bitcast.3.refs_0_), channel_id=1, source_target_pairs={{0,2},{2,0},{4,6},{6,4},{1,3},{3,1},{5,7},{7,5},{8,10},{10,8},{12,... | collective-permute-start | bytes 1572872 | tf_op jit(solution)/shard_map/ppermute | solution.py:381
  6.3 1.0 copy-done.7
  7.4 1.0 copy-done.8
  8.4 1.0 copy-done.9
  9.4 1.6 %shard_map.96 = bf16[4,3,512,128]{3,2,1,0:T(8,128)(2,1)} custom-call(bf16[1,128,2048]{2,1,0:T(8,128)(2,1)S(1)} %copy-done.7, bf16[1,128,2048]{2,1,0:T(8,128)(2,1)S(1)} %copy-done.8, bf16[1,128,2048]{2,1,0:T(8,128)(2,1)S(1)} %copy-done.9), custom_call_target="tpu_custom_call" | custom-call | flops 3449999872 | tf_op jit(solution)/shard_map/pallas_call | solution.py:41
  11.0 3.7 %all-to-all-start = ((bf16[4,3,512,128]{3,2,1,0:T(8,128)(2,1)}), bf16[4,3,512,128]{3,2,1,0:T(8,128)(2,1)S(1)}, u32[]{:S(2)}, u32[]{:S(2)}) async-start(bf16[4,3,512,128]{3,2,1,0:T(8,128)(2,1)} %shard_map.96), calls=%async_computation | async-start | bytes 3145728 | tf_op jit(solution)/shard_map/all_to_all | solution.py:390
  14.8 1.5 %collective-permute-start.2 = (bf16[128,2048]{1,0:T(8,128)(2,1)}, bf16[128,2048]{1,0:T(8,128)(2,1)}, u32[]{:S(2)}, u32[]{:S(2)}) collective-permute-start(bf16[128,2048]{1,0:T(8,128)(2,1)} %bitcast.3.refs_0_), channel_id=1, source_target_pairs={{2,4},{4,2},{3,5},{5,3},{10,12},{12,10},{11,13},{13,11},{18,20},{2... | collective-permute-start | bytes 1572872 | tf_op jit(solution)/shard_map/ppermute | solution.py:383
  16.3 12.8 %collective-permute-done.1.refs_2_ = bf16[128,2048]{1,0:T(8,128)(2,1)} collective-permute-done((bf16[128,2048]{1,0:T(8,128)(2,1)}, bf16[128,2048]{1,0:T(8,128)(2,1)}, u32[]{:S(2)}, u32[]{:S(2)}) %collective-permute-start.1) | collective-permute-done | bytes 524320 | tf_op jit(solution)/shard_map/ppermute | solution.py:382
  29.1 1.3 collective-permute-start.3
  30.4 7.0 %shard_map.94 = (f32[384,512]{1,0:T(8,128)S(1)}, bf16[4,384,512]{2,1,0:T(8,128)(2,1)S(1)}) custom-call(s32[3]{0:T(128)S(1)} %pad_add_fusion.pos_ref, bf16[128,2048]{1,0:T(8,128)(2,1)} %bitcast.3.refs_0_, bf16[128,2048]{1,0:T(8,128)(2,1)S(1)} %collective-permute-done.refs_1_, bf16[128,2048]{1,0:T(8,128)(2,1)} %collective-permute-done.1.refs_2_, ...), custom_call_target="tpu_custom_call" | custom-call | flops 9200000000 | tf_op jit(solution)/shard_map/pallas_call | solution.py:224
  37.4 1.1 copy-done
  38.5 0.9 copy-done.13
  39.4 4.1 %all-to-all-start.1 = ((bf16[4,384,512]{2,1,0:T(8,128)(2,1)}), bf16[4,384,512]{2,1,0:T(8,128)(2,1)S(1)}, u32[]{:S(2)}, u32[]{:S(2)}) async-start(bf16[4,384,512]{2,1,0:T(8,128)(2,1)} %copy-done), calls=%async_computation.1 | async-start | bytes 3145728 | tf_op jit(solution)/shard_map/all_to_all | solution.py:390
  43.6 1.1 broadcast_select_fusion.1.refs_0_.refs_3_
  44.7 4.4 %collective-permute-start.5 = (bf16[128,2048]{1,0:T(8,128)(2,1)}, bf16[128,2048]{1,0:T(8,128)(2,1)}, u32[]{:S(2)}, u32[]{:S(2)}) collective-permute-start(bf16[128,2048]{1,0:T(8,128)(2,1)} %bitcast.5), channel_id=1, source_target_pairs={{0,4},{4,0},{2,6},{6,2},{1,5},{5,1},{3,7},{7,3},{8,12},{12,8},{10,... | collective-permute-start | bytes 1572872 | tf_op jit(solution)/shard_map/ppermute | solution.py:382
  49.1 0.5 collective-permute-start.4
  49.5 4.5 %shard_map.95 = (f32[128,512]{1,0:T(8,128)S(1)}, bf16[4,128,512]{2,1,0:T(8,128)(2,1)S(1)}) custom-call(s32[3]{0:T(128)S(1)} %pad_add_fusion.pos_ref, bf16[128,2048]{1,0:T(8,128)(2,1)S(1)} %broadcast_select_fusion.1.refs_0_.refs_3_, bf16[2048,2048]{1,0:T(8,128)(2,1)} %refs_1_.1), custom_call_target="tpu_custom_call" | custom-call | flops 9200000000 | tf_op jit(solution)/shard_map/pallas_call | solution.py:224
  54.1 0.8 copy-done.3
  54.9 4.6 %shard_map.97.refs_8_ = bf16[512,512]{1,0:T(8,128)(2,1)} custom-call(s32[3]{0:T(128)S(1)} %pad_add_fusion.pos_ref, f32[128,128]{1,0:T(8,128)S(1)} %copy-done.5, bf16[4,3,512,128]{3,2,1,0:T(8,128)(2,1)S(1)} %all-to-all-done.parts_ref), custom_call_target="tpu_custom_call" | custom-call | tf_op jit(solution)/shard_map/pallas_call | solution.py:98
  59.5 1.5 %collective-permute-start.7 = (bf16[512,512]{1,0:T(8,128)(2,1)}, bf16[512,512]{1,0:T(8,128)(2,1)}, u32[]{:S(2)}, u32[]{:S(2)}) collective-permute-start(bf16[512,512]{1,0:T(8,128)(2,1)} %shard_map.97.refs_8_), channel_id=1, source_target_pairs={{0,16},{16,0},{8,24},{24,8},{1,17},{17,1},{9,25},{25,9},{2,18},{18... | collective-permute-start | bytes 1572872 | tf_op jit(solution)/shard_map/ppermute | solution.py:395
  61.0 1.5 %collective-permute-start.6 = (bf16[512,512]{1,0:T(8,128)(2,1)}, bf16[512,512]{1,0:T(8,128)(2,1)}, u32[]{:S(2)}, u32[]{:S(2)}) collective-permute-start(bf16[512,512]{1,0:T(8,128)(2,1)} %shard_map.97.refs_8_), channel_id=1, source_target_pairs={{0,8},{8,0},{16,24},{24,16},{1,9},{9,1},{17,25},{25,17},{2,10},{10... | collective-permute-start | bytes 1572872 | tf_op jit(solution)/shard_map/ppermute | solution.py:394
  62.5 4.1 %all-to-all-start.2 = ((bf16[4,128,512]{2,1,0:T(8,128)(2,1)}), bf16[4,128,512]{2,1,0:T(8,128)(2,1)}, u32[]{:S(2)}, u32[]{:S(2)}) async-start(bf16[4,128,512]{2,1,0:T(8,128)(2,1)} %copy-done.3), calls=%async_computation.2 | async-start | bytes 1048576 | tf_op jit(solution)/shard_map/all_to_all | solution.py:390
  66.7 1.5 %collective-permute-start.19 = (bf16[128,2048]{1,0:T(8,128)(2,1)}, bf16[128,2048]{1,0:T(8,128)(2,1)}, u32[]{:S(2)}, u32[]{:S(2)}) collective-permute-start(bf16[128,2048]{1,0:T(8,128)(2,1)} %bitcast.7), channel_id=1, source_target_pairs={{2,4},{4,2},{3,5},{5,3},{10,12},{12,10},{11,13},{13,11},{18,20},{2... | collective-permute-start | bytes 1572872 | tf_op jit(solution)/shard_map/ppermute | solution.py:383
  68.2 3.6 %collective-permute-done.5.refs_2_ = bf16[128,2048]{1,0:T(8,128)(2,1)} collective-permute-done((bf16[128,2048]{1,0:T(8,128)(2,1)}, bf16[128,2048]{1,0:T(8,128)(2,1)}, u32[]{:S(2)}, u32[]{:S(2)}) %collective-permute-start.5) | collective-permute-done | bytes 524320 | tf_op jit(solution)/shard_map/ppermute | solution.py:382
  71.8 1.8 %collective-permute-done.4.refs_1_ = bf16[128,2048]{1,0:T(8,128)(2,1)} collective-permute-done((bf16[128,2048]{1,0:T(8,128)(2,1)}, bf16[128,2048]{1,0:T(8,128)(2,1)}, u32[]{:S(2)}, u32[]{:S(2)}) %collective-permute-start.4) | collective-permute-done | bytes 524320 | tf_op jit(solution)/shard_map/ppermute | solution.py:381
  73.6 1.5 %collective-permute-start.20 = (bf16[128,2048]{1,0:T(8,128)(2,1)}, bf16[128,2048]{1,0:T(8,128)(2,1)}, u32[]{:S(2)}, u32[]{:S(2)}) collective-permute-start(bf16[128,2048]{1,0:T(8,128)(2,1)} %collective-permute-done.5.refs_2_), channel_id=1, source_target_pairs={{4,6},{2,0},{5,7},{3,1},{12,14},{10,8},{13,15},{11,9},{20,22},{18,... | collective-permute-start | bytes 1572872 | tf_op jit(solution)/shard_map/ppermute | solution.py:384
  75.1 0.2 collective-permute-done.7.refs_10_
  75.2 1.7 %slice.17 = bf16[256,512]{1,0:T(8,128)(2,1)} slice(bf16[512,512]{1,0:T(8,128)(2,1)} %collective-permute-done.7.refs_10_), slice={[256:512], [0:512]} | slice | bytes 524288 | tf_op jit(solution)/shard_map/slice | solution.py:403
  76.9 1.5 %collective-permute-start.9 = (bf16[256,512]{1,0:T(8,128)(2,1)}, bf16[256,512]{1,0:T(8,128)(2,1)S(1)}, u32[]{:S(2)}, u32[]{:S(2)}) collective-permute-start(bf16[256,512]{1,0:T(8,128)(2,1)} %slice.17), channel_id=1, source_target_pairs={{0,8},{8,0},{16,24},{24,16},{1,9},{9,1},{17,25},{25,17},{2,10},{10... | collective-permute-start | bytes 786440 | tf_op jit(solution)/shard_map/ppermute | solution.py:403
  78.4 1.7 %slice.16 = bf16[256,512]{1,0:T(8,128)(2,1)} slice(bf16[512,512]{1,0:T(8,128)(2,1)} %collective-permute-done.6.refs_9_), slice={[0:256], [0:512]} | slice | bytes 524288 | tf_op jit(solution)/shard_map/slice | solution.py:402
  80.1 1.5 %collective-permute-start.8 = (bf16[256,512]{1,0:T(8,128)(2,1)}, bf16[256,512]{1,0:T(8,128)(2,1)}, u32[]{:S(2)}, u32[]{:S(2)}) collective-permute-start(bf16[256,512]{1,0:T(8,128)(2,1)} %slice.16), channel_id=1, source_target_pairs={{0,16},{16,0},{8,24},{24,8},{1,17},{17,1},{9,25},{25,9},{2,18},{18... | collective-permute-start | bytes 786440 | tf_op jit(solution)/shard_map/ppermute | solution.py:402
  81.6 1.1 copy-done.14
  82.7 0.9 copy-done.16
  83.7 9.6 %shard_map.98.refs_8_.refs_12_ = bf16[528,512]{1,0:T(8,128)(2,1)S(1)} custom-call(s32[3]{0:T(128)S(1)} %pad_add_fusion.pos_ref, f32[128,128]{1,0:T(8,128)S(1)} %copy-done.5, bf16[4,3,512,128]{3,2,1,0:T(8,128)(2,1)S(1)} %all-to-all-done.parts_ref, f32[384,512]{1,0:T(8,128)S(1)} %copy-done.14, bf16[4,384,512]{2,1,0:T(8,128)(2,1)S(1)} %all-to-all-done.1.refs_1_, ...), custom_call_target="tpu_custom_call" | custom-call | flops 13799999488 | tf_op jit(solution)/shard_map/pallas_call | solution.py:187
  93.4 0.5 collective-permute-start.11
  94.0 0.4 collective-permute-start.18
  94.5 1.8 %collective-permute-done.17.refs_16_ = bf16[256,512]{1,0:T(8,128)(2,1)S(1)} collective-permute-done((bf16[256,512]{1,0:T(8,128)(2,1)}, bf16[256,512]{1,0:T(8,128)(2,1)S(1)}, u32[]{:S(2)}, u32[]{:S(2)}) %collective-permute-start.17) | collective-permute-done | bytes 262176 | tf_op jit(solution)/shard_map/ppermute | solution.py:408
  96.2 0.1 collective-permute-start.13
  96.4 1.1 collective-permute-done.18.refs_17_
  97.6 0.4 collective-permute-start.15
  98.0 0.1 collective-permute-start.16
  98.2 1.1 broadcast_select_fusion.refs_3_
  99.3 0.4 collective-permute-start.29
  99.7 0.6 collective-permute-start.26
  100.3 1.8 %collective-permute-start.25 = (bf16[528,512]{1,0:T(8,128)(2,1)S(1)}, bf16[528,512]{1,0:T(8,128)(2,1)S(1)}, u32[]{:S(2)}, u32[]{:S(2)}) collective-permute-start(bf16[528,512]{1,0:T(8,128)(2,1)S(1)} %shard_map.98.refs_8_.refs_12_), channel_id=1, source_target_pairs={{0,8},{8,0},{16,24},{24,16},{1,9},{9,1},{17,25},{25,17},{2,10},{10... | collective-permute-start | bytes 1622024 | tf_op jit(solution)/shard_map/ppermute | solution.py:394
  102.1 0.5 collective-permute-start.21
  102.6 0.2 copy-done.21
  102.8 0.2 copy-done.22
  103.1 14.7 %shard_map.99 = f32[2048,2048]{1,0:T(8,128)} custom-call(s32[3]{0:T(128)S(1)} %pad_add_fusion.pos_ref, bf16[128,2048]{1,0:T(8,128)(2,1)} %bitcast.3.refs_0_, bf16[128,2048]{1,0:T(8,128)(2,1)S(1)} %copy-done.12, bf16[128,2048]{1,0:T(8,128)(2,1)} %collective-permute-done.1.refs_2_, bf16[128,2048]{1,0:T(8,128)(2,1)S(1)} %copy-done.2, ...), custom_call_target="tpu_custom_call" | custom-call | flops 18400000000 | tf_op jit(solution)/shard_map/pallas_call | solution.py:286
  117.8 0.4 collective-permute-start.30
  118.2 0.2 collective-permute-start.31
  118.4 0.3 collective-permute-start.22
  118.7 0.2 collective-permute-start.23
  119.0 2.6 %collective-permute-done.22.refs_5_ = bf16[128,2048]{1,0:T(8,128)(2,1)S(1)} collective-permute-done((bf16[128,2048]{1,0:T(8,128)(2,1)}, bf16[128,2048]{1,0:T(8,128)(2,1)S(1)}, u32[]{:S(2)}, u32[]{:S(2)}) %collective-permute-start.22) | collective-permute-done | bytes 524320 | tf_op jit(solution)/shard_map/ppermute | solution.py:408
  121.6 0.4 collective-permute-start.27
  121.9 0.4 collective-permute-done.23.refs_6_
  122.3 1.0 collective-permute-start.28
  123.3 0.8 copy-done.18
  124.2 0.8 copy-done.19
  125.0 11.8 %shard_map.100.refs_20_ = f32[2048,2048]{1,0:T(8,128)} custom-call(s32[3]{0:T(128)S(1)} %pad_add_fusion.pos_ref, bf16[128,2048]{1,0:T(8,128)(2,1)S(1)} %bitcast.9, bf16[128,2048]{1,0:T(8,128)(2,1)} %collective-permute-done.4.refs_1_, bf16[128,2048]{1,0:T(8,128)(2,1)} %collective-permute-done.5.refs_2_, bf16[128,2048]{1,0:T(8,128)(2,1)S(1)} %broadcast_select_fusion.refs_3_, ...), custom_call_target="tpu_custom_call" | custom-call | flops 11500000256 | tf_op jit(solution)/shard_map/pallas_call | solution.py:362
  136.8 0.5 collective-permute-start.32
  137.3 1.4 collective-permute-done.32.refs_10_
  138.8 6.3 %shard_map.101 = (f32[2048,2048]{1,0:T(8,128)}, f32[128,128]{1,0:T(8,128)}) custom-call(s32[3]{0:T(128)S(1)} %pad_add_fusion.pos_ref, bf16[128,2048]{1,0:T(8,128)(2,1)S(1)} %bitcast.10, bf16[128,2048]{1,0:T(8,128)(2,1)} %collective-permute-done.4.refs_1_, bf16[128,2048]{1,0:T(8,128)(2,1)} %collective-permute-done.5.refs_2_, ...), custom_call_target="tpu_custom_call", output_to_operand_aliasing={{0}: (21, {})} | custom-call | flops 11500000256 | tf_op jit(solution)/shard_map/pallas_call | solution.py:362
  (71 shorter events, 0.8 us)
Async XLA Ops:
  0.6 28.5 %collective-permute-start.1 = (bf16[128,2048]{1,0:T(8,128)(2,1)}, bf16[128,2048]{1,0:T(8,128)(2,1)}, u32[]{:S(2)}, u32[]{:S(2)}) collective-permute-start(bf16[128,2048]{1,0:T(8,128)(2,1)} %bitcast.3.refs_0_), channel_id=1, source_target_pairs={{0,4},{4,0},{2,6},{6,2},{1,5},{5,1},{3,7},{7,3},{8,12},{12,8},{10,... | collective-permute-start | bytes 1572872 | tf_op jit(solution)/shard_map/ppermute | solution.py:382
  4.7 25.6 %collective-permute-start = (bf16[128,2048]{1,0:T(8,128)(2,1)}, bf16[128,2048]{1,0:T(8,128)(2,1)S(1)}, u32[]{:S(2)}, u32[]{:S(2)}) collective-permute-start(bf16[128,2048]{1,0:T(8,128)(2,1)} %bitcast.3.refs_0_), channel_id=1, source_target_pairs={{0,2},{2,0},{4,6},{6,4},{1,3},{3,1},{5,7},{7,5},{8,10},{10,8},{12,... | collective-permute-start | bytes 1572872 | tf_op jit(solution)/shard_map/ppermute | solution.py:381
  6.3 1.0 copy-start.7
  7.4 1.0 copy-start.8
  8.4 1.0 copy-start.9
  11.0 28.4 %all-to-all-start = ((bf16[4,3,512,128]{3,2,1,0:T(8,128)(2,1)}), bf16[4,3,512,128]{3,2,1,0:T(8,128)(2,1)S(1)}, u32[]{:S(2)}, u32[]{:S(2)}) async-start(bf16[4,3,512,128]{3,2,1,0:T(8,128)(2,1)} %shard_map.96), calls=%async_computation | async-start | bytes 3145728 | tf_op jit(solution)/shard_map/all_to_all | solution.py:390
  14.8 28.7 %collective-permute-start.2 = (bf16[128,2048]{1,0:T(8,128)(2,1)}, bf16[128,2048]{1,0:T(8,128)(2,1)}, u32[]{:S(2)}, u32[]{:S(2)}) collective-permute-start(bf16[128,2048]{1,0:T(8,128)(2,1)} %bitcast.3.refs_0_), channel_id=1, source_target_pairs={{2,4},{4,2},{3,5},{5,3},{10,12},{12,10},{11,13},{13,11},{18,20},{2... | collective-permute-start | bytes 1572872 | tf_op jit(solution)/shard_map/ppermute | solution.py:383
  29.1 14.5 %collective-permute-start.3 = (bf16[128,2048]{1,0:T(8,128)(2,1)}, bf16[128,2048]{1,0:T(8,128)(2,1)}, u32[]{:S(2)}, u32[]{:S(2)}) collective-permute-start(bf16[128,2048]{1,0:T(8,128)(2,1)} %collective-permute-done.1.refs_2_), channel_id=1, source_target_pairs={{4,6},{2,0},{5,7},{3,1},{12,14},{10,8},{13,15},{11,9},{20,22},{18,... | collective-permute-start | bytes 1572872 | tf_op jit(solution)/shard_map/ppermute | solution.py:384
  30.4 7.0 %copy-start.11 = (bf16[128,2048]{1,0:T(8,128)(2,1)}, bf16[128,2048]{1,0:T(8,128)(2,1)S(1)}, u32[]{:S(2)}) copy-start(bf16[128,2048]{1,0:T(8,128)(2,1)S(1)} %collective-permute-done.refs_1_) | copy-start | bytes 1572868
  37.4 1.1 copy-start
  38.5 0.9 copy-start.13
  39.4 23.1 %all-to-all-start.1 = ((bf16[4,384,512]{2,1,0:T(8,128)(2,1)}), bf16[4,384,512]{2,1,0:T(8,128)(2,1)S(1)}, u32[]{:S(2)}, u32[]{:S(2)}) async-start(bf16[4,384,512]{2,1,0:T(8,128)(2,1)} %copy-done), calls=%async_computation.1 | async-start | bytes 3145728 | tf_op jit(solution)/shard_map/all_to_all | solution.py:390
  44.7 9.4 %copy-start.1 = (bf16[128,2048]{1,0:T(8,128)(2,1)}, bf16[128,2048]{1,0:T(8,128)(2,1)S(1)}, u32[]{:S(2)}) copy-start(bf16[128,2048]{1,0:T(8,128)(2,1)S(1)} %broadcast_select_fusion.1.refs_0_.refs_3_) | copy-start | bytes 1572868
  44.7 10.2 %copy-start.5 = (f32[128,128]{1,0:T(8,128)S(1)}, f32[128,128]{1,0:T(8,128)}, u32[]{:S(2)}) copy-start(f32[128,128]{1,0:T(8,128)} %f_ref.3) | copy-start | bytes 196612
  44.7 27.1 %collective-permute-start.5 = (bf16[128,2048]{1,0:T(8,128)(2,1)}, bf16[128,2048]{1,0:T(8,128)(2,1)}, u32[]{:S(2)}, u32[]{:S(2)}) collective-permute-start(bf16[128,2048]{1,0:T(8,128)(2,1)} %bitcast.5), channel_id=1, source_target_pairs={{0,4},{4,0},{2,6},{6,2},{1,5},{5,1},{3,7},{7,3},{8,12},{12,8},{10,... | collective-permute-start | bytes 1572872 | tf_op jit(solution)/shard_map/ppermute | solution.py:382
  49.1 24.5 %collective-permute-start.4 = (bf16[128,2048]{1,0:T(8,128)(2,1)}, bf16[128,2048]{1,0:T(8,128)(2,1)}, u32[]{:S(2)}, u32[]{:S(2)}) collective-permute-start(bf16[128,2048]{1,0:T(8,128)(2,1)} %bitcast.6), channel_id=1, source_target_pairs={{0,2},{2,0},{4,6},{6,4},{1,3},{3,1},{5,7},{7,5},{8,10},{10,8},{12,... | collective-permute-start | bytes 1572872 | tf_op jit(solution)/shard_map/ppermute | solution.py:381
  54.1 0.8 copy-start.3
  54.9 6.1 %copy-start.15 = (f32[128,512]{1,0:T(8,128)}, f32[128,512]{1,0:T(8,128)S(1)}, u32[]{:S(2)}) copy-start(f32[128,512]{1,0:T(8,128)S(1)} %get-tuple-element.35.refs_2_) | copy-start | bytes 786436
  59.5 15.7 %collective-permute-start.7 = (bf16[512,512]{1,0:T(8,128)(2,1)}, bf16[512,512]{1,0:T(8,128)(2,1)}, u32[]{:S(2)}, u32[]{:S(2)}) collective-permute-start(bf16[512,512]{1,0:T(8,128)(2,1)} %shard_map.97.refs_8_), channel_id=1, source_target_pairs={{0,16},{16,0},{8,24},{24,8},{1,17},{17,1},{9,25},{25,9},{2,18},{18... | collective-permute-start | bytes 1572872 | tf_op jit(solution)/shard_map/ppermute | solution.py:395
  61.0 17.4 %collective-permute-start.6 = (bf16[512,512]{1,0:T(8,128)(2,1)}, bf16[512,512]{1,0:T(8,128)(2,1)}, u32[]{:S(2)}, u32[]{:S(2)}) collective-permute-start(bf16[512,512]{1,0:T(8,128)(2,1)} %shard_map.97.refs_8_), channel_id=1, source_target_pairs={{0,8},{8,0},{16,24},{24,16},{1,9},{9,1},{17,25},{25,17},{2,10},{10... | collective-permute-start | bytes 1572872 | tf_op jit(solution)/shard_map/ppermute | solution.py:394
  62.5 19.0 %all-to-all-start.2 = ((bf16[4,128,512]{2,1,0:T(8,128)(2,1)}), bf16[4,128,512]{2,1,0:T(8,128)(2,1)}, u32[]{:S(2)}, u32[]{:S(2)}) async-start(bf16[4,128,512]{2,1,0:T(8,128)(2,1)} %copy-done.3), calls=%async_computation.2 | async-start | bytes 1048576 | tf_op jit(solution)/shard_map/all_to_all | solution.py:390
  66.7 27.3 %collective-permute-start.19 = (bf16[128,2048]{1,0:T(8,128)(2,1)}, bf16[128,2048]{1,0:T(8,128)(2,1)}, u32[]{:S(2)}, u32[]{:S(2)}) collective-permute-start(bf16[128,2048]{1,0:T(8,128)(2,1)} %bitcast.7), channel_id=1, source_target_pairs={{2,4},{4,2},{3,5},{5,3},{10,12},{12,10},{11,13},{13,11},{18,20},{2... | collective-permute-start | bytes 1572872 | tf_op jit(solution)/shard_map/ppermute | solution.py:383
  73.6 20.8 %collective-permute-start.20 = (bf16[128,2048]{1,0:T(8,128)(2,1)}, bf16[128,2048]{1,0:T(8,128)(2,1)}, u32[]{:S(2)}, u32[]{:S(2)}) collective-permute-start(bf16[128,2048]{1,0:T(8,128)(2,1)} %collective-permute-done.5.refs_2_), channel_id=1, source_target_pairs={{4,6},{2,0},{5,7},{3,1},{12,14},{10,8},{13,15},{11,9},{20,22},{18,... | collective-permute-start | bytes 1572872 | tf_op jit(solution)/shard_map/ppermute | solution.py:384
  76.9 16.3 %collective-permute-start.9 = (bf16[256,512]{1,0:T(8,128)(2,1)}, bf16[256,512]{1,0:T(8,128)(2,1)S(1)}, u32[]{:S(2)}, u32[]{:S(2)}) collective-permute-start(bf16[256,512]{1,0:T(8,128)(2,1)} %slice.17), channel_id=1, source_target_pairs={{0,8},{8,0},{16,24},{24,16},{1,9},{9,1},{17,25},{25,17},{2,10},{10... | collective-permute-start | bytes 786440 | tf_op jit(solution)/shard_map/ppermute | solution.py:403
  80.1 13.2 %collective-permute-start.8 = (bf16[256,512]{1,0:T(8,128)(2,1)}, bf16[256,512]{1,0:T(8,128)(2,1)}, u32[]{:S(2)}, u32[]{:S(2)}) collective-permute-start(bf16[256,512]{1,0:T(8,128)(2,1)} %slice.16), channel_id=1, source_target_pairs={{0,16},{16,0},{8,24},{24,8},{1,17},{17,1},{9,25},{25,9},{2,18},{18... | collective-permute-start | bytes 786440 | tf_op jit(solution)/shard_map/ppermute | solution.py:402
  81.6 1.1 copy-start.14
  82.7 0.9 copy-start.16
  83.7 9.7 %copy-start.12 = (bf16[128,2048]{1,0:T(8,128)(2,1)S(1)}, bf16[128,2048]{1,0:T(8,128)(2,1)}, u32[]{:S(2)}) copy-start(bf16[128,2048]{1,0:T(8,128)(2,1)} %copy-done.11) | copy-start | bytes 1572868
  83.7 12.5 %copy-start.2 = (bf16[128,2048]{1,0:T(8,128)(2,1)S(1)}, bf16[128,2048]{1,0:T(8,128)(2,1)}, u32[]{:S(2)}) copy-start(bf16[128,2048]{1,0:T(8,128)(2,1)} %copy-done.1) | copy-start | bytes 1572868
  83.7 18.4 %copy-start.10 = (bf16[1,128,2048]{2,1,0:T(8,128)(2,1)S(1)}, bf16[1,128,2048]{2,1,0:T(8,128)(2,1)}, u32[]{:S(2)}) copy-start(bf16[1,128,2048]{2,1,0:T(8,128)(2,1)} %param.8) | copy-start | bytes 1572868
  93.3 4.4 %collective-permute-start.10 = (bf16[128,2048]{1,0:T(8,128)(2,1)}, bf16[128,2048]{1,0:T(8,128)(2,1)S(1)}, u32[]{:S(2)}, u32[]{:S(2)}) collective-permute-start(bf16[128,2048]{1,0:T(8,128)(2,1)} %bitcast.3.refs_0_), channel_id=1, source_target_pairs={{0,1},{1,0},{2,3},{3,2},{4,5},{5,4},{6,7},{7,6},{8,9},{9,8},{10,11... | collective-permute-start | bytes 1572872 | tf_op jit(solution)/shard_map/ppermute | solution.py:408
  93.4 4.7 %collective-permute-start.11 = (bf16[128,2048]{1,0:T(8,128)(2,1)S(1)}, bf16[128,2048]{1,0:T(8,128)(2,1)S(1)}, u32[]{:S(2)}, u32[]{:S(2)}) collective-permute-start(bf16[128,2048]{1,0:T(8,128)(2,1)S(1)} %copy-done.12), channel_id=1, source_target_pairs={{0,1},{1,0},{2,3},{3,2},{4,5},{5,4},{6,7},{7,6},{8,9},{9,8},{10,11... | collective-permute-start | bytes 1572872 | tf_op jit(solution)/shard_map/ppermute | solution.py:408
  93.9 2.4 %collective-permute-start.17 = (bf16[256,512]{1,0:T(8,128)(2,1)}, bf16[256,512]{1,0:T(8,128)(2,1)S(1)}, u32[]{:S(2)}, u32[]{:S(2)}) collective-permute-start(bf16[256,512]{1,0:T(8,128)(2,1)} %collective-permute-done.8.refs_11_), channel_id=1, source_target_pairs={{0,1},{1,0},{2,3},{3,2},{4,5},{5,4},{6,7},{7,6},{8,9},{9,8},{10,11... | collective-permute-start | bytes 786440 | tf_op jit(solution)/shard_map/ppermute | solution.py:408
  94.0 3.6 %collective-permute-start.18 = (bf16[256,512]{1,0:T(8,128)(2,1)S(1)}, bf16[256,512]{1,0:T(8,128)(2,1)S(1)}, u32[]{:S(2)}, u32[]{:S(2)}) collective-permute-start(bf16[256,512]{1,0:T(8,128)(2,1)S(1)} %collective-permute-done.9.refs_12_), channel_id=1, source_target_pairs={{0,1},{1,0},{2,3},{3,2},{4,5},{5,4},{6,7},{7,6},{8,9},{9,8},{10,11... | collective-permute-start | bytes 786440 | tf_op jit(solution)/shard_map/ppermute | solution.py:408
  94.4 4.9 %collective-permute-start.12 = (bf16[128,2048]{1,0:T(8,128)(2,1)}, bf16[128,2048]{1,0:T(8,128)(2,1)S(1)}, u32[]{:S(2)}, u32[]{:S(2)}) collective-permute-start(bf16[128,2048]{1,0:T(8,128)(2,1)} %collective-permute-done.1.refs_2_), channel_id=1, source_target_pairs={{0,1},{1,0},{2,3},{3,2},{4,5},{5,4},{6,7},{7,6},{8,9},{9,8},{10,11... | collective-permute-start | bytes 1572872 | tf_op jit(solution)/shard_map/ppermute | solution.py:408
  96.2 3.5 %collective-permute-start.13 = (bf16[128,2048]{1,0:T(8,128)(2,1)S(1)}, bf16[128,2048]{1,0:T(8,128)(2,1)S(1)}, u32[]{:S(2)}, u32[]{:S(2)}) collective-permute-start(bf16[128,2048]{1,0:T(8,128)(2,1)S(1)} %copy-done.2), channel_id=1, source_target_pairs={{0,1},{1,0},{2,3},{3,2},{4,5},{5,4},{6,7},{7,6},{8,9},{9,8},{10,11... | collective-permute-start | bytes 1572872 | tf_op jit(solution)/shard_map/ppermute | solution.py:408
  97.5 2.8 %collective-permute-start.14 = (bf16[512,512]{1,0:T(8,128)(2,1)}, bf16[512,512]{1,0:T(8,128)(2,1)S(1)}, u32[]{:S(2)}, u32[]{:S(2)}) collective-permute-start(bf16[512,512]{1,0:T(8,128)(2,1)} %shard_map.97.refs_8_), channel_id=1, source_target_pairs={{0,1},{1,0},{2,3},{3,2},{4,5},{5,4},{6,7},{7,6},{8,9},{9,8},{10,11... | collective-permute-start | bytes 1572872 | tf_op jit(solution)/shard_map/ppermute | solution.py:408
  97.6 4.4 %collective-permute-start.15 = (bf16[512,512]{1,0:T(8,128)(2,1)}, bf16[512,512]{1,0:T(8,128)(2,1)S(1)}, u32[]{:S(2)}, u32[]{:S(2)}) collective-permute-start(bf16[512,512]{1,0:T(8,128)(2,1)} %collective-permute-done.6.refs_9_), channel_id=1, source_target_pairs={{0,1},{1,0},{2,3},{3,2},{4,5},{5,4},{6,7},{7,6},{8,9},{9,8},{10,11... | collective-permute-start | bytes 1572872 | tf_op jit(solution)/shard_map/ppermute | solution.py:408
  98.0 4.0 %collective-permute-start.16 = (bf16[512,512]{1,0:T(8,128)(2,1)}, bf16[512,512]{1,0:T(8,128)(2,1)S(1)}, u32[]{:S(2)}, u32[]{:S(2)}) collective-permute-start(bf16[512,512]{1,0:T(8,128)(2,1)} %collective-permute-done.7.refs_10_), channel_id=1, source_target_pairs={{0,1},{1,0},{2,3},{3,2},{4,5},{5,4},{6,7},{7,6},{8,9},{9,8},{10,11... | collective-permute-start | bytes 1572872 | tf_op jit(solution)/shard_map/ppermute | solution.py:408
  99.3 24.0 %collective-permute-start.29 = (bf16[528,512]{1,0:T(8,128)(2,1)S(1)}, bf16[528,512]{1,0:T(8,128)(2,1)S(1)}, u32[]{:S(2)}, u32[]{:S(2)}) collective-permute-start(bf16[528,512]{1,0:T(8,128)(2,1)S(1)} %shard_map.98.refs_8_.refs_12_), channel_id=1, source_target_pairs={{0,1},{1,0},{2,3},{3,2},{4,5},{5,4},{6,7},{7,6},{8,9},{9,8},{10,11... | collective-permute-start | bytes 1622024 | tf_op jit(solution)/shard_map/ppermute | solution.py:408
  99.7 18.1 %collective-permute-start.26 = (bf16[528,512]{1,0:T(8,128)(2,1)S(1)}, bf16[528,512]{1,0:T(8,128)(2,1)S(1)}, u32[]{:S(2)}, u32[]{:S(2)}) collective-permute-start(bf16[528,512]{1,0:T(8,128)(2,1)S(1)} %shard_map.98.refs_8_.refs_12_), channel_id=1, source_target_pairs={{0,16},{16,0},{8,24},{24,8},{1,17},{17,1},{9,25},{25,9},{2,18},{18... | collective-permute-start | bytes 1622024 | tf_op jit(solution)/shard_map/ppermute | solution.py:395
  100.3 2.3 %copy-start.20 = (bf16[512,512]{1,0:T(8,128)(2,1)}, bf16[512,512]{1,0:T(8,128)(2,1)S(1)}, u32[]{:S(2)}) copy-start(bf16[512,512]{1,0:T(8,128)(2,1)S(1)} %collective-permute-done.14.refs_13_) | copy-start | bytes 1572868
  100.3 17.5 %collective-permute-start.25 = (bf16[528,512]{1,0:T(8,128)(2,1)S(1)}, bf16[528,512]{1,0:T(8,128)(2,1)S(1)}, u32[]{:S(2)}, u32[]{:S(2)}) collective-permute-start(bf16[528,512]{1,0:T(8,128)(2,1)S(1)} %shard_map.98.refs_8_.refs_12_), channel_id=1, source_target_pairs={{0,8},{8,0},{16,24},{24,16},{1,9},{9,1},{17,25},{25,17},{2,10},{10... | collective-permute-start | bytes 1622024 | tf_op jit(solution)/shard_map/ppermute | solution.py:394
  102.0 0.8 copy-start.21
  102.0 16.4 %collective-permute-start.24 = (bf16[128,2048]{1,0:T(8,128)(2,1)S(1)}, bf16[128,2048]{1,0:T(8,128)(2,1)S(1)}, u32[]{:S(2)}, u32[]{:S(2)}) collective-permute-start(bf16[128,2048]{1,0:T(8,128)(2,1)S(1)} %broadcast_select_fusion.refs_3_), channel_id=1, source_target_pairs={{0,1},{1,0},{2,3},{3,2},{4,5},{5,4},{6,7},{7,6},{8,9},{9,8},{10,11... | collective-permute-start | bytes 1572872 | tf_op jit(solution)/shard_map/ppermute | solution.py:408
  102.1 1.0 copy-start.22
  102.1 16.7 %collective-permute-start.21 = (bf16[128,2048]{1,0:T(8,128)(2,1)S(1)}, bf16[128,2048]{1,0:T(8,128)(2,1)S(1)}, u32[]{:S(2)}, u32[]{:S(2)}) collective-permute-start(bf16[128,2048]{1,0:T(8,128)(2,1)S(1)} %bitcast.8), channel_id=1, source_target_pairs={{0,1},{1,0},{2,3},{3,2},{4,5},{5,4},{6,7},{7,6},{8,9},{9,8},{10,11... | collective-permute-start | bytes 1572872 | tf_op jit(solution)/shard_map/ppermute | solution.py:408
  117.8 5.5 %copy-start.17 = (bf16[528,512]{1,0:T(8,128)(2,1)}, bf16[528,512]{1,0:T(8,128)(2,1)S(1)}, u32[]{:S(2)}) copy-start(bf16[528,512]{1,0:T(8,128)(2,1)S(1)} %collective-permute-done.26.refs_12_.refs_14_) | copy-start | bytes 1622020
  117.8 18.9 %copy-start.4 = (bf16[528,512]{1,0:T(8,128)(2,1)}, bf16[528,512]{1,0:T(8,128)(2,1)S(1)}, u32[]{:S(2)}) copy-start(bf16[528,512]{1,0:T(8,128)(2,1)S(1)} %collective-permute-done.25.refs_10_.refs_13_) | copy-start | bytes 1622020
  117.8 5.5 %collective-permute-start.30 = (bf16[528,512]{1,0:T(8,128)(2,1)S(1)}, bf16[528,512]{1,0:T(8,128)(2,1)S(1)}, u32[]{:S(2)}, u32[]{:S(2)}) collective-permute-start(bf16[528,512]{1,0:T(8,128)(2,1)S(1)} %collective-permute-done.25.refs_10_.refs_13_), channel_id=1, source_target_pairs={{0,1},{1,0},{2,3},{3,2},{4,5},{5,4},{6,7},{7,6},{8,9},{9,8},{10,11... | collective-permute-start | bytes 1622024 | tf_op jit(solution)/shard_map/ppermute | solution.py:408
  118.2 5.1 %collective-permute-start.31 = (bf16[528,512]{1,0:T(8,128)(2,1)S(1)}, bf16[528,512]{1,0:T(8,128)(2,1)S(1)}, u32[]{:S(2)}, u32[]{:S(2)}) collective-permute-start(bf16[528,512]{1,0:T(8,128)(2,1)S(1)} %collective-permute-done.26.refs_12_.refs_14_), channel_id=1, source_target_pairs={{0,1},{1,0},{2,3},{3,2},{4,5},{5,4},{6,7},{7,6},{8,9},{9,8},{10,11... | collective-permute-start | bytes 1622024 | tf_op jit(solution)/shard_map/ppermute | solution.py:408
  118.4 3.1 %collective-permute-start.22 = (bf16[128,2048]{1,0:T(8,128)(2,1)}, bf16[128,2048]{1,0:T(8,128)(2,1)S(1)}, u32[]{:S(2)}, u32[]{:S(2)}) collective-permute-start(bf16[128,2048]{1,0:T(8,128)(2,1)} %collective-permute-done.4.refs_1_), channel_id=1, source_target_pairs={{0,1},{1,0},{2,3},{3,2},{4,5},{5,4},{6,7},{7,6},{8,9},{9,8},{10,11... | collective-permute-start | bytes 1572872 | tf_op jit(solution)/shard_map/ppermute | solution.py:408
  118.7 3.6 %collective-permute-start.23 = (bf16[128,2048]{1,0:T(8,128)(2,1)}, bf16[128,2048]{1,0:T(8,128)(2,1)S(1)}, u32[]{:S(2)}, u32[]{:S(2)}) collective-permute-start(bf16[128,2048]{1,0:T(8,128)(2,1)} %collective-permute-done.5.refs_2_), channel_id=1, source_target_pairs={{0,1},{1,0},{2,3},{3,2},{4,5},{5,4},{6,7},{7,6},{8,9},{9,8},{10,11... | collective-permute-start | bytes 1572872 | tf_op jit(solution)/shard_map/ppermute | solution.py:408
  121.6 15.3 %collective-permute-start.27 = (bf16[256,512]{1,0:T(8,128)(2,1)S(1)}, bf16[256,512]{1,0:T(8,128)(2,1)S(1)}, u32[]{:S(2)}, u32[]{:S(2)}) collective-permute-start(bf16[256,512]{1,0:T(8,128)(2,1)S(1)} %slice.14), channel_id=1, source_target_pairs={{0,16},{16,0},{8,24},{24,8},{1,17},{17,1},{9,25},{25,9},{2,18},{18... | collective-permute-start | bytes 786440 | tf_op jit(solution)/shard_map/ppermute | solution.py:402
  122.3 14.4 %collective-permute-start.28 = (bf16[272,512]{1,0:T(8,128)(2,1)S(1)}, bf16[272,512]{1,0:T(8,128)(2,1)S(1)}, u32[]{:S(2)}, u32[]{:S(2)}) collective-permute-start(bf16[272,512]{1,0:T(8,128)(2,1)S(1)} %slice.15), channel_id=1, source_target_pairs={{0,8},{8,0},{16,24},{24,16},{1,9},{9,1},{17,25},{25,17},{2,10},{10... | collective-permute-start | bytes 835592 | tf_op jit(solution)/shard_map/ppermute | solution.py:403
  123.3 13.4 %copy-start.6 = (bf16[528,512]{1,0:T(8,128)(2,1)}, bf16[528,512]{1,0:T(8,128)(2,1)S(1)}, u32[]{:S(2)}) copy-start(bf16[528,512]{1,0:T(8,128)(2,1)S(1)} %collective-permute-done.29.refs_9_.refs_16_) | copy-start | bytes 1622020
  123.3 0.8 copy-start.18
  124.2 0.8 copy-start.19
  136.8 2.0 %collective-permute-start.33 = (bf16[272,512]{1,0:T(8,128)(2,1)S(1)}, bf16[272,512]{1,0:T(8,128)(2,1)S(1)}, u32[]{:S(2)}, u32[]{:S(2)}) collective-permute-start(bf16[272,512]{1,0:T(8,128)(2,1)S(1)} %collective-permute-done.28.refs_9_.refs_15_), channel_id=1, source_target_pairs={{0,1},{1,0},{2,3},{3,2},{4,5},{5,4},{6,7},{7,6},{8,9},{9,8},{10,11... | collective-permute-start | bytes 835592 | tf_op jit(solution)/shard_map/ppermute | solution.py:408
  136.8 1.9 %collective-permute-start.32 = (bf16[256,512]{1,0:T(8,128)(2,1)S(1)}, bf16[256,512]{1,0:T(8,128)(2,1)S(1)}, u32[]{:S(2)}, u32[]{:S(2)}) collective-permute-start(bf16[256,512]{1,0:T(8,128)(2,1)S(1)} %collective-permute-done.27.refs_8_), channel_id=1, source_target_pairs={{0,1},{1,0},{2,3},{3,2},{4,5},{5,4},{6,7},{7,6},{8,9},{9,8},{10,11... | collective-permute-start | bytes 786440 | tf_op jit(solution)/shard_map/ppermute | solution.py:408

commit v5 on v4

--- a/solution.py
+++ b/solution.py
@@ -87,7 +87,7 @@
             gt[rows, b * n : (b + 1) * n] = gate * conv[b * size : (b + 1) * size]
         return carry
 
-    lax.fori_loop(0, groups, one, 0, unroll=4)
+    lax.fori_loop(0, groups, one, 0, unroll=16)
     for b in range(blocks):
         out_ref[b * n : (b + 1) * n, :] = gt[:, b * n : (b + 1) * n].T.astype(bf16)
 
@@ -171,7 +171,7 @@
         sums[pl.ds(pl.multiple_of(g * 8, 8), 8), :] = ring
         return carry
 
-    lax.fori_loop(0, groups, one, 0, unroll=4)
+    lax.fori_loop(0, groups, one, 0, unroll=16)
     total = sums[pl.ds(0, groups, stride=8), :]
     for i in range(1, 8):
         total = total + pltpu.roll(sums[pl.ds(i, groups, stride=8), :], n - i, 1)
@@ -291,7 +291,7 @@
         scratch_shapes=[
             pltpu.VMEM((toks, left_width), bf16),
             pltpu.VMEM((toks, right_width), bf16),
-            pltpu.VMEM((2, TILE, right_width), f32),
+            pltpu.VMEM((2, 2 * TILE, right_width), f32),
             pltpu.SemaphoreType.DMA((8 + len(pieces),)),
             pltpu.SemaphoreType.DMA((2,)),
         ],

time: 147 us -> 143 us (0.973)
  Pallas kernels: 60.1 us -> 55.3 us
    pallas_call x1, Pallas kernels: 9.58 us -> 6.55 us  [backward(): pl.pallas_call(functools.partial(backward_kernel, size, counts), out_shap...]
  transfers between devices with their start and end apart: 37 -> 37, of which waited for: 10 -> 10; matrix products, arithmetic and copies ran while one was open for 4% -> 4% of each run, Pallas kernels for 37% -> 35%
where the time goes in v5:
time: 143 us; the launch traced here: 142 us
  Pallas kernels  55.3 us (39%)
  starting transfers between devices  42.2 us (30%)
  waiting for transfers between devices  27 us (19%)
  local copies, waits for them, and re-layouts  13.7 us (10%)
  other arithmetic  2.27 us (2%)
    pallas_call x2, Pallas kernels, value_part(): pl.pallas_call(functools.partial(value_kernel, n, width, which, layout, w...  18.1 us
    ppermute x2, waiting for transfers between devices, line_slots(): second = lax.ppermute(x, 'col', far)  16.8 us
    pallas_call x1, Pallas kernels, out_gradient(): pl.pallas_call(functools.partial(out_kernel, n, layout), out_shape=jax.Sh...  14.3 us
    all_to_all x3, starting transfers between devices, swap_rows(): return lax.all_to_all(x, 'row', split_axis=0, concat_axis=0, tiled=True)  11.9 us
    pallas_call x2, Pallas kernels, project(): pl.pallas_call(functools.partial(project_kernel, len(slots)), out_shape=[...  11.5 us
    unnamed x46, local copies, waits for them, and re-layouts  10.3 us
    ppermute x2, starting transfers between devices, line_slots(): second = lax.ppermute(x, 'col', far)  8.49 us
    ppermute x18, waiting for transfers between devices, other_core(): return [lax.ppermute(x, 'dp', swap) for x in xs]  7.41 us
  transfers between devices with their start and end apart: 37, of which 10 were waited for; matrix products, arithmetic and copies ran while one was open for 4% of the time, Pallas kernels for 35%

profile of v5, /device:TPU:0, one launch (start us, length us, event | category | flops | bytes accessed | tf_op | source)
XLA Modules:
  0.0 141.8 jit_solution(10739279765311488799)
XLA Ops:
  0.6 4.1 %collective-permute-start.1 = (bf16[128,2048]{1,0:T(8,128)(2,1)}, bf16[128,2048]{1,0:T(8,128)(2,1)}, u32[]{:S(2)}, u32[]{:S(2)}) collective-permute-start(bf16[128,2048]{1,0:T(8,128)(2,1)} %bitcast.3.refs_0_), channel_id=1, source_target_pairs={{0,4},{4,0},{2,6},{6,2},{1,5},{5,1},{3,7},{7,3},{8,12},{12,8},{10,... | collective-permute-start | bytes 1572872 | tf_op jit(solution)/shard_map/ppermute | solution.py:382
  4.7 1.6 %collective-permute-start = (bf16[128,2048]{1,0:T(8,128)(2,1)}, bf16[128,2048]{1,0:T(8,128)(2,1)S(1)}, u32[]{:S(2)}, u32[]{:S(2)}) collective-permute-start(bf16[128,2048]{1,0:T(8,128)(2,1)} %bitcast.3.refs_0_), channel_id=1, source_target_pairs={{0,2},{2,0},{4,6},{6,4},{1,3},{3,1},{5,7},{7,5},{8,10},{10,8},{12,... | collective-permute-start | bytes 1572872 | tf_op jit(solution)/shard_map/ppermute | solution.py:381
  6.3 1.0 copy-done.7
  7.4 1.0 copy-done.8
  8.4 1.0 copy-done.9
  9.4 1.6 %shard_map.96 = bf16[4,3,512,128]{3,2,1,0:T(8,128)(2,1)} custom-call(bf16[1,128,2048]{2,1,0:T(8,128)(2,1)S(1)} %copy-done.7, bf16[1,128,2048]{2,1,0:T(8,128)(2,1)S(1)} %copy-done.8, bf16[1,128,2048]{2,1,0:T(8,128)(2,1)S(1)} %copy-done.9), custom_call_target="tpu_custom_call" | custom-call | flops 3449999872 | tf_op jit(solution)/shard_map/pallas_call | solution.py:41
  11.0 3.7 %all-to-all-start = ((bf16[4,3,512,128]{3,2,1,0:T(8,128)(2,1)}), bf16[4,3,512,128]{3,2,1,0:T(8,128)(2,1)S(1)}, u32[]{:S(2)}, u32[]{:S(2)}) async-start(bf16[4,3,512,128]{3,2,1,0:T(8,128)(2,1)} %shard_map.96), calls=%async_computation | async-start | bytes 3145728 | tf_op jit(solution)/shard_map/all_to_all | solution.py:390
  14.8 1.5 %collective-permute-start.2 = (bf16[128,2048]{1,0:T(8,128)(2,1)}, bf16[128,2048]{1,0:T(8,128)(2,1)}, u32[]{:S(2)}, u32[]{:S(2)}) collective-permute-start(bf16[128,2048]{1,0:T(8,128)(2,1)} %bitcast.3.refs_0_), channel_id=1, source_target_pairs={{2,4},{4,2},{3,5},{5,3},{10,12},{12,10},{11,13},{13,11},{18,20},{2... | collective-permute-start | bytes 1572872 | tf_op jit(solution)/shard_map/ppermute | solution.py:383
  16.3 12.8 %collective-permute-done.1.refs_2_ = bf16[128,2048]{1,0:T(8,128)(2,1)} collective-permute-done((bf16[128,2048]{1,0:T(8,128)(2,1)}, bf16[128,2048]{1,0:T(8,128)(2,1)}, u32[]{:S(2)}, u32[]{:S(2)}) %collective-permute-start.1) | collective-permute-done | bytes 524320 | tf_op jit(solution)/shard_map/ppermute | solution.py:382
  29.1 1.3 collective-permute-start.3
  30.4 7.0 %shard_map.94 = (f32[384,512]{1,0:T(8,128)S(1)}, bf16[4,384,512]{2,1,0:T(8,128)(2,1)S(1)}) custom-call(s32[3]{0:T(128)S(1)} %pad_add_fusion.pos_ref, bf16[128,2048]{1,0:T(8,128)(2,1)} %bitcast.3.refs_0_, bf16[128,2048]{1,0:T(8,128)(2,1)S(1)} %collective-permute-done.refs_1_, bf16[128,2048]{1,0:T(8,128)(2,1)} %collective-permute-done.1.refs_2_, ...), custom_call_target="tpu_custom_call" | custom-call | flops 9200000000 | tf_op jit(solution)/shard_map/pallas_call | solution.py:224
  37.4 1.1 copy-done
  38.5 0.9 copy-done.13
  39.4 4.1 %all-to-all-start.1 = ((bf16[4,384,512]{2,1,0:T(8,128)(2,1)}), bf16[4,384,512]{2,1,0:T(8,128)(2,1)S(1)}, u32[]{:S(2)}, u32[]{:S(2)}) async-start(bf16[4,384,512]{2,1,0:T(8,128)(2,1)} %copy-done), calls=%async_computation.1 | async-start | bytes 3145728 | tf_op jit(solution)/shard_map/all_to_all | solution.py:390
  43.6 1.1 broadcast_select_fusion.1.refs_0_.refs_3_
  44.7 4.4 %collective-permute-start.5 = (bf16[128,2048]{1,0:T(8,128)(2,1)}, bf16[128,2048]{1,0:T(8,128)(2,1)}, u32[]{:S(2)}, u32[]{:S(2)}) collective-permute-start(bf16[128,2048]{1,0:T(8,128)(2,1)} %bitcast.5), channel_id=1, source_target_pairs={{0,4},{4,0},{2,6},{6,2},{1,5},{5,1},{3,7},{7,3},{8,12},{12,8},{10,... | collective-permute-start | bytes 1572872 | tf_op jit(solution)/shard_map/ppermute | solution.py:382
  49.1 0.5 collective-permute-start.4
  49.5 4.5 %shard_map.95 = (f32[128,512]{1,0:T(8,128)S(1)}, bf16[4,128,512]{2,1,0:T(8,128)(2,1)S(1)}) custom-call(s32[3]{0:T(128)S(1)} %pad_add_fusion.pos_ref, bf16[128,2048]{1,0:T(8,128)(2,1)S(1)} %broadcast_select_fusion.1.refs_0_.refs_3_, bf16[2048,2048]{1,0:T(8,128)(2,1)} %refs_1_.1), custom_call_target="tpu_custom_call" | custom-call | flops 9200000000 | tf_op jit(solution)/shard_map/pallas_call | solution.py:224
  54.1 0.8 copy-done.3
  54.9 3.3 %shard_map.97.refs_8_ = bf16[512,512]{1,0:T(8,128)(2,1)} custom-call(s32[3]{0:T(128)S(1)} %pad_add_fusion.pos_ref, f32[128,128]{1,0:T(8,128)S(1)} %copy-done.5, bf16[4,3,512,128]{3,2,1,0:T(8,128)(2,1)S(1)} %all-to-all-done.parts_ref), custom_call_target="tpu_custom_call" | custom-call | tf_op jit(solution)/shard_map/pallas_call | solution.py:98
  58.2 1.5 %collective-permute-start.7 = (bf16[512,512]{1,0:T(8,128)(2,1)}, bf16[512,512]{1,0:T(8,128)(2,1)}, u32[]{:S(2)}, u32[]{:S(2)}) collective-permute-start(bf16[512,512]{1,0:T(8,128)(2,1)} %shard_map.97.refs_8_), channel_id=1, source_target_pairs={{0,16},{16,0},{8,24},{24,8},{1,17},{17,1},{9,25},{25,9},{2,18},{18... | collective-permute-start | bytes 1572872 | tf_op jit(solution)/shard_map/ppermute | solution.py:395
  59.7 1.5 %collective-permute-start.6 = (bf16[512,512]{1,0:T(8,128)(2,1)}, bf16[512,512]{1,0:T(8,128)(2,1)}, u32[]{:S(2)}, u32[]{:S(2)}) collective-permute-start(bf16[512,512]{1,0:T(8,128)(2,1)} %shard_map.97.refs_8_), channel_id=1, source_target_pairs={{0,8},{8,0},{16,24},{24,16},{1,9},{9,1},{17,25},{25,17},{2,10},{10... | collective-permute-start | bytes 1572872 | tf_op jit(solution)/shard_map/ppermute | solution.py:394
  61.2 0.9 all-to-all-done.1.refs_1_
  62.1 4.1 %all-to-all-start.2 = ((bf16[4,128,512]{2,1,0:T(8,128)(2,1)}), bf16[4,128,512]{2,1,0:T(8,128)(2,1)}, u32[]{:S(2)}, u32[]{:S(2)}) async-start(bf16[4,128,512]{2,1,0:T(8,128)(2,1)} %copy-done.3), calls=%async_computation.2 | async-start | bytes 1048576 | tf_op jit(solution)/shard_map/all_to_all | solution.py:390
  66.3 1.5 %collective-permute-start.19 = (bf16[128,2048]{1,0:T(8,128)(2,1)}, bf16[128,2048]{1,0:T(8,128)(2,1)}, u32[]{:S(2)}, u32[]{:S(2)}) collective-permute-start(bf16[128,2048]{1,0:T(8,128)(2,1)} %bitcast.7), channel_id=1, source_target_pairs={{2,4},{4,2},{3,5},{5,3},{10,12},{12,10},{11,13},{13,11},{18,20},{2... | collective-permute-start | bytes 1572872 | tf_op jit(solution)/shard_map/ppermute | solution.py:383
  67.8 4.0 %collective-permute-done.5.refs_2_ = bf16[128,2048]{1,0:T(8,128)(2,1)} collective-permute-done((bf16[128,2048]{1,0:T(8,128)(2,1)}, bf16[128,2048]{1,0:T(8,128)(2,1)}, u32[]{:S(2)}, u32[]{:S(2)}) %collective-permute-start.5) | collective-permute-done | bytes 524320 | tf_op jit(solution)/shard_map/ppermute | solution.py:382
  71.8 1.8 %collective-permute-done.4.refs_1_ = bf16[128,2048]{1,0:T(8,128)(2,1)} collective-permute-done((bf16[128,2048]{1,0:T(8,128)(2,1)}, bf16[128,2048]{1,0:T(8,128)(2,1)}, u32[]{:S(2)}, u32[]{:S(2)}) %collective-permute-start.4) | collective-permute-done | bytes 524320 | tf_op jit(solution)/shard_map/ppermute | solution.py:381
  73.6 1.5 %collective-permute-start.20 = (bf16[128,2048]{1,0:T(8,128)(2,1)}, bf16[128,2048]{1,0:T(8,128)(2,1)}, u32[]{:S(2)}, u32[]{:S(2)}) collective-permute-start(bf16[128,2048]{1,0:T(8,128)(2,1)} %collective-permute-done.5.refs_2_), channel_id=1, source_target_pairs={{4,6},{2,0},{5,7},{3,1},{12,14},{10,8},{13,15},{11,9},{20,22},{18,... | collective-permute-start | bytes 1572872 | tf_op jit(solution)/shard_map/ppermute | solution.py:384
  75.1 1.7 %slice.17 = bf16[256,512]{1,0:T(8,128)(2,1)} slice(bf16[512,512]{1,0:T(8,128)(2,1)} %collective-permute-done.7.refs_10_), slice={[256:512], [0:512]} | slice | bytes 524288 | tf_op jit(solution)/shard_map/slice | solution.py:403
  76.8 1.7 %collective-permute-start.9 = (bf16[256,512]{1,0:T(8,128)(2,1)}, bf16[256,512]{1,0:T(8,128)(2,1)S(1)}, u32[]{:S(2)}, u32[]{:S(2)}) collective-permute-start(bf16[256,512]{1,0:T(8,128)(2,1)} %slice.17), channel_id=1, source_target_pairs={{0,8},{8,0},{16,24},{24,16},{1,9},{9,1},{17,25},{25,17},{2,10},{10... | collective-permute-start | bytes 786440 | tf_op jit(solution)/shard_map/ppermute | solution.py:403
  78.4 1.7 %slice.16 = bf16[256,512]{1,0:T(8,128)(2,1)} slice(bf16[512,512]{1,0:T(8,128)(2,1)} %collective-permute-done.6.refs_9_), slice={[0:256], [0:512]} | slice | bytes 524288 | tf_op jit(solution)/shard_map/slice | solution.py:402
  80.1 1.5 %collective-permute-start.8 = (bf16[256,512]{1,0:T(8,128)(2,1)}, bf16[256,512]{1,0:T(8,128)(2,1)}, u32[]{:S(2)}, u32[]{:S(2)}) collective-permute-start(bf16[256,512]{1,0:T(8,128)(2,1)} %slice.16), channel_id=1, source_target_pairs={{0,16},{16,0},{8,24},{24,8},{1,17},{17,1},{9,25},{25,9},{2,18},{18... | collective-permute-start | bytes 786440 | tf_op jit(solution)/shard_map/ppermute | solution.py:402
  81.6 1.1 copy-done.14
  82.7 0.9 copy-done.16
  83.7 6.5 %shard_map.98.refs_8_.refs_12_ = bf16[528,512]{1,0:T(8,128)(2,1)S(1)} custom-call(s32[3]{0:T(128)S(1)} %pad_add_fusion.pos_ref, f32[128,128]{1,0:T(8,128)S(1)} %copy-done.5, bf16[4,3,512,128]{3,2,1,0:T(8,128)(2,1)S(1)} %all-to-all-done.parts_ref, f32[384,512]{1,0:T(8,128)S(1)} %copy-done.14, bf16[4,384,512]{2,1,0:T(8,128)(2,1)S(1)} %all-to-all-done.1.refs_1_, ...), custom_call_target="tpu_custom_call" | custom-call | flops 13799999488 | tf_op jit(solution)/shard_map/pallas_call | solution.py:187
  90.3 0.5 collective-permute-start.11
  90.9 0.4 collective-permute-start.18
  91.4 1.8 %collective-permute-done.17.refs_16_ = bf16[256,512]{1,0:T(8,128)(2,1)S(1)} collective-permute-done((bf16[256,512]{1,0:T(8,128)(2,1)}, bf16[256,512]{1,0:T(8,128)(2,1)S(1)}, u32[]{:S(2)}, u32[]{:S(2)}) %collective-permute-start.17) | collective-permute-done | bytes 262176 | tf_op jit(solution)/shard_map/ppermute | solution.py:408
  93.2 0.1 collective-permute-start.13
  93.3 1.1 collective-permute-done.18.refs_17_
  94.5 0.1 collective-permute-start.14
  94.6 0.4 collective-permute-start.15
  95.0 0.1 collective-permute-start.16
  95.1 1.1 broadcast_select_fusion.refs_3_
  96.2 0.4 collective-permute-start.29
  96.7 0.6 collective-permute-start.26
  97.2 0.3 collective-permute-start.25
  97.6 0.5 collective-permute-done.16.refs_15_
  98.1 0.1 collective-permute-start.21
  98.2 0.2 copy-done.21
  98.4 0.5 copy-done.22
  98.9 14.3 %shard_map.99 = f32[2048,2048]{1,0:T(8,128)} custom-call(s32[3]{0:T(128)S(1)} %pad_add_fusion.pos_ref, bf16[128,2048]{1,0:T(8,128)(2,1)} %bitcast.3.refs_0_, bf16[128,2048]{1,0:T(8,128)(2,1)S(1)} %copy-done.12, bf16[128,2048]{1,0:T(8,128)(2,1)} %collective-permute-done.1.refs_2_, bf16[128,2048]{1,0:T(8,128)(2,1)S(1)} %copy-done.2, ...), custom_call_target="tpu_custom_call" | custom-call | flops 18400000000 | tf_op jit(solution)/shard_map/pallas_call | solution.py:286
  113.3 0.2 collective-permute-start.30
  113.5 0.4 collective-permute-start.31
  114.0 0.4 collective-permute-start.23
  114.4 2.6 %collective-permute-done.22.refs_5_ = bf16[128,2048]{1,0:T(8,128)(2,1)S(1)} collective-permute-done((bf16[128,2048]{1,0:T(8,128)(2,1)}, bf16[128,2048]{1,0:T(8,128)(2,1)S(1)}, u32[]{:S(2)}, u32[]{:S(2)}) %collective-permute-start.22) | collective-permute-done | bytes 524320 | tf_op jit(solution)/shard_map/ppermute | solution.py:408
  117.0 1.4 collective-permute-start.27
  118.3 1.5 %collective-permute-start.28 = (bf16[272,512]{1,0:T(8,128)(2,1)S(1)}, bf16[272,512]{1,0:T(8,128)(2,1)S(1)}, u32[]{:S(2)}, u32[]{:S(2)}) collective-permute-start(bf16[272,512]{1,0:T(8,128)(2,1)S(1)} %slice.15), channel_id=1, source_target_pairs={{0,8},{8,0},{16,24},{24,16},{1,9},{9,1},{17,25},{25,17},{2,10},{10... | collective-permute-start | bytes 835592 | tf_op jit(solution)/shard_map/ppermute | solution.py:403
  119.9 0.8 copy-done.18
  120.7 0.8 copy-done.19
  121.5 11.8 %shard_map.100.refs_20_ = f32[2048,2048]{1,0:T(8,128)} custom-call(s32[3]{0:T(128)S(1)} %pad_add_fusion.pos_ref, bf16[128,2048]{1,0:T(8,128)(2,1)S(1)} %bitcast.9, bf16[128,2048]{1,0:T(8,128)(2,1)} %collective-permute-done.4.refs_1_, bf16[128,2048]{1,0:T(8,128)(2,1)} %collective-permute-done.5.refs_2_, bf16[128,2048]{1,0:T(8,128)(2,1)S(1)} %broadcast_select_fusion.refs_3_, ...), custom_call_target="tpu_custom_call" | custom-call | flops 11500000256 | tf_op jit(solution)/shard_map/pallas_call | solution.py:362
  133.4 0.5 collective-permute-start.32
  133.9 1.4 %collective-permute-done.32.refs_10_ = bf16[256,512]{1,0:T(8,128)(2,1)S(1)} collective-permute-done((bf16[256,512]{1,0:T(8,128)(2,1)S(1)}, bf16[256,512]{1,0:T(8,128)(2,1)S(1)}, u32[]{:S(2)}, u32[]{:S(2)}) %collective-permute-start.32) | collective-permute-done | bytes 262176 | tf_op jit(solution)/shard_map/ppermute | solution.py:408
  135.3 6.3 %shard_map.101 = (f32[2048,2048]{1,0:T(8,128)}, f32[128,128]{1,0:T(8,128)}) custom-call(s32[3]{0:T(128)S(1)} %pad_add_fusion.pos_ref, bf16[128,2048]{1,0:T(8,128)(2,1)S(1)} %bitcast.10, bf16[128,2048]{1,0:T(8,128)(2,1)} %collective-permute-done.4.refs_1_, bf16[128,2048]{1,0:T(8,128)(2,1)} %collective-permute-done.5.refs_2_, ...), custom_call_target="tpu_custom_call", output_to_operand_aliasing={{0}: (21, {})} | custom-call | flops 11500000256 | tf_op jit(solution)/shard_map/pallas_call | solution.py:362
  (71 shorter events, 0.8 us)
Async XLA Ops:
  0.6 28.5 %collective-permute-start.1 = (bf16[128,2048]{1,0:T(8,128)(2,1)}, bf16[128,2048]{1,0:T(8,128)(2,1)}, u32[]{:S(2)}, u32[]{:S(2)}) collective-permute-start(bf16[128,2048]{1,0:T(8,128)(2,1)} %bitcast.3.refs_0_), channel_id=1, source_target_pairs={{0,4},{4,0},{2,6},{6,2},{1,5},{5,1},{3,7},{7,3},{8,12},{12,8},{10,... | collective-permute-start | bytes 1572872 | tf_op jit(solution)/shard_map/ppermute | solution.py:382
  4.7 25.6 %collective-permute-start = (bf16[128,2048]{1,0:T(8,128)(2,1)}, bf16[128,2048]{1,0:T(8,128)(2,1)S(1)}, u32[]{:S(2)}, u32[]{:S(2)}) collective-permute-start(bf16[128,2048]{1,0:T(8,128)(2,1)} %bitcast.3.refs_0_), channel_id=1, source_target_pairs={{0,2},{2,0},{4,6},{6,4},{1,3},{3,1},{5,7},{7,5},{8,10},{10,8},{12,... | collective-permute-start | bytes 1572872 | tf_op jit(solution)/shard_map/ppermute | solution.py:381
  6.3 1.0 copy-start.7
  7.4 1.0 copy-start.8
  8.4 1.0 copy-start.9
  11.0 28.4 %all-to-all-start = ((bf16[4,3,512,128]{3,2,1,0:T(8,128)(2,1)}), bf16[4,3,512,128]{3,2,1,0:T(8,128)(2,1)S(1)}, u32[]{:S(2)}, u32[]{:S(2)}) async-start(bf16[4,3,512,128]{3,2,1,0:T(8,128)(2,1)} %shard_map.96), calls=%async_computation | async-start | bytes 3145728 | tf_op jit(solution)/shard_map/all_to_all | solution.py:390
  14.8 28.7 %collective-permute-start.2 = (bf16[128,2048]{1,0:T(8,128)(2,1)}, bf16[128,2048]{1,0:T(8,128)(2,1)}, u32[]{:S(2)}, u32[]{:S(2)}) collective-permute-start(bf16[128,2048]{1,0:T(8,128)(2,1)} %bitcast.3.refs_0_), channel_id=1, source_target_pairs={{2,4},{4,2},{3,5},{5,3},{10,12},{12,10},{11,13},{13,11},{18,20},{2... | collective-permute-start | bytes 1572872 | tf_op jit(solution)/shard_map/ppermute | solution.py:383
  29.1 14.5 %collective-permute-start.3 = (bf16[128,2048]{1,0:T(8,128)(2,1)}, bf16[128,2048]{1,0:T(8,128)(2,1)}, u32[]{:S(2)}, u32[]{:S(2)}) collective-permute-start(bf16[128,2048]{1,0:T(8,128)(2,1)} %collective-permute-done.1.refs_2_), channel_id=1, source_target_pairs={{4,6},{2,0},{5,7},{3,1},{12,14},{10,8},{13,15},{11,9},{20,22},{18,... | collective-permute-start | bytes 1572872 | tf_op jit(solution)/shard_map/ppermute | solution.py:384
  30.4 7.0 %copy-start.11 = (bf16[128,2048]{1,0:T(8,128)(2,1)}, bf16[128,2048]{1,0:T(8,128)(2,1)S(1)}, u32[]{:S(2)}) copy-start(bf16[128,2048]{1,0:T(8,128)(2,1)S(1)} %collective-permute-done.refs_1_) | copy-start | bytes 1572868
  37.4 1.1 copy-start
  38.5 0.9 copy-start.13
  39.4 22.7 %all-to-all-start.1 = ((bf16[4,384,512]{2,1,0:T(8,128)(2,1)}), bf16[4,384,512]{2,1,0:T(8,128)(2,1)S(1)}, u32[]{:S(2)}, u32[]{:S(2)}) async-start(bf16[4,384,512]{2,1,0:T(8,128)(2,1)} %copy-done), calls=%async_computation.1 | async-start | bytes 3145728 | tf_op jit(solution)/shard_map/all_to_all | solution.py:390
  44.7 9.4 %copy-start.1 = (bf16[128,2048]{1,0:T(8,128)(2,1)}, bf16[128,2048]{1,0:T(8,128)(2,1)S(1)}, u32[]{:S(2)}) copy-start(bf16[128,2048]{1,0:T(8,128)(2,1)S(1)} %broadcast_select_fusion.1.refs_0_.refs_3_) | copy-start | bytes 1572868
  44.7 10.2 %copy-start.5 = (f32[128,128]{1,0:T(8,128)S(1)}, f32[128,128]{1,0:T(8,128)}, u32[]{:S(2)}) copy-start(f32[128,128]{1,0:T(8,128)} %f_ref.3) | copy-start | bytes 196612
  44.7 27.1 %collective-permute-start.5 = (bf16[128,2048]{1,0:T(8,128)(2,1)}, bf16[128,2048]{1,0:T(8,128)(2,1)}, u32[]{:S(2)}, u32[]{:S(2)}) collective-permute-start(bf16[128,2048]{1,0:T(8,128)(2,1)} %bitcast.5), channel_id=1, source_target_pairs={{0,4},{4,0},{2,6},{6,2},{1,5},{5,1},{3,7},{7,3},{8,12},{12,8},{10,... | collective-permute-start | bytes 1572872 | tf_op jit(solution)/shard_map/ppermute | solution.py:382
  49.1 24.5 %collective-permute-start.4 = (bf16[128,2048]{1,0:T(8,128)(2,1)}, bf16[128,2048]{1,0:T(8,128)(2,1)}, u32[]{:S(2)}, u32[]{:S(2)}) collective-permute-start(bf16[128,2048]{1,0:T(8,128)(2,1)} %bitcast.6), channel_id=1, source_target_pairs={{0,2},{2,0},{4,6},{6,4},{1,3},{3,1},{5,7},{7,5},{8,10},{10,8},{12,... | collective-permute-start | bytes 1572872 | tf_op jit(solution)/shard_map/ppermute | solution.py:381
  54.1 0.8 copy-start.3
  54.9 4.8 %copy-start.15 = (f32[128,512]{1,0:T(8,128)}, f32[128,512]{1,0:T(8,128)S(1)}, u32[]{:S(2)}) copy-start(f32[128,512]{1,0:T(8,128)S(1)} %get-tuple-element.35.refs_2_) | copy-start | bytes 786436
  58.2 16.9 %collective-permute-start.7 = (bf16[512,512]{1,0:T(8,128)(2,1)}, bf16[512,512]{1,0:T(8,128)(2,1)}, u32[]{:S(2)}, u32[]{:S(2)}) collective-permute-start(bf16[512,512]{1,0:T(8,128)(2,1)} %shard_map.97.refs_8_), channel_id=1, source_target_pairs={{0,16},{16,0},{8,24},{24,8},{1,17},{17,1},{9,25},{25,9},{2,18},{18... | collective-permute-start | bytes 1572872 | tf_op jit(solution)/shard_map/ppermute | solution.py:395
  59.7 18.7 %collective-permute-start.6 = (bf16[512,512]{1,0:T(8,128)(2,1)}, bf16[512,512]{1,0:T(8,128)(2,1)}, u32[]{:S(2)}, u32[]{:S(2)}) collective-permute-start(bf16[512,512]{1,0:T(8,128)(2,1)} %shard_map.97.refs_8_), channel_id=1, source_target_pairs={{0,8},{8,0},{16,24},{24,16},{1,9},{9,1},{17,25},{25,17},{2,10},{10... | collective-permute-start | bytes 1572872 | tf_op jit(solution)/shard_map/ppermute | solution.py:394
  62.1 19.4 %all-to-all-start.2 = ((bf16[4,128,512]{2,1,0:T(8,128)(2,1)}), bf16[4,128,512]{2,1,0:T(8,128)(2,1)}, u32[]{:S(2)}, u32[]{:S(2)}) async-start(bf16[4,128,512]{2,1,0:T(8,128)(2,1)} %copy-done.3), calls=%async_computation.2 | async-start | bytes 1048576 | tf_op jit(solution)/shard_map/all_to_all | solution.py:390
  66.3 24.6 %collective-permute-start.19 = (bf16[128,2048]{1,0:T(8,128)(2,1)}, bf16[128,2048]{1,0:T(8,128)(2,1)}, u32[]{:S(2)}, u32[]{:S(2)}) collective-permute-start(bf16[128,2048]{1,0:T(8,128)(2,1)} %bitcast.7), channel_id=1, source_target_pairs={{2,4},{4,2},{3,5},{5,3},{10,12},{12,10},{11,13},{13,11},{18,20},{2... | collective-permute-start | bytes 1572872 | tf_op jit(solution)/shard_map/ppermute | solution.py:383
  73.6 17.8 %collective-permute-start.20 = (bf16[128,2048]{1,0:T(8,128)(2,1)}, bf16[128,2048]{1,0:T(8,128)(2,1)}, u32[]{:S(2)}, u32[]{:S(2)}) collective-permute-start(bf16[128,2048]{1,0:T(8,128)(2,1)} %collective-permute-done.5.refs_2_), channel_id=1, source_target_pairs={{4,6},{2,0},{5,7},{3,1},{12,14},{10,8},{13,15},{11,9},{20,22},{18,... | collective-permute-start | bytes 1572872 | tf_op jit(solution)/shard_map/ppermute | solution.py:384
  76.8 13.5 %collective-permute-start.9 = (bf16[256,512]{1,0:T(8,128)(2,1)}, bf16[256,512]{1,0:T(8,128)(2,1)S(1)}, u32[]{:S(2)}, u32[]{:S(2)}) collective-permute-start(bf16[256,512]{1,0:T(8,128)(2,1)} %slice.17), channel_id=1, source_target_pairs={{0,8},{8,0},{16,24},{24,16},{1,9},{9,1},{17,25},{25,17},{2,10},{10... | collective-permute-start | bytes 786440 | tf_op jit(solution)/shard_map/ppermute | solution.py:403
  80.1 10.1 %collective-permute-start.8 = (bf16[256,512]{1,0:T(8,128)(2,1)}, bf16[256,512]{1,0:T(8,128)(2,1)}, u32[]{:S(2)}, u32[]{:S(2)}) collective-permute-start(bf16[256,512]{1,0:T(8,128)(2,1)} %slice.16), channel_id=1, source_target_pairs={{0,16},{16,0},{8,24},{24,8},{1,17},{17,1},{9,25},{25,9},{2,18},{18... | collective-permute-start | bytes 786440 | tf_op jit(solution)/shard_map/ppermute | solution.py:402
  81.6 1.1 copy-start.14
  82.7 0.9 copy-start.16
  83.7 6.7 %copy-start.12 = (bf16[128,2048]{1,0:T(8,128)(2,1)S(1)}, bf16[128,2048]{1,0:T(8,128)(2,1)}, u32[]{:S(2)}) copy-start(bf16[128,2048]{1,0:T(8,128)(2,1)} %copy-done.11) | copy-start | bytes 1572868
  83.7 9.5 %copy-start.2 = (bf16[128,2048]{1,0:T(8,128)(2,1)S(1)}, bf16[128,2048]{1,0:T(8,128)(2,1)}, u32[]{:S(2)}) copy-start(bf16[128,2048]{1,0:T(8,128)(2,1)} %copy-done.1) | copy-start | bytes 1572868
  83.7 14.4 %copy-start.10 = (bf16[1,128,2048]{2,1,0:T(8,128)(2,1)S(1)}, bf16[1,128,2048]{2,1,0:T(8,128)(2,1)}, u32[]{:S(2)}) copy-start(bf16[1,128,2048]{2,1,0:T(8,128)(2,1)} %param.8) | copy-start | bytes 1572868
  90.2 4.4 %collective-permute-start.10 = (bf16[128,2048]{1,0:T(8,128)(2,1)}, bf16[128,2048]{1,0:T(8,128)(2,1)S(1)}, u32[]{:S(2)}, u32[]{:S(2)}) collective-permute-start(bf16[128,2048]{1,0:T(8,128)(2,1)} %bitcast.3.refs_0_), channel_id=1, source_target_pairs={{0,1},{1,0},{2,3},{3,2},{4,5},{5,4},{6,7},{7,6},{8,9},{9,8},{10,11... | collective-permute-start | bytes 1572872 | tf_op jit(solution)/shard_map/ppermute | solution.py:408
  90.3 4.7 %collective-permute-start.11 = (bf16[128,2048]{1,0:T(8,128)(2,1)S(1)}, bf16[128,2048]{1,0:T(8,128)(2,1)S(1)}, u32[]{:S(2)}, u32[]{:S(2)}) collective-permute-start(bf16[128,2048]{1,0:T(8,128)(2,1)S(1)} %copy-done.12), channel_id=1, source_target_pairs={{0,1},{1,0},{2,3},{3,2},{4,5},{5,4},{6,7},{7,6},{8,9},{9,8},{10,11... | collective-permute-start | bytes 1572872 | tf_op jit(solution)/shard_map/ppermute | solution.py:408
  90.8 2.4 %collective-permute-start.17 = (bf16[256,512]{1,0:T(8,128)(2,1)}, bf16[256,512]{1,0:T(8,128)(2,1)S(1)}, u32[]{:S(2)}, u32[]{:S(2)}) collective-permute-start(bf16[256,512]{1,0:T(8,128)(2,1)} %collective-permute-done.8.refs_11_), channel_id=1, source_target_pairs={{0,1},{1,0},{2,3},{3,2},{4,5},{5,4},{6,7},{7,6},{8,9},{9,8},{10,11... | collective-permute-start | bytes 786440 | tf_op jit(solution)/shard_map/ppermute | solution.py:408
  90.9 3.6 %collective-permute-start.18 = (bf16[256,512]{1,0:T(8,128)(2,1)S(1)}, bf16[256,512]{1,0:T(8,128)(2,1)S(1)}, u32[]{:S(2)}, u32[]{:S(2)}) collective-permute-start(bf16[256,512]{1,0:T(8,128)(2,1)S(1)} %collective-permute-done.9.refs_12_), channel_id=1, source_target_pairs={{0,1},{1,0},{2,3},{3,2},{4,5},{5,4},{6,7},{7,6},{8,9},{9,8},{10,11... | collective-permute-start | bytes 786440 | tf_op jit(solution)/shard_map/ppermute | solution.py:408
  91.3 4.9 %collective-permute-start.12 = (bf16[128,2048]{1,0:T(8,128)(2,1)}, bf16[128,2048]{1,0:T(8,128)(2,1)S(1)}, u32[]{:S(2)}, u32[]{:S(2)}) collective-permute-start(bf16[128,2048]{1,0:T(8,128)(2,1)} %collective-permute-done.1.refs_2_), channel_id=1, source_target_pairs={{0,1},{1,0},{2,3},{3,2},{4,5},{5,4},{6,7},{7,6},{8,9},{9,8},{10,11... | collective-permute-start | bytes 1572872 | tf_op jit(solution)/shard_map/ppermute | solution.py:408
  93.2 3.5 %collective-permute-start.13 = (bf16[128,2048]{1,0:T(8,128)(2,1)S(1)}, bf16[128,2048]{1,0:T(8,128)(2,1)S(1)}, u32[]{:S(2)}, u32[]{:S(2)}) collective-permute-start(bf16[128,2048]{1,0:T(8,128)(2,1)S(1)} %copy-done.2), channel_id=1, source_target_pairs={{0,1},{1,0},{2,3},{3,2},{4,5},{5,4},{6,7},{7,6},{8,9},{9,8},{10,11... | collective-permute-start | bytes 1572872 | tf_op jit(solution)/shard_map/ppermute | solution.py:408
  94.5 2.8 %collective-permute-start.14 = (bf16[512,512]{1,0:T(8,128)(2,1)}, bf16[512,512]{1,0:T(8,128)(2,1)S(1)}, u32[]{:S(2)}, u32[]{:S(2)}) collective-permute-start(bf16[512,512]{1,0:T(8,128)(2,1)} %shard_map.97.refs_8_), channel_id=1, source_target_pairs={{0,1},{1,0},{2,3},{3,2},{4,5},{5,4},{6,7},{7,6},{8,9},{9,8},{10,11... | collective-permute-start | bytes 1572872 | tf_op jit(solution)/shard_map/ppermute | solution.py:408
  94.6 3.0 %collective-permute-start.15 = (bf16[512,512]{1,0:T(8,128)(2,1)}, bf16[512,512]{1,0:T(8,128)(2,1)S(1)}, u32[]{:S(2)}, u32[]{:S(2)}) collective-permute-start(bf16[512,512]{1,0:T(8,128)(2,1)} %collective-permute-done.6.refs_9_), channel_id=1, source_target_pairs={{0,1},{1,0},{2,3},{3,2},{4,5},{5,4},{6,7},{7,6},{8,9},{9,8},{10,11... | collective-permute-start | bytes 1572872 | tf_op jit(solution)/shard_map/ppermute | solution.py:408
  95.0 3.1 %collective-permute-start.16 = (bf16[512,512]{1,0:T(8,128)(2,1)}, bf16[512,512]{1,0:T(8,128)(2,1)S(1)}, u32[]{:S(2)}, u32[]{:S(2)}) collective-permute-start(bf16[512,512]{1,0:T(8,128)(2,1)} %collective-permute-done.7.refs_10_), channel_id=1, source_target_pairs={{0,1},{1,0},{2,3},{3,2},{4,5},{5,4},{6,7},{7,6},{8,9},{9,8},{10,11... | collective-permute-start | bytes 1572872 | tf_op jit(solution)/shard_map/ppermute | solution.py:408
  96.2 23.6 %collective-permute-start.29 = (bf16[528,512]{1,0:T(8,128)(2,1)S(1)}, bf16[528,512]{1,0:T(8,128)(2,1)S(1)}, u32[]{:S(2)}, u32[]{:S(2)}) collective-permute-start(bf16[528,512]{1,0:T(8,128)(2,1)S(1)} %shard_map.98.refs_8_.refs_12_), channel_id=1, source_target_pairs={{0,1},{1,0},{2,3},{3,2},{4,5},{5,4},{6,7},{7,6},{8,9},{9,8},{10,11... | collective-permute-start | bytes 1622024 | tf_op jit(solution)/shard_map/ppermute | solution.py:408
  96.7 16.5 %collective-permute-start.26 = (bf16[528,512]{1,0:T(8,128)(2,1)S(1)}, bf16[528,512]{1,0:T(8,128)(2,1)S(1)}, u32[]{:S(2)}, u32[]{:S(2)}) collective-permute-start(bf16[528,512]{1,0:T(8,128)(2,1)S(1)} %shard_map.98.refs_8_.refs_12_), channel_id=1, source_target_pairs={{0,16},{16,0},{8,24},{24,8},{1,17},{17,1},{9,25},{25,9},{2,18},{18... | collective-permute-start | bytes 1622024 | tf_op jit(solution)/shard_map/ppermute | solution.py:395
  97.2 1.0 copy-start.20
  97.2 16.0 %collective-permute-start.25 = (bf16[528,512]{1,0:T(8,128)(2,1)S(1)}, bf16[528,512]{1,0:T(8,128)(2,1)S(1)}, u32[]{:S(2)}, u32[]{:S(2)}) collective-permute-start(bf16[528,512]{1,0:T(8,128)(2,1)S(1)} %shard_map.98.refs_8_.refs_12_), channel_id=1, source_target_pairs={{0,8},{8,0},{16,24},{24,16},{1,9},{9,1},{17,25},{25,17},{2,10},{10... | collective-permute-start | bytes 1622024 | tf_op jit(solution)/shard_map/ppermute | solution.py:394
  97.6 0.8 copy-start.21
  97.6 16.2 %collective-permute-start.24 = (bf16[128,2048]{1,0:T(8,128)(2,1)S(1)}, bf16[128,2048]{1,0:T(8,128)(2,1)S(1)}, u32[]{:S(2)}, u32[]{:S(2)}) collective-permute-start(bf16[128,2048]{1,0:T(8,128)(2,1)S(1)} %broadcast_select_fusion.refs_3_), channel_id=1, source_target_pairs={{0,1},{1,0},{2,3},{3,2},{4,5},{5,4},{6,7},{7,6},{8,9},{9,8},{10,11... | collective-permute-start | bytes 1572872 | tf_op jit(solution)/shard_map/ppermute | solution.py:408
  98.1 0.8 copy-start.22
  98.1 15.9 %collective-permute-start.21 = (bf16[128,2048]{1,0:T(8,128)(2,1)S(1)}, bf16[128,2048]{1,0:T(8,128)(2,1)S(1)}, u32[]{:S(2)}, u32[]{:S(2)}) collective-permute-start(bf16[128,2048]{1,0:T(8,128)(2,1)S(1)} %bitcast.8), channel_id=1, source_target_pairs={{0,1},{1,0},{2,3},{3,2},{4,5},{5,4},{6,7},{7,6},{8,9},{9,8},{10,11... | collective-permute-start | bytes 1572872 | tf_op jit(solution)/shard_map/ppermute | solution.py:408
  113.2 6.6 %copy-start.17 = (bf16[528,512]{1,0:T(8,128)(2,1)}, bf16[528,512]{1,0:T(8,128)(2,1)S(1)}, u32[]{:S(2)}) copy-start(bf16[528,512]{1,0:T(8,128)(2,1)S(1)} %collective-permute-done.26.refs_12_.refs_14_) | copy-start | bytes 1622020
  113.2 20.0 %copy-start.4 = (bf16[528,512]{1,0:T(8,128)(2,1)}, bf16[528,512]{1,0:T(8,128)(2,1)S(1)}, u32[]{:S(2)}) copy-start(bf16[528,512]{1,0:T(8,128)(2,1)S(1)} %collective-permute-done.25.refs_10_.refs_13_) | copy-start | bytes 1622020
  113.3 6.6 %collective-permute-start.30 = (bf16[528,512]{1,0:T(8,128)(2,1)S(1)}, bf16[528,512]{1,0:T(8,128)(2,1)S(1)}, u32[]{:S(2)}, u32[]{:S(2)}) collective-permute-start(bf16[528,512]{1,0:T(8,128)(2,1)S(1)} %collective-permute-done.25.refs_10_.refs_13_), channel_id=1, source_target_pairs={{0,1},{1,0},{2,3},{3,2},{4,5},{5,4},{6,7},{7,6},{8,9},{9,8},{10,11... | collective-permute-start | bytes 1622024 | tf_op jit(solution)/shard_map/ppermute | solution.py:408
  113.5 6.4 %collective-permute-start.31 = (bf16[528,512]{1,0:T(8,128)(2,1)S(1)}, bf16[528,512]{1,0:T(8,128)(2,1)S(1)}, u32[]{:S(2)}, u32[]{:S(2)}) collective-permute-start(bf16[528,512]{1,0:T(8,128)(2,1)S(1)} %collective-permute-done.26.refs_12_.refs_14_), channel_id=1, source_target_pairs={{0,1},{1,0},{2,3},{3,2},{4,5},{5,4},{6,7},{7,6},{8,9},{9,8},{10,11... | collective-permute-start | bytes 1622024 | tf_op jit(solution)/shard_map/ppermute | solution.py:408
  113.8 3.1 %collective-permute-start.22 = (bf16[128,2048]{1,0:T(8,128)(2,1)}, bf16[128,2048]{1,0:T(8,128)(2,1)S(1)}, u32[]{:S(2)}, u32[]{:S(2)}) collective-permute-start(bf16[128,2048]{1,0:T(8,128)(2,1)} %collective-permute-done.4.refs_1_), channel_id=1, source_target_pairs={{0,1},{1,0},{2,3},{3,2},{4,5},{5,4},{6,7},{7,6},{8,9},{9,8},{10,11... | collective-permute-start | bytes 1572872 | tf_op jit(solution)/shard_map/ppermute | solution.py:408
  114.0 4.4 %collective-permute-start.23 = (bf16[128,2048]{1,0:T(8,128)(2,1)}, bf16[128,2048]{1,0:T(8,128)(2,1)S(1)}, u32[]{:S(2)}, u32[]{:S(2)}) collective-permute-start(bf16[128,2048]{1,0:T(8,128)(2,1)} %collective-permute-done.5.refs_2_), channel_id=1, source_target_pairs={{0,1},{1,0},{2,3},{3,2},{4,5},{5,4},{6,7},{7,6},{8,9},{9,8},{10,11... | collective-permute-start | bytes 1572872 | tf_op jit(solution)/shard_map/ppermute | solution.py:408
  117.0 16.4 %collective-permute-start.27 = (bf16[256,512]{1,0:T(8,128)(2,1)S(1)}, bf16[256,512]{1,0:T(8,128)(2,1)S(1)}, u32[]{:S(2)}, u32[]{:S(2)}) collective-permute-start(bf16[256,512]{1,0:T(8,128)(2,1)S(1)} %slice.14), channel_id=1, source_target_pairs={{0,16},{16,0},{8,24},{24,8},{1,17},{17,1},{9,25},{25,9},{2,18},{18... | collective-permute-start | bytes 786440 | tf_op jit(solution)/shard_map/ppermute | solution.py:402
  118.3 14.9 %collective-permute-start.28 = (bf16[272,512]{1,0:T(8,128)(2,1)S(1)}, bf16[272,512]{1,0:T(8,128)(2,1)S(1)}, u32[]{:S(2)}, u32[]{:S(2)}) collective-permute-start(bf16[272,512]{1,0:T(8,128)(2,1)S(1)} %slice.15), channel_id=1, source_target_pairs={{0,8},{8,0},{16,24},{24,16},{1,9},{9,1},{17,25},{25,17},{2,10},{10... | collective-permute-start | bytes 835592 | tf_op jit(solution)/shard_map/ppermute | solution.py:403
  119.8 13.4 %copy-start.6 = (bf16[528,512]{1,0:T(8,128)(2,1)}, bf16[528,512]{1,0:T(8,128)(2,1)S(1)}, u32[]{:S(2)}) copy-start(bf16[528,512]{1,0:T(8,128)(2,1)S(1)} %collective-permute-done.29.refs_9_.refs_16_) | copy-start | bytes 1622020
  119.8 0.8 copy-start.18
  120.7 0.8 copy-start.19
  133.3 2.0 %collective-permute-start.33 = (bf16[272,512]{1,0:T(8,128)(2,1)S(1)}, bf16[272,512]{1,0:T(8,128)(2,1)S(1)}, u32[]{:S(2)}, u32[]{:S(2)}) collective-permute-start(bf16[272,512]{1,0:T(8,128)(2,1)S(1)} %collective-permute-done.28.refs_9_.refs_15_), channel_id=1, source_target_pairs={{0,1},{1,0},{2,3},{3,2},{4,5},{5,4},{6,7},{7,6},{8,9},{9,8},{10,11... | collective-permute-start | bytes 835592 | tf_op jit(solution)/shard_map/ppermute | solution.py:408
  133.4 1.9 %collective-permute-start.32 = (bf16[256,512]{1,0:T(8,128)(2,1)S(1)}, bf16[256,512]{1,0:T(8,128)(2,1)S(1)}, u32[]{:S(2)}, u32[]{:S(2)}) collective-permute-start(bf16[256,512]{1,0:T(8,128)(2,1)S(1)} %collective-permute-done.27.refs_8_), channel_id=1, source_target_pairs={{0,1},{1,0},{2,3},{3,2},{4,5},{5,4},{6,7},{7,6},{8,9},{9,8},{10,11... | collective-permute-start | bytes 786440 | tf_op jit(solution)/shard_map/ppermute | solution.py:408

commit v6 on v5

--- a/solution.py
+++ b/solution.py
@@ -87,7 +87,7 @@
             gt[rows, b * n : (b + 1) * n] = gate * conv[b * size : (b + 1) * size]
         return carry
 
-    lax.fori_loop(0, groups, one, 0, unroll=16)
+    lax.fori_loop(0, groups, one, 0, unroll=32)
     for b in range(blocks):
         out_ref[b * n : (b + 1) * n, :] = gt[:, b * n : (b + 1) * n].T.astype(bf16)
 
@@ -171,7 +171,7 @@
         sums[pl.ds(pl.multiple_of(g * 8, 8), 8), :] = ring
         return carry
 
-    lax.fori_loop(0, groups, one, 0, unroll=16)
+    lax.fori_loop(0, groups, one, 0, unroll=32)
     total = sums[pl.ds(0, groups, stride=8), :]
     for i in range(1, 8):
         total = total + pltpu.roll(sums[pl.ds(i, groups, stride=8), :], n - i, 1)

time: 143 us -> 143 us (level)
  transfers between devices with their start and end apart: 37 -> 37, of which waited for: 10 -> 10; matrix products, arithmetic and copies ran while one was open for 4% -> 4% of each run, Pallas kernels for 35% -> 34%
where the time goes in v6:
time: 143 us; the launch traced here: 141 us
  Pallas kernels  54.7 us (38%)
  starting transfers between devices  42.2 us (30%)
  waiting for transfers between devices  27.1 us (19%)
  local copies, waits for them, and re-layouts  13.7 us (10%)
  other arithmetic  2.27 us (2%)
    pallas_call x2, Pallas kernels, value_part(): pl.pallas_call(functools.partial(value_kernel, n, width, which, layout, w...  18.1 us
    ppermute x2, waiting for transfers between devices, line_slots(): second = lax.ppermute(x, 'col', far)  16.8 us
    pallas_call x1, Pallas kernels, out_gradient(): pl.pallas_call(functools.partial(out_kernel, n, layout), out_shape=jax.Sh...  14.4 us
    all_to_all x3, starting transfers between devices, swap_rows(): return lax.all_to_all(x, 'row', split_axis=0, concat_axis=0, tiled=True)  11.9 us
    pallas_call x2, Pallas kernels, project(): pl.pallas_call(functools.partial(project_kernel, len(slots)), out_shape=[...  11.5 us
    unnamed x46, local copies, waits for them, and re-layouts  10.3 us
    ppermute x2, starting transfers between devices, line_slots(): second = lax.ppermute(x, 'col', far)  8.49 us
    ppermute x18, waiting for transfers between devices, other_core(): return [lax.ppermute(x, 'dp', swap) for x in xs]  7.41 us
  transfers between devices with their start and end apart: 37, of which 10 were waited for; matrix products, arithmetic and copies ran while one was open for 4% of the time, Pallas kernels for 34%

profile of v6, /device:TPU:0, one launch (start us, length us, event | category | flops | bytes accessed | tf_op | source)
XLA Modules:
  0.0 141.2 jit_solution(14611897352172087835)
XLA Ops:
  0.6 4.1 %collective-permute-start.1 = (bf16[128,2048]{1,0:T(8,128)(2,1)}, bf16[128,2048]{1,0:T(8,128)(2,1)}, u32[]{:S(2)}, u32[]{:S(2)}) collective-permute-start(bf16[128,2048]{1,0:T(8,128)(2,1)} %bitcast.3.refs_0_), channel_id=1, source_target_pairs={{0,4},{4,0},{2,6},{6,2},{1,5},{5,1},{3,7},{7,3},{8,12},{12,8},{10,... | collective-permute-start | bytes 1572872 | tf_op jit(solution)/shard_map/ppermute | solution.py:382
  4.7 1.6 %collective-permute-start = (bf16[128,2048]{1,0:T(8,128)(2,1)}, bf16[128,2048]{1,0:T(8,128)(2,1)S(1)}, u32[]{:S(2)}, u32[]{:S(2)}) collective-permute-start(bf16[128,2048]{1,0:T(8,128)(2,1)} %bitcast.3.refs_0_), channel_id=1, source_target_pairs={{0,2},{2,0},{4,6},{6,4},{1,3},{3,1},{5,7},{7,5},{8,10},{10,8},{12,... | collective-permute-start | bytes 1572872 | tf_op jit(solution)/shard_map/ppermute | solution.py:381
  6.3 1.0 copy-done.7
  7.4 1.0 copy-done.8
  8.4 1.0 copy-done.9
  9.4 1.6 %shard_map.96 = bf16[4,3,512,128]{3,2,1,0:T(8,128)(2,1)} custom-call(bf16[1,128,2048]{2,1,0:T(8,128)(2,1)S(1)} %copy-done.7, bf16[1,128,2048]{2,1,0:T(8,128)(2,1)S(1)} %copy-done.8, bf16[1,128,2048]{2,1,0:T(8,128)(2,1)S(1)} %copy-done.9), custom_call_target="tpu_custom_call" | custom-call | flops 3449999872 | tf_op jit(solution)/shard_map/pallas_call | solution.py:41
  11.0 3.7 %all-to-all-start = ((bf16[4,3,512,128]{3,2,1,0:T(8,128)(2,1)}), bf16[4,3,512,128]{3,2,1,0:T(8,128)(2,1)S(1)}, u32[]{:S(2)}, u32[]{:S(2)}) async-start(bf16[4,3,512,128]{3,2,1,0:T(8,128)(2,1)} %shard_map.96), calls=%async_computation | async-start | bytes 3145728 | tf_op jit(solution)/shard_map/all_to_all | solution.py:390
  14.8 1.5 %collective-permute-start.2 = (bf16[128,2048]{1,0:T(8,128)(2,1)}, bf16[128,2048]{1,0:T(8,128)(2,1)}, u32[]{:S(2)}, u32[]{:S(2)}) collective-permute-start(bf16[128,2048]{1,0:T(8,128)(2,1)} %bitcast.3.refs_0_), channel_id=1, source_target_pairs={{2,4},{4,2},{3,5},{5,3},{10,12},{12,10},{11,13},{13,11},{18,20},{2... | collective-permute-start | bytes 1572872 | tf_op jit(solution)/shard_map/ppermute | solution.py:383
  16.3 12.8 %collective-permute-done.1.refs_2_ = bf16[128,2048]{1,0:T(8,128)(2,1)} collective-permute-done((bf16[128,2048]{1,0:T(8,128)(2,1)}, bf16[128,2048]{1,0:T(8,128)(2,1)}, u32[]{:S(2)}, u32[]{:S(2)}) %collective-permute-start.1) | collective-permute-done | bytes 524320 | tf_op jit(solution)/shard_map/ppermute | solution.py:382
  29.1 1.3 collective-permute-start.3
  30.4 7.0 %shard_map.94 = (f32[384,512]{1,0:T(8,128)S(1)}, bf16[4,384,512]{2,1,0:T(8,128)(2,1)S(1)}) custom-call(s32[3]{0:T(128)S(1)} %pad_add_fusion.pos_ref, bf16[128,2048]{1,0:T(8,128)(2,1)} %bitcast.3.refs_0_, bf16[128,2048]{1,0:T(8,128)(2,1)S(1)} %collective-permute-done.refs_1_, bf16[128,2048]{1,0:T(8,128)(2,1)} %collective-permute-done.1.refs_2_, ...), custom_call_target="tpu_custom_call" | custom-call | flops 9200000000 | tf_op jit(solution)/shard_map/pallas_call | solution.py:224
  37.4 1.1 copy-done
  38.5 0.9 copy-done.13
  39.4 4.1 %all-to-all-start.1 = ((bf16[4,384,512]{2,1,0:T(8,128)(2,1)}), bf16[4,384,512]{2,1,0:T(8,128)(2,1)S(1)}, u32[]{:S(2)}, u32[]{:S(2)}) async-start(bf16[4,384,512]{2,1,0:T(8,128)(2,1)} %copy-done), calls=%async_computation.1 | async-start | bytes 3145728 | tf_op jit(solution)/shard_map/all_to_all | solution.py:390
  43.6 1.1 broadcast_select_fusion.1.refs_0_.refs_3_
  44.7 4.4 %collective-permute-start.5 = (bf16[128,2048]{1,0:T(8,128)(2,1)}, bf16[128,2048]{1,0:T(8,128)(2,1)}, u32[]{:S(2)}, u32[]{:S(2)}) collective-permute-start(bf16[128,2048]{1,0:T(8,128)(2,1)} %bitcast.5), channel_id=1, source_target_pairs={{0,4},{4,0},{2,6},{6,2},{1,5},{5,1},{3,7},{7,3},{8,12},{12,8},{10,... | collective-permute-start | bytes 1572872 | tf_op jit(solution)/shard_map/ppermute | solution.py:382
  49.1 0.5 collective-permute-start.4
  49.5 4.5 %shard_map.95 = (f32[128,512]{1,0:T(8,128)S(1)}, bf16[4,128,512]{2,1,0:T(8,128)(2,1)S(1)}) custom-call(s32[3]{0:T(128)S(1)} %pad_add_fusion.pos_ref, bf16[128,2048]{1,0:T(8,128)(2,1)S(1)} %broadcast_select_fusion.1.refs_0_.refs_3_, bf16[2048,2048]{1,0:T(8,128)(2,1)} %refs_1_.1), custom_call_target="tpu_custom_call" | custom-call | flops 9200000000 | tf_op jit(solution)/shard_map/pallas_call | solution.py:224
  54.1 0.8 copy-done.3
  54.9 3.3 %shard_map.97.refs_8_ = bf16[512,512]{1,0:T(8,128)(2,1)} custom-call(s32[3]{0:T(128)S(1)} %pad_add_fusion.pos_ref, f32[128,128]{1,0:T(8,128)S(1)} %copy-done.5, bf16[4,3,512,128]{3,2,1,0:T(8,128)(2,1)S(1)} %all-to-all-done.parts_ref), custom_call_target="tpu_custom_call" | custom-call | tf_op jit(solution)/shard_map/pallas_call | solution.py:98
  58.1 1.5 %collective-permute-start.7 = (bf16[512,512]{1,0:T(8,128)(2,1)}, bf16[512,512]{1,0:T(8,128)(2,1)}, u32[]{:S(2)}, u32[]{:S(2)}) collective-permute-start(bf16[512,512]{1,0:T(8,128)(2,1)} %shard_map.97.refs_8_), channel_id=1, source_target_pairs={{0,16},{16,0},{8,24},{24,8},{1,17},{17,1},{9,25},{25,9},{2,18},{18... | collective-permute-start | bytes 1572872 | tf_op jit(solution)/shard_map/ppermute | solution.py:395
  59.7 1.5 %collective-permute-start.6 = (bf16[512,512]{1,0:T(8,128)(2,1)}, bf16[512,512]{1,0:T(8,128)(2,1)}, u32[]{:S(2)}, u32[]{:S(2)}) collective-permute-start(bf16[512,512]{1,0:T(8,128)(2,1)} %shard_map.97.refs_8_), channel_id=1, source_target_pairs={{0,8},{8,0},{16,24},{24,16},{1,9},{9,1},{17,25},{25,17},{2,10},{10... | collective-permute-start | bytes 1572872 | tf_op jit(solution)/shard_map/ppermute | solution.py:394
  61.2 1.0 all-to-all-done.1.refs_1_
  62.1 4.1 %all-to-all-start.2 = ((bf16[4,128,512]{2,1,0:T(8,128)(2,1)}), bf16[4,128,512]{2,1,0:T(8,128)(2,1)}, u32[]{:S(2)}, u32[]{:S(2)}) async-start(bf16[4,128,512]{2,1,0:T(8,128)(2,1)} %copy-done.3), calls=%async_computation.2 | async-start | bytes 1048576 | tf_op jit(solution)/shard_map/all_to_all | solution.py:390
  66.3 1.5 %collective-permute-start.19 = (bf16[128,2048]{1,0:T(8,128)(2,1)}, bf16[128,2048]{1,0:T(8,128)(2,1)}, u32[]{:S(2)}, u32[]{:S(2)}) collective-permute-start(bf16[128,2048]{1,0:T(8,128)(2,1)} %bitcast.7), channel_id=1, source_target_pairs={{2,4},{4,2},{3,5},{5,3},{10,12},{12,10},{11,13},{13,11},{18,20},{2... | collective-permute-start | bytes 1572872 | tf_op jit(solution)/shard_map/ppermute | solution.py:383
  67.8 4.0 %collective-permute-done.5.refs_2_ = bf16[128,2048]{1,0:T(8,128)(2,1)} collective-permute-done((bf16[128,2048]{1,0:T(8,128)(2,1)}, bf16[128,2048]{1,0:T(8,128)(2,1)}, u32[]{:S(2)}, u32[]{:S(2)}) %collective-permute-start.5) | collective-permute-done | bytes 524320 | tf_op jit(solution)/shard_map/ppermute | solution.py:382
  71.8 1.8 %collective-permute-done.4.refs_1_ = bf16[128,2048]{1,0:T(8,128)(2,1)} collective-permute-done((bf16[128,2048]{1,0:T(8,128)(2,1)}, bf16[128,2048]{1,0:T(8,128)(2,1)}, u32[]{:S(2)}, u32[]{:S(2)}) %collective-permute-start.4) | collective-permute-done | bytes 524320 | tf_op jit(solution)/shard_map/ppermute | solution.py:381
  73.6 1.5 %collective-permute-start.20 = (bf16[128,2048]{1,0:T(8,128)(2,1)}, bf16[128,2048]{1,0:T(8,128)(2,1)}, u32[]{:S(2)}, u32[]{:S(2)}) collective-permute-start(bf16[128,2048]{1,0:T(8,128)(2,1)} %collective-permute-done.5.refs_2_), channel_id=1, source_target_pairs={{4,6},{2,0},{5,7},{3,1},{12,14},{10,8},{13,15},{11,9},{20,22},{18,... | collective-permute-start | bytes 1572872 | tf_op jit(solution)/shard_map/ppermute | solution.py:384
  75.1 1.7 %slice.17 = bf16[256,512]{1,0:T(8,128)(2,1)} slice(bf16[512,512]{1,0:T(8,128)(2,1)} %collective-permute-done.7.refs_10_), slice={[256:512], [0:512]} | slice | bytes 524288 | tf_op jit(solution)/shard_map/slice | solution.py:403
  76.8 1.7 %collective-permute-start.9 = (bf16[256,512]{1,0:T(8,128)(2,1)}, bf16[256,512]{1,0:T(8,128)(2,1)S(1)}, u32[]{:S(2)}, u32[]{:S(2)}) collective-permute-start(bf16[256,512]{1,0:T(8,128)(2,1)} %slice.17), channel_id=1, source_target_pairs={{0,8},{8,0},{16,24},{24,16},{1,9},{9,1},{17,25},{25,17},{2,10},{10... | collective-permute-start | bytes 786440 | tf_op jit(solution)/shard_map/ppermute | solution.py:403
  78.4 1.7 %slice.16 = bf16[256,512]{1,0:T(8,128)(2,1)} slice(bf16[512,512]{1,0:T(8,128)(2,1)} %collective-permute-done.6.refs_9_), slice={[0:256], [0:512]} | slice | bytes 524288 | tf_op jit(solution)/shard_map/slice | solution.py:402
  80.1 1.5 %collective-permute-start.8 = (bf16[256,512]{1,0:T(8,128)(2,1)}, bf16[256,512]{1,0:T(8,128)(2,1)}, u32[]{:S(2)}, u32[]{:S(2)}) collective-permute-start(bf16[256,512]{1,0:T(8,128)(2,1)} %slice.16), channel_id=1, source_target_pairs={{0,16},{16,0},{8,24},{24,8},{1,17},{17,1},{9,25},{25,9},{2,18},{18... | collective-permute-start | bytes 786440 | tf_op jit(solution)/shard_map/ppermute | solution.py:402
  81.6 1.1 copy-done.14
  82.7 0.9 copy-done.16
  83.7 5.8 %shard_map.98.refs_8_.refs_12_ = bf16[528,512]{1,0:T(8,128)(2,1)S(1)} custom-call(s32[3]{0:T(128)S(1)} %pad_add_fusion.pos_ref, f32[128,128]{1,0:T(8,128)S(1)} %copy-done.5, bf16[4,3,512,128]{3,2,1,0:T(8,128)(2,1)S(1)} %all-to-all-done.parts_ref, f32[384,512]{1,0:T(8,128)S(1)} %copy-done.14, bf16[4,384,512]{2,1,0:T(8,128)(2,1)S(1)} %all-to-all-done.1.refs_1_, ...), custom_call_target="tpu_custom_call" | custom-call | flops 13799999488 | tf_op jit(solution)/shard_map/pallas_call | solution.py:187
  89.6 0.5 collective-permute-start.11
  90.2 0.4 collective-permute-start.18
  90.7 1.8 %collective-permute-done.17.refs_16_ = bf16[256,512]{1,0:T(8,128)(2,1)S(1)} collective-permute-done((bf16[256,512]{1,0:T(8,128)(2,1)}, bf16[256,512]{1,0:T(8,128)(2,1)S(1)}, u32[]{:S(2)}, u32[]{:S(2)}) %collective-permute-start.17) | collective-permute-done | bytes 262176 | tf_op jit(solution)/shard_map/ppermute | solution.py:408
  92.5 0.1 collective-permute-start.13
  92.6 1.1 collective-permute-done.18.refs_17_
  93.7 0.1 collective-permute-start.14
  93.9 0.4 collective-permute-start.15
  94.3 0.1 collective-permute-start.16
  94.4 1.1 broadcast_select_fusion.refs_3_
  95.5 0.4 collective-permute-start.29
  96.0 0.6 collective-permute-start.26
  96.5 0.3 collective-permute-start.25
  96.9 0.5 collective-permute-done.16.refs_15_
  97.4 0.1 collective-permute-start.21
  97.5 0.2 copy-done.21
  97.7 0.5 copy-done.22
  98.2 14.4 %shard_map.99 = f32[2048,2048]{1,0:T(8,128)} custom-call(s32[3]{0:T(128)S(1)} %pad_add_fusion.pos_ref, bf16[128,2048]{1,0:T(8,128)(2,1)} %bitcast.3.refs_0_, bf16[128,2048]{1,0:T(8,128)(2,1)S(1)} %copy-done.12, bf16[128,2048]{1,0:T(8,128)(2,1)} %collective-permute-done.1.refs_2_, bf16[128,2048]{1,0:T(8,128)(2,1)S(1)} %copy-done.2, ...), custom_call_target="tpu_custom_call" | custom-call | flops 18400000000 | tf_op jit(solution)/shard_map/pallas_call | solution.py:286
  112.7 0.2 collective-permute-start.30
  112.9 0.4 collective-permute-start.31
  113.4 0.4 collective-permute-start.23
  113.8 2.6 %collective-permute-done.22.refs_5_ = bf16[128,2048]{1,0:T(8,128)(2,1)S(1)} collective-permute-done((bf16[128,2048]{1,0:T(8,128)(2,1)}, bf16[128,2048]{1,0:T(8,128)(2,1)S(1)}, u32[]{:S(2)}, u32[]{:S(2)}) %collective-permute-start.22) | collective-permute-done | bytes 524320 | tf_op jit(solution)/shard_map/ppermute | solution.py:408
  116.4 1.3 collective-permute-start.27
  117.7 1.5 %collective-permute-start.28 = (bf16[272,512]{1,0:T(8,128)(2,1)S(1)}, bf16[272,512]{1,0:T(8,128)(2,1)S(1)}, u32[]{:S(2)}, u32[]{:S(2)}) collective-permute-start(bf16[272,512]{1,0:T(8,128)(2,1)S(1)} %slice.15), channel_id=1, source_target_pairs={{0,8},{8,0},{16,24},{24,16},{1,9},{9,1},{17,25},{25,17},{2,10},{10... | collective-permute-start | bytes 835592 | tf_op jit(solution)/shard_map/ppermute | solution.py:403
  119.3 0.8 copy-done.18
  120.1 0.8 copy-done.19
  120.9 11.8 %shard_map.100.refs_20_ = f32[2048,2048]{1,0:T(8,128)} custom-call(s32[3]{0:T(128)S(1)} %pad_add_fusion.pos_ref, bf16[128,2048]{1,0:T(8,128)(2,1)S(1)} %bitcast.9, bf16[128,2048]{1,0:T(8,128)(2,1)} %collective-permute-done.4.refs_1_, bf16[128,2048]{1,0:T(8,128)(2,1)} %collective-permute-done.5.refs_2_, bf16[128,2048]{1,0:T(8,128)(2,1)S(1)} %broadcast_select_fusion.refs_3_, ...), custom_call_target="tpu_custom_call" | custom-call | flops 11500000256 | tf_op jit(solution)/shard_map/pallas_call | solution.py:362
  132.8 0.5 collective-permute-start.32
  133.3 1.4 %collective-permute-done.32.refs_10_ = bf16[256,512]{1,0:T(8,128)(2,1)S(1)} collective-permute-done((bf16[256,512]{1,0:T(8,128)(2,1)S(1)}, bf16[256,512]{1,0:T(8,128)(2,1)S(1)}, u32[]{:S(2)}, u32[]{:S(2)}) %collective-permute-start.32) | collective-permute-done | bytes 262176 | tf_op jit(solution)/shard_map/ppermute | solution.py:408
  134.7 6.3 %shard_map.101 = (f32[2048,2048]{1,0:T(8,128)}, f32[128,128]{1,0:T(8,128)}) custom-call(s32[3]{0:T(128)S(1)} %pad_add_fusion.pos_ref, bf16[128,2048]{1,0:T(8,128)(2,1)S(1)} %bitcast.10, bf16[128,2048]{1,0:T(8,128)(2,1)} %collective-permute-done.4.refs_1_, bf16[128,2048]{1,0:T(8,128)(2,1)} %collective-permute-done.5.refs_2_, ...), custom_call_target="tpu_custom_call", output_to_operand_aliasing={{0}: (21, {})} | custom-call | flops 11500000256 | tf_op jit(solution)/shard_map/pallas_call | solution.py:362
  (71 shorter events, 0.8 us)
Async XLA Ops:
  0.6 28.5 %collective-permute-start.1 = (bf16[128,2048]{1,0:T(8,128)(2,1)}, bf16[128,2048]{1,0:T(8,128)(2,1)}, u32[]{:S(2)}, u32[]{:S(2)}) collective-permute-start(bf16[128,2048]{1,0:T(8,128)(2,1)} %bitcast.3.refs_0_), channel_id=1, source_target_pairs={{0,4},{4,0},{2,6},{6,2},{1,5},{5,1},{3,7},{7,3},{8,12},{12,8},{10,... | collective-permute-start | bytes 1572872 | tf_op jit(solution)/shard_map/ppermute | solution.py:382
  4.7 25.6 %collective-permute-start = (bf16[128,2048]{1,0:T(8,128)(2,1)}, bf16[128,2048]{1,0:T(8,128)(2,1)S(1)}, u32[]{:S(2)}, u32[]{:S(2)}) collective-permute-start(bf16[128,2048]{1,0:T(8,128)(2,1)} %bitcast.3.refs_0_), channel_id=1, source_target_pairs={{0,2},{2,0},{4,6},{6,4},{1,3},{3,1},{5,7},{7,5},{8,10},{10,8},{12,... | collective-permute-start | bytes 1572872 | tf_op jit(solution)/shard_map/ppermute | solution.py:381
  6.3 1.0 copy-start.7
  7.4 1.0 copy-start.8
  8.4 1.0 copy-start.9
  11.0 28.4 %all-to-all-start = ((bf16[4,3,512,128]{3,2,1,0:T(8,128)(2,1)}), bf16[4,3,512,128]{3,2,1,0:T(8,128)(2,1)S(1)}, u32[]{:S(2)}, u32[]{:S(2)}) async-start(bf16[4,3,512,128]{3,2,1,0:T(8,128)(2,1)} %shard_map.96), calls=%async_computation | async-start | bytes 3145728 | tf_op jit(solution)/shard_map/all_to_all | solution.py:390
  14.8 28.7 %collective-permute-start.2 = (bf16[128,2048]{1,0:T(8,128)(2,1)}, bf16[128,2048]{1,0:T(8,128)(2,1)}, u32[]{:S(2)}, u32[]{:S(2)}) collective-permute-start(bf16[128,2048]{1,0:T(8,128)(2,1)} %bitcast.3.refs_0_), channel_id=1, source_target_pairs={{2,4},{4,2},{3,5},{5,3},{10,12},{12,10},{11,13},{13,11},{18,20},{2... | collective-permute-start | bytes 1572872 | tf_op jit(solution)/shard_map/ppermute | solution.py:383
  29.1 14.5 %collective-permute-start.3 = (bf16[128,2048]{1,0:T(8,128)(2,1)}, bf16[128,2048]{1,0:T(8,128)(2,1)}, u32[]{:S(2)}, u32[]{:S(2)}) collective-permute-start(bf16[128,2048]{1,0:T(8,128)(2,1)} %collective-permute-done.1.refs_2_), channel_id=1, source_target_pairs={{4,6},{2,0},{5,7},{3,1},{12,14},{10,8},{13,15},{11,9},{20,22},{18,... | collective-permute-start | bytes 1572872 | tf_op jit(solution)/shard_map/ppermute | solution.py:384
  30.4 7.0 %copy-start.11 = (bf16[128,2048]{1,0:T(8,128)(2,1)}, bf16[128,2048]{1,0:T(8,128)(2,1)S(1)}, u32[]{:S(2)}) copy-start(bf16[128,2048]{1,0:T(8,128)(2,1)S(1)} %collective-permute-done.refs_1_) | copy-start | bytes 1572868
  37.4 1.1 copy-start
  38.5 0.9 copy-start.13
  39.4 22.7 %all-to-all-start.1 = ((bf16[4,384,512]{2,1,0:T(8,128)(2,1)}), bf16[4,384,512]{2,1,0:T(8,128)(2,1)S(1)}, u32[]{:S(2)}, u32[]{:S(2)}) async-start(bf16[4,384,512]{2,1,0:T(8,128)(2,1)} %copy-done), calls=%async_computation.1 | async-start | bytes 3145728 | tf_op jit(solution)/shard_map/all_to_all | solution.py:390
  44.7 9.4 %copy-start.1 = (bf16[128,2048]{1,0:T(8,128)(2,1)}, bf16[128,2048]{1,0:T(8,128)(2,1)S(1)}, u32[]{:S(2)}) copy-start(bf16[128,2048]{1,0:T(8,128)(2,1)S(1)} %broadcast_select_fusion.1.refs_0_.refs_3_) | copy-start | bytes 1572868
  44.7 10.2 %copy-start.5 = (f32[128,128]{1,0:T(8,128)S(1)}, f32[128,128]{1,0:T(8,128)}, u32[]{:S(2)}) copy-start(f32[128,128]{1,0:T(8,128)} %f_ref.3) | copy-start | bytes 196612
  44.7 27.1 %collective-permute-start.5 = (bf16[128,2048]{1,0:T(8,128)(2,1)}, bf16[128,2048]{1,0:T(8,128)(2,1)}, u32[]{:S(2)}, u32[]{:S(2)}) collective-permute-start(bf16[128,2048]{1,0:T(8,128)(2,1)} %bitcast.5), channel_id=1, source_target_pairs={{0,4},{4,0},{2,6},{6,2},{1,5},{5,1},{3,7},{7,3},{8,12},{12,8},{10,... | collective-permute-start | bytes 1572872 | tf_op jit(solution)/shard_map/ppermute | solution.py:382
  49.1 24.5 %collective-permute-start.4 = (bf16[128,2048]{1,0:T(8,128)(2,1)}, bf16[128,2048]{1,0:T(8,128)(2,1)}, u32[]{:S(2)}, u32[]{:S(2)}) collective-permute-start(bf16[128,2048]{1,0:T(8,128)(2,1)} %bitcast.6), channel_id=1, source_target_pairs={{0,2},{2,0},{4,6},{6,4},{1,3},{3,1},{5,7},{7,5},{8,10},{10,8},{12,... | collective-permute-start | bytes 1572872 | tf_op jit(solution)/shard_map/ppermute | solution.py:381
  54.1 0.8 copy-start.3
  54.9 4.8 %copy-start.15 = (f32[128,512]{1,0:T(8,128)}, f32[128,512]{1,0:T(8,128)S(1)}, u32[]{:S(2)}) copy-start(f32[128,512]{1,0:T(8,128)S(1)} %get-tuple-element.35.refs_2_) | copy-start | bytes 786436
  58.1 16.9 %collective-permute-start.7 = (bf16[512,512]{1,0:T(8,128)(2,1)}, bf16[512,512]{1,0:T(8,128)(2,1)}, u32[]{:S(2)}, u32[]{:S(2)}) collective-permute-start(bf16[512,512]{1,0:T(8,128)(2,1)} %shard_map.97.refs_8_), channel_id=1, source_target_pairs={{0,16},{16,0},{8,24},{24,8},{1,17},{17,1},{9,25},{25,9},{2,18},{18... | collective-permute-start | bytes 1572872 | tf_op jit(solution)/shard_map/ppermute | solution.py:395
  59.7 18.7 %collective-permute-start.6 = (bf16[512,512]{1,0:T(8,128)(2,1)}, bf16[512,512]{1,0:T(8,128)(2,1)}, u32[]{:S(2)}, u32[]{:S(2)}) collective-permute-start(bf16[512,512]{1,0:T(8,128)(2,1)} %shard_map.97.refs_8_), channel_id=1, source_target_pairs={{0,8},{8,0},{16,24},{24,16},{1,9},{9,1},{17,25},{25,17},{2,10},{10... | collective-permute-start | bytes 1572872 | tf_op jit(solution)/shard_map/ppermute | solution.py:394
  62.1 19.4 %all-to-all-start.2 = ((bf16[4,128,512]{2,1,0:T(8,128)(2,1)}), bf16[4,128,512]{2,1,0:T(8,128)(2,1)}, u32[]{:S(2)}, u32[]{:S(2)}) async-start(bf16[4,128,512]{2,1,0:T(8,128)(2,1)} %copy-done.3), calls=%async_computation.2 | async-start | bytes 1048576 | tf_op jit(solution)/shard_map/all_to_all | solution.py:390
  66.3 23.9 %collective-permute-start.19 = (bf16[128,2048]{1,0:T(8,128)(2,1)}, bf16[128,2048]{1,0:T(8,128)(2,1)}, u32[]{:S(2)}, u32[]{:S(2)}) collective-permute-start(bf16[128,2048]{1,0:T(8,128)(2,1)} %bitcast.7), channel_id=1, source_target_pairs={{2,4},{4,2},{3,5},{5,3},{10,12},{12,10},{11,13},{13,11},{18,20},{2... | collective-permute-start | bytes 1572872 | tf_op jit(solution)/shard_map/ppermute | solution.py:383
  73.6 17.0 %collective-permute-start.20 = (bf16[128,2048]{1,0:T(8,128)(2,1)}, bf16[128,2048]{1,0:T(8,128)(2,1)}, u32[]{:S(2)}, u32[]{:S(2)}) collective-permute-start(bf16[128,2048]{1,0:T(8,128)(2,1)} %collective-permute-done.5.refs_2_), channel_id=1, source_target_pairs={{4,6},{2,0},{5,7},{3,1},{12,14},{10,8},{13,15},{11,9},{20,22},{18,... | collective-permute-start | bytes 1572872 | tf_op jit(solution)/shard_map/ppermute | solution.py:384
  76.8 12.7 %collective-permute-start.9 = (bf16[256,512]{1,0:T(8,128)(2,1)}, bf16[256,512]{1,0:T(8,128)(2,1)S(1)}, u32[]{:S(2)}, u32[]{:S(2)}) collective-permute-start(bf16[256,512]{1,0:T(8,128)(2,1)} %slice.17), channel_id=1, source_target_pairs={{0,8},{8,0},{16,24},{24,16},{1,9},{9,1},{17,25},{25,17},{2,10},{10... | collective-permute-start | bytes 786440 | tf_op jit(solution)/shard_map/ppermute | solution.py:403
  80.1 9.4 %collective-permute-start.8 = (bf16[256,512]{1,0:T(8,128)(2,1)}, bf16[256,512]{1,0:T(8,128)(2,1)}, u32[]{:S(2)}, u32[]{:S(2)}) collective-permute-start(bf16[256,512]{1,0:T(8,128)(2,1)} %slice.16), channel_id=1, source_target_pairs={{0,16},{16,0},{8,24},{24,8},{1,17},{17,1},{9,25},{25,9},{2,18},{18... | collective-permute-start | bytes 786440 | tf_op jit(solution)/shard_map/ppermute | solution.py:402
  81.6 1.1 copy-start.14
  82.7 0.9 copy-start.16
  83.7 5.9 %copy-start.12 = (bf16[128,2048]{1,0:T(8,128)(2,1)S(1)}, bf16[128,2048]{1,0:T(8,128)(2,1)}, u32[]{:S(2)}) copy-start(bf16[128,2048]{1,0:T(8,128)(2,1)} %copy-done.11) | copy-start | bytes 1572868
  83.7 8.8 %copy-start.2 = (bf16[128,2048]{1,0:T(8,128)(2,1)S(1)}, bf16[128,2048]{1,0:T(8,128)(2,1)}, u32[]{:S(2)}) copy-start(bf16[128,2048]{1,0:T(8,128)(2,1)} %copy-done.1) | copy-start | bytes 1572868
  83.7 13.7 %copy-start.10 = (bf16[1,128,2048]{2,1,0:T(8,128)(2,1)S(1)}, bf16[1,128,2048]{2,1,0:T(8,128)(2,1)}, u32[]{:S(2)}) copy-start(bf16[1,128,2048]{2,1,0:T(8,128)(2,1)} %param.8) | copy-start | bytes 1572868
  89.5 4.4 %collective-permute-start.10 = (bf16[128,2048]{1,0:T(8,128)(2,1)}, bf16[128,2048]{1,0:T(8,128)(2,1)S(1)}, u32[]{:S(2)}, u32[]{:S(2)}) collective-permute-start(bf16[128,2048]{1,0:T(8,128)(2,1)} %bitcast.3.refs_0_), channel_id=1, source_target_pairs={{0,1},{1,0},{2,3},{3,2},{4,5},{5,4},{6,7},{7,6},{8,9},{9,8},{10,11... | collective-permute-start | bytes 1572872 | tf_op jit(solution)/shard_map/ppermute | solution.py:408
  89.6 4.7 %collective-permute-start.11 = (bf16[128,2048]{1,0:T(8,128)(2,1)S(1)}, bf16[128,2048]{1,0:T(8,128)(2,1)S(1)}, u32[]{:S(2)}, u32[]{:S(2)}) collective-permute-start(bf16[128,2048]{1,0:T(8,128)(2,1)S(1)} %copy-done.12), channel_id=1, source_target_pairs={{0,1},{1,0},{2,3},{3,2},{4,5},{5,4},{6,7},{7,6},{8,9},{9,8},{10,11... | collective-permute-start | bytes 1572872 | tf_op jit(solution)/shard_map/ppermute | solution.py:408
  90.1 2.4 %collective-permute-start.17 = (bf16[256,512]{1,0:T(8,128)(2,1)}, bf16[256,512]{1,0:T(8,128)(2,1)S(1)}, u32[]{:S(2)}, u32[]{:S(2)}) collective-permute-start(bf16[256,512]{1,0:T(8,128)(2,1)} %collective-permute-done.8.refs_11_), channel_id=1, source_target_pairs={{0,1},{1,0},{2,3},{3,2},{4,5},{5,4},{6,7},{7,6},{8,9},{9,8},{10,11... | collective-permute-start | bytes 786440 | tf_op jit(solution)/shard_map/ppermute | solution.py:408
  90.2 3.6 %collective-permute-start.18 = (bf16[256,512]{1,0:T(8,128)(2,1)S(1)}, bf16[256,512]{1,0:T(8,128)(2,1)S(1)}, u32[]{:S(2)}, u32[]{:S(2)}) collective-permute-start(bf16[256,512]{1,0:T(8,128)(2,1)S(1)} %collective-permute-done.9.refs_12_), channel_id=1, source_target_pairs={{0,1},{1,0},{2,3},{3,2},{4,5},{5,4},{6,7},{7,6},{8,9},{9,8},{10,11... | collective-permute-start | bytes 786440 | tf_op jit(solution)/shard_map/ppermute | solution.py:408
  90.6 4.9 %collective-permute-start.12 = (bf16[128,2048]{1,0:T(8,128)(2,1)}, bf16[128,2048]{1,0:T(8,128)(2,1)S(1)}, u32[]{:S(2)}, u32[]{:S(2)}) collective-permute-start(bf16[128,2048]{1,0:T(8,128)(2,1)} %collective-permute-done.1.refs_2_), channel_id=1, source_target_pairs={{0,1},{1,0},{2,3},{3,2},{4,5},{5,4},{6,7},{7,6},{8,9},{9,8},{10,11... | collective-permute-start | bytes 1572872 | tf_op jit(solution)/shard_map/ppermute | solution.py:408
  92.5 3.5 %collective-permute-start.13 = (bf16[128,2048]{1,0:T(8,128)(2,1)S(1)}, bf16[128,2048]{1,0:T(8,128)(2,1)S(1)}, u32[]{:S(2)}, u32[]{:S(2)}) collective-permute-start(bf16[128,2048]{1,0:T(8,128)(2,1)S(1)} %copy-done.2), channel_id=1, source_target_pairs={{0,1},{1,0},{2,3},{3,2},{4,5},{5,4},{6,7},{7,6},{8,9},{9,8},{10,11... | collective-permute-start | bytes 1572872 | tf_op jit(solution)/shard_map/ppermute | solution.py:408
  93.7 2.8 %collective-permute-start.14 = (bf16[512,512]{1,0:T(8,128)(2,1)}, bf16[512,512]{1,0:T(8,128)(2,1)S(1)}, u32[]{:S(2)}, u32[]{:S(2)}) collective-permute-start(bf16[512,512]{1,0:T(8,128)(2,1)} %shard_map.97.refs_8_), channel_id=1, source_target_pairs={{0,1},{1,0},{2,3},{3,2},{4,5},{5,4},{6,7},{7,6},{8,9},{9,8},{10,11... | collective-permute-start | bytes 1572872 | tf_op jit(solution)/shard_map/ppermute | solution.py:408
  93.9 3.0 %collective-permute-start.15 = (bf16[512,512]{1,0:T(8,128)(2,1)}, bf16[512,512]{1,0:T(8,128)(2,1)S(1)}, u32[]{:S(2)}, u32[]{:S(2)}) collective-permute-start(bf16[512,512]{1,0:T(8,128)(2,1)} %collective-permute-done.6.refs_9_), channel_id=1, source_target_pairs={{0,1},{1,0},{2,3},{3,2},{4,5},{5,4},{6,7},{7,6},{8,9},{9,8},{10,11... | collective-permute-start | bytes 1572872 | tf_op jit(solution)/shard_map/ppermute | solution.py:408
  94.3 3.1 %collective-permute-start.16 = (bf16[512,512]{1,0:T(8,128)(2,1)}, bf16[512,512]{1,0:T(8,128)(2,1)S(1)}, u32[]{:S(2)}, u32[]{:S(2)}) collective-permute-start(bf16[512,512]{1,0:T(8,128)(2,1)} %collective-permute-done.7.refs_10_), channel_id=1, source_target_pairs={{0,1},{1,0},{2,3},{3,2},{4,5},{5,4},{6,7},{7,6},{8,9},{9,8},{10,11... | collective-permute-start | bytes 1572872 | tf_op jit(solution)/shard_map/ppermute | solution.py:408
  95.5 23.7 %collective-permute-start.29 = (bf16[528,512]{1,0:T(8,128)(2,1)S(1)}, bf16[528,512]{1,0:T(8,128)(2,1)S(1)}, u32[]{:S(2)}, u32[]{:S(2)}) collective-permute-start(bf16[528,512]{1,0:T(8,128)(2,1)S(1)} %shard_map.98.refs_8_.refs_12_), channel_id=1, source_target_pairs={{0,1},{1,0},{2,3},{3,2},{4,5},{5,4},{6,7},{7,6},{8,9},{9,8},{10,11... | collective-permute-start | bytes 1622024 | tf_op jit(solution)/shard_map/ppermute | solution.py:408
  96.0 16.7 %collective-permute-start.26 = (bf16[528,512]{1,0:T(8,128)(2,1)S(1)}, bf16[528,512]{1,0:T(8,128)(2,1)S(1)}, u32[]{:S(2)}, u32[]{:S(2)}) collective-permute-start(bf16[528,512]{1,0:T(8,128)(2,1)S(1)} %shard_map.98.refs_8_.refs_12_), channel_id=1, source_target_pairs={{0,16},{16,0},{8,24},{24,8},{1,17},{17,1},{9,25},{25,9},{2,18},{18... | collective-permute-start | bytes 1622024 | tf_op jit(solution)/shard_map/ppermute | solution.py:395
  96.5 1.0 copy-start.20
  96.5 16.1 %collective-permute-start.25 = (bf16[528,512]{1,0:T(8,128)(2,1)S(1)}, bf16[528,512]{1,0:T(8,128)(2,1)S(1)}, u32[]{:S(2)}, u32[]{:S(2)}) collective-permute-start(bf16[528,512]{1,0:T(8,128)(2,1)S(1)} %shard_map.98.refs_8_.refs_12_), channel_id=1, source_target_pairs={{0,8},{8,0},{16,24},{24,16},{1,9},{9,1},{17,25},{25,17},{2,10},{10... | collective-permute-start | bytes 1622024 | tf_op jit(solution)/shard_map/ppermute | solution.py:394
  96.9 0.8 copy-start.21
  96.9 16.4 %collective-permute-start.24 = (bf16[128,2048]{1,0:T(8,128)(2,1)S(1)}, bf16[128,2048]{1,0:T(8,128)(2,1)S(1)}, u32[]{:S(2)}, u32[]{:S(2)}) collective-permute-start(bf16[128,2048]{1,0:T(8,128)(2,1)S(1)} %broadcast_select_fusion.refs_3_), channel_id=1, source_target_pairs={{0,1},{1,0},{2,3},{3,2},{4,5},{5,4},{6,7},{7,6},{8,9},{9,8},{10,11... | collective-permute-start | bytes 1572872 | tf_op jit(solution)/shard_map/ppermute | solution.py:408
  97.4 0.8 copy-start.22
  97.4 16.0 %collective-permute-start.21 = (bf16[128,2048]{1,0:T(8,128)(2,1)S(1)}, bf16[128,2048]{1,0:T(8,128)(2,1)S(1)}, u32[]{:S(2)}, u32[]{:S(2)}) collective-permute-start(bf16[128,2048]{1,0:T(8,128)(2,1)S(1)} %bitcast.8), channel_id=1, source_target_pairs={{0,1},{1,0},{2,3},{3,2},{4,5},{5,4},{6,7},{7,6},{8,9},{9,8},{10,11... | collective-permute-start | bytes 1572872 | tf_op jit(solution)/shard_map/ppermute | solution.py:408
  112.6 6.6 %copy-start.17 = (bf16[528,512]{1,0:T(8,128)(2,1)}, bf16[528,512]{1,0:T(8,128)(2,1)S(1)}, u32[]{:S(2)}) copy-start(bf16[528,512]{1,0:T(8,128)(2,1)S(1)} %collective-permute-done.26.refs_12_.refs_14_) | copy-start | bytes 1622020
  112.7 20.0 %copy-start.4 = (bf16[528,512]{1,0:T(8,128)(2,1)}, bf16[528,512]{1,0:T(8,128)(2,1)S(1)}, u32[]{:S(2)}) copy-start(bf16[528,512]{1,0:T(8,128)(2,1)S(1)} %collective-permute-done.25.refs_10_.refs_13_) | copy-start | bytes 1622020
  112.7 6.6 %collective-permute-start.30 = (bf16[528,512]{1,0:T(8,128)(2,1)S(1)}, bf16[528,512]{1,0:T(8,128)(2,1)S(1)}, u32[]{:S(2)}, u32[]{:S(2)}) collective-permute-start(bf16[528,512]{1,0:T(8,128)(2,1)S(1)} %collective-permute-done.25.refs_10_.refs_13_), channel_id=1, source_target_pairs={{0,1},{1,0},{2,3},{3,2},{4,5},{5,4},{6,7},{7,6},{8,9},{9,8},{10,11... | collective-permute-start | bytes 1622024 | tf_op jit(solution)/shard_map/ppermute | solution.py:408
  112.9 6.4 %collective-permute-start.31 = (bf16[528,512]{1,0:T(8,128)(2,1)S(1)}, bf16[528,512]{1,0:T(8,128)(2,1)S(1)}, u32[]{:S(2)}, u32[]{:S(2)}) collective-permute-start(bf16[528,512]{1,0:T(8,128)(2,1)S(1)} %collective-permute-done.26.refs_12_.refs_14_), channel_id=1, source_target_pairs={{0,1},{1,0},{2,3},{3,2},{4,5},{5,4},{6,7},{7,6},{8,9},{9,8},{10,11... | collective-permute-start | bytes 1622024 | tf_op jit(solution)/shard_map/ppermute | solution.py:408
  113.3 3.1 %collective-permute-start.22 = (bf16[128,2048]{1,0:T(8,128)(2,1)}, bf16[128,2048]{1,0:T(8,128)(2,1)S(1)}, u32[]{:S(2)}, u32[]{:S(2)}) collective-permute-start(bf16[128,2048]{1,0:T(8,128)(2,1)} %collective-permute-done.4.refs_1_), channel_id=1, source_target_pairs={{0,1},{1,0},{2,3},{3,2},{4,5},{5,4},{6,7},{7,6},{8,9},{9,8},{10,11... | collective-permute-start | bytes 1572872 | tf_op jit(solution)/shard_map/ppermute | solution.py:408
  113.4 4.3 %collective-permute-start.23 = (bf16[128,2048]{1,0:T(8,128)(2,1)}, bf16[128,2048]{1,0:T(8,128)(2,1)S(1)}, u32[]{:S(2)}, u32[]{:S(2)}) collective-permute-start(bf16[128,2048]{1,0:T(8,128)(2,1)} %collective-permute-done.5.refs_2_), channel_id=1, source_target_pairs={{0,1},{1,0},{2,3},{3,2},{4,5},{5,4},{6,7},{7,6},{8,9},{9,8},{10,11... | collective-permute-start | bytes 1572872 | tf_op jit(solution)/shard_map/ppermute | solution.py:408
  116.4 16.4 %collective-permute-start.27 = (bf16[256,512]{1,0:T(8,128)(2,1)S(1)}, bf16[256,512]{1,0:T(8,128)(2,1)S(1)}, u32[]{:S(2)}, u32[]{:S(2)}) collective-permute-start(bf16[256,512]{1,0:T(8,128)(2,1)S(1)} %slice.14), channel_id=1, source_target_pairs={{0,16},{16,0},{8,24},{24,8},{1,17},{17,1},{9,25},{25,9},{2,18},{18... | collective-permute-start | bytes 786440 | tf_op jit(solution)/shard_map/ppermute | solution.py:402
  117.7 15.0 %collective-permute-start.28 = (bf16[272,512]{1,0:T(8,128)(2,1)S(1)}, bf16[272,512]{1,0:T(8,128)(2,1)S(1)}, u32[]{:S(2)}, u32[]{:S(2)}) collective-permute-start(bf16[272,512]{1,0:T(8,128)(2,1)S(1)} %slice.15), channel_id=1, source_target_pairs={{0,8},{8,0},{16,24},{24,16},{1,9},{9,1},{17,25},{25,17},{2,10},{10... | collective-permute-start | bytes 835592 | tf_op jit(solution)/shard_map/ppermute | solution.py:403
  119.3 13.5 %copy-start.6 = (bf16[528,512]{1,0:T(8,128)(2,1)}, bf16[528,512]{1,0:T(8,128)(2,1)S(1)}, u32[]{:S(2)}) copy-start(bf16[528,512]{1,0:T(8,128)(2,1)S(1)} %collective-permute-done.29.refs_9_.refs_16_) | copy-start | bytes 1622020
  119.3 0.8 copy-start.18
  120.1 0.8 copy-start.19
  132.7 2.0 %collective-permute-start.33 = (bf16[272,512]{1,0:T(8,128)(2,1)S(1)}, bf16[272,512]{1,0:T(8,128)(2,1)S(1)}, u32[]{:S(2)}, u32[]{:S(2)}) collective-permute-start(bf16[272,512]{1,0:T(8,128)(2,1)S(1)} %collective-permute-done.28.refs_9_.refs_15_), channel_id=1, source_target_pairs={{0,1},{1,0},{2,3},{3,2},{4,5},{5,4},{6,7},{7,6},{8,9},{9,8},{10,11... | collective-permute-start | bytes 835592 | tf_op jit(solution)/shard_map/ppermute | solution.py:408
  132.8 1.9 %collective-permute-start.32 = (bf16[256,512]{1,0:T(8,128)(2,1)S(1)}, bf16[256,512]{1,0:T(8,128)(2,1)S(1)}, u32[]{:S(2)}, u32[]{:S(2)}) collective-permute-start(bf16[256,512]{1,0:T(8,128)(2,1)S(1)} %collective-permute-done.27.refs_8_), channel_id=1, source_target_pairs={{0,1},{1,0},{2,3},{3,2},{4,5},{5,4},{6,7},{7,6},{8,9},{9,8},{10,11... | collective-permute-start | bytes 786440 | tf_op jit(solution)/shard_map/ppermute | solution.py:408
